TPU v7x, 128 devices: a whole 4x4x4 slice. The times are simulated.
128 devices in a mesh: rep: 4 (over x), row: 32 (over z, y, core).
Axes of the slice: x: 4, y: 4, z: 4, core: 2. Of those that a mesh axis runs over, the one named last changes fastest.
Arguments:
- features: float32 [262144, 128], P(('rep', 'row')), may hold values from -6 to 6
- tile_values: float32 [16384, 128, 128], P(('rep', 'row')), may hold values from -0.25 to 0.25
- tile_owner: int32 [16384, 1], P(('rep', 'row')), may hold values from 0 to 31; in each aligned block of 128 rows (0 to 127, 128 to 255, ...) at most 6 rows name the same one
- tile_local: int32 [16384], P(('rep', 'row')), may hold values from 0 to 15
- tile_source: int32 [16384], P(('rep', 'row')), may hold values from 0 to 63
- w_self: float32 [128, 256], replicated, may hold values from -0.5 to 0.5
- w_neigh: float32 [128, 256], replicated, may hold values from -0.5 to 0.5
- bias: float32 [256], replicated, may hold values from -3 to 3
- cotangent: float32 [262144, 256], P(('rep', 'row')), may hold values from -6 to 6
Outputs:
- output: float32 [262144, 256], P(('rep', 'row'))
- grad_x: float32 [262144, 128], P(('rep', 'row'))
- grad_self: float32 [128, 256], replicated
- grad_neigh: float32 [128, 256], replicated
- grad_bias: float32 [256], replicated
Inputs may be any that keep to these rules, and one draw needn't show every extreme that they name: `tile_owner`: among the tiles of one device, no value is named by more than 6 tiles, a bound that some device reaches.
All inputs are finite; a program needn't handle non-finite values.
Results may differ from a plain program's by a relative error of at most 0.0003.
Values sent between devices are 32-bit elements; how exact they have to be, the bound alone decides.
No kernel may reach another device: no remote copies, remote signals or barrier semaphores. Data moves between devices by JAX's collectives and lax.ppermute only.
A program may use at most 128 MiB of HBM per device.

v0:
```python
import math

import jax
import jax.numpy as jnp
from jax import lax
from jax.sharding import PartitionSpec as P

SLOTS = 6


def local(
    features, tile_values, tile_owner, tile_local, tile_source, w_self, w_neigh, bias, cotangent
):
    highest = lax.Precision.HIGHEST
    node_dev, feat = features.shape
    tiles_dev, block = (tile_values.shape[0], tile_values.shape[1])
    blocks_dev = node_dev // block
    n_row = lax.axis_size("row")
    n_rep = lax.axis_size("rep")
    slab_blocks = n_rep * blocks_dev
    width = block * feat
    slot_count = n_row * SLOTS
    slab = lax.all_gather(features, "rep", axis=0, tiled=True)
    source_rows = jnp.take(slab.reshape(slab_blocks, width), tile_source, axis=0)
    partial_rows = jnp.einsum(
        "kij,kjf->kif", tile_values, source_rows.reshape(tiles_dev, block, feat), precision=highest
    ).reshape(tiles_dev, width)
    owner = tile_owner[:, 0]
    owner_hot = (owner[:, None] == jnp.arange(n_row, dtype=jnp.int32)[None, :]).astype(jnp.int32)
    before = jnp.cumsum(owner_hot, axis=0) - owner_hot
    rank = jnp.sum(before * owner_hot, axis=1)
    slot = owner * SLOTS + rank
    leader = jnp.ones((tiles_dev,), jnp.float32)
    send_hot = (slot[None, :] == jnp.arange(slot_count, dtype=jnp.int32)[:, None]).astype(
        jnp.float32
    )
    send_rows = jnp.dot(
        send_hot, partial_rows, precision=highest, preferred_element_type=jnp.float32
    )
    slot_blocks = (
        jnp.dot(
            send_hot,
            leader * (tile_local + 1).astype(jnp.float32),
            precision=highest,
            preferred_element_type=jnp.float32,
        )
        - 1.0
    )
    received, received_ids = (
        lax.all_to_all(
            send_rows.reshape(n_row, SLOTS, width), "row", split_axis=0, concat_axis=0, tiled=True
        ),
        lax.all_to_all(
            slot_blocks.reshape(n_row, SLOTS), "row", split_axis=0, concat_axis=0, tiled=True
        ),
    )
    recv_hot = (
        received_ids.reshape(slot_count)[None, :]
        == jnp.arange(blocks_dev, dtype=jnp.float32)[:, None]
    ).astype(jnp.float32)
    aggregated = jnp.dot(
        recv_hot,
        received.reshape(slot_count, width),
        precision=highest,
        preferred_element_type=jnp.float32,
    ).reshape(node_dev, feat)
    pre = (
        jnp.dot(features, w_self, precision=highest, preferred_element_type=jnp.float32)
        + jnp.dot(aggregated, w_neigh, precision=highest, preferred_element_type=jnp.float32)
        + bias
    )
    sigma = jax.nn.sigmoid(pre)
    output = pre * sigma
    grad_pre = cotangent * sigma * (1.0 + pre * (1.0 - sigma))
    term_self = jnp.dot(features.T, grad_pre, precision=highest, preferred_element_type=jnp.float32)
    term_neigh = jnp.dot(
        aggregated.T, grad_pre, precision=highest, preferred_element_type=jnp.float32
    )
    term_bias = jnp.sum(grad_pre, axis=0)
    sum_self, sum_neigh, sum_bias = lax.psum((term_self, term_neigh, term_bias), ("rep", "row"))
    scale = 1.0 / math.sqrt(node_dev * n_rep * n_row)
    grad_self = sum_self * scale
    grad_neigh = sum_neigh * scale
    grad_bias = sum_bias * scale
    grad_agg = jnp.dot(grad_pre, w_neigh.T, precision=highest, preferred_element_type=jnp.float32)
    back_rows = jnp.dot(
        recv_hot.T,
        grad_agg.reshape(blocks_dev, width),
        precision=highest,
        preferred_element_type=jnp.float32,
    )
    returned = lax.all_to_all(
        back_rows.reshape(n_row, SLOTS, width), "row", split_axis=0, concat_axis=0, tiled=True
    )
    tile_grads = jnp.dot(
        send_hot.T,
        returned.reshape(slot_count, width),
        precision=highest,
        preferred_element_type=jnp.float32,
    )
    source_terms = jnp.einsum(
        "kji,kjf->kif", tile_values, tile_grads.reshape(tiles_dev, block, feat), precision=highest
    ).reshape(tiles_dev, width)
    source_hot = (tile_source[None, :] == jnp.arange(slab_blocks, dtype=jnp.int32)[:, None]).astype(
        jnp.float32
    )
    slab_grad = jnp.dot(
        source_hot, source_terms, precision=highest, preferred_element_type=jnp.float32
    ).reshape(n_rep * node_dev, feat)
    own_grad = jnp.dot(grad_pre, w_self.T, precision=highest, preferred_element_type=jnp.float32)
    grad_x = lax.psum_scatter(slab_grad, "rep", scatter_dimension=0, tiled=True) + own_grad
    return (output, grad_x, grad_self, grad_neigh, grad_bias)


def solution(mesh):
    return jax.shard_map(
        local,
        mesh=mesh,
        in_specs=(
            P(("rep", "row"), None),
            P(("rep", "row"), None, None),
            P(("rep", "row"), None),
            P(("rep", "row")),
            P(("rep", "row")),
            P(),
            P(),
            P(),
            P(("rep", "row"), None),
        ),
        out_specs=(P(("rep", "row"), None), P(("rep", "row"), None), P(), P(), P()),
        check_vma=False,
    )
```

profile of v0, /device:TPU:5, one launch (start us, length us, event | category | flops | bytes accessed | tf_op | source)
XLA Modules:
  0.0 802.3 jit_solution(210990872926128358)
XLA Ops:
  11.9 8.8 %all-to-all-start = ((f32[32,1,6]{2,1,0:T(1,128)}), f32[32,1,6]{2,1,0:T(1,128)S(1)}, u32[]{:S(2)}, u32[]{:S(2)}) async-start(f32[32,1,6]{2,1,0:T(1,128)} %bitcast.3), calls=%async_computation | async-start | bytes 32768 | tf_op jit(solution)/shard_map/all_to_all | solution.py:53
  22.1 37.3 %all-gather.2.cloned.1.call-done = f32[8192,128]{1,0:T(8,128)} async-done(((f32[2048,128]{1,0:T(8,128)}), f32[8192,128]{1,0:T(8,128)}) %all-gather.2.cloned.1.call-update) | async-done | bytes 4194320 | tf_op jit(solution)/shard_map/all_gather | solution.py:23
  59.4 5.0 reshape.102
  64.3 11.8 %gather_fusion = f32[128,16384]{1,0:T(8,128)} fusion(f32[64,16384]{1,0:T(8,128)} %reshape.102, s32[1024]{0:T(1024)S(1)} %pad_clamp_fusion), kind=kCustom, calls=%fused_computation | custom fusion | bytes 16777728 | tf_op jit(solution)/shard_map/jit(_take)/gather | solution.py:24
  76.2 8.1 %copy.57 = f32[16,8,128,128]{3,2,1,0:T(8,128)} copy(f32[16,8,128,128]{3,1,2,0:T(8,128)} %bitcast.55) | data formatting | bytes 16777216
  84.2 9.0 %copy.41 = f32[128,128,128]{1,2,0:T(8,128)} copy(f32[128,128,128]{2,1,0:T(8,128)} %bitcast.53) | data formatting | bytes 16777216 | tf_op jit(solution)/shard_map/jit(_take)/gather | solution.py:24
  93.2 23.3 %fusion.9 = f32[128,128,128]{1,2,0:T(8,128)} fusion(f32[128,128,128]{2,1,0:T(8,128)} %param.10, f32[128,128,128]{1,2,0:T(8,128)} %copy.41, pred[128]{0:T(512)(128)(4,1)S(1)} %compare_and_fusion), kind=kOutput, calls=%fused_computation.10 | convolution fusion | flops 3223322624 | bytes 25165952 | tf_op jit(solution)/shard_map/kij,kjf->kif/dot_general | solution.py:25
  116.5 9.3 %copy.42 = f32[128,128,128]{0,2,1:T(8,128)} copy(f32[128,128,128]{1,2,0:T(8,128)} %fusion.9) | data formatting | bytes 16777216 | tf_op jit(solution)/shard_map/kij,kjf->kif/dot_general | solution.py:25
  125.8 10.6 %fusion.20 = f32[32,6,16384]{2,0,1:T(8,128)} fusion(f32[128,16384,1]{0,1,2:T(8,128)} %bitcast.52, s32[32,6]{0,1:T(8,128)S(1)} %multiply_add_fusion, s32[128]{0:T(128)S(1)} %multiply_add_fusion.1), kind=kOutput, calls=%fused_computation.22 | convolution fusion | flops 4831862784 | bytes 20972800 | tf_op jit(solution)/shard_map/dot_general | solution.py:37
  136.5 17.8 %copy.44 = f32[32,6,16384]{2,1,0:T(8,128)} copy(f32[32,6,16384]{2,0,1:T(8,128)} %fusion.20) | data formatting | bytes 25165824 | tf_op jit(solution)/shard_map/dot_general | solution.py:37
  154.3 8.5 %all-to-all-start.1 = ((f32[32,6,16384]{2,1,0:T(8,128)}), f32[32,6,16384]{2,1,0:T(8,128)}, u32[]{:S(2)}, u32[]{:S(2)}) async-start(f32[32,6,16384]{2,1,0:T(8,128)} %copy.44), calls=%async_computation.1 | async-start | bytes 33554432 | tf_op jit(solution)/shard_map/all_to_all | solution.py:50
  162.8 3.1 fusion.40
  167.3 196.9 %all-to-all-done.1 = f32[32,6,16384]{2,1,0:T(8,128)} async-done(((f32[32,6,16384]{2,1,0:T(8,128)}), f32[32,6,16384]{2,1,0:T(8,128)}, u32[]{:S(2)}, u32[]{:S(2)}) %all-to-all-start.1) | async-done | bytes 12582944 | tf_op jit(solution)/shard_map/all_to_all | solution.py:50
  364.2 12.6 %reshape.104 = f32[192,16384]{1,0:T(8,128)} reshape(f32[32,6,16384]{2,1,0:T(8,128)} %all-to-all-done.1) | data formatting | bytes 25165824 | tf_op jit(solution)/shard_map/reshape | solution.py:63
  376.9 7.0 fusion.33
  385.0 6.3 fusion.39
  391.3 2.8 fusion.41
  394.1 2.5 reshape.122
  396.5 9.2 %fusion.28 = f32[32,6,16384]{2,0,1:T(8,128)} fusion(f32[16,16384,1]{1,0,2:T(8,128)} %reshape.122, f32[32,6]{0,1:T(8,128)S(1)} %copy.45), kind=kOutput, calls=%fused_computation.35 | convolution fusion | flops 603982848 | bytes 13632256 | tf_op jit(solution)/shard_map/dot_general | solution.py:86
  405.7 17.8 %copy.46 = f32[32,6,16384]{2,1,0:T(8,128)} copy(f32[32,6,16384]{2,0,1:T(8,128)} %fusion.28) | data formatting | bytes 25165824 | tf_op jit(solution)/shard_map/dot_general | solution.py:86
  423.5 16.8 %all-to-all-start.2 = ((f32[32,6,16384]{2,1,0:T(8,128)}), f32[32,6,16384]{2,1,0:T(8,128)}, u32[]{:S(2)}, u32[]{:S(2)}) async-start(f32[32,6,16384]{2,1,0:T(8,128)} %copy.46), calls=%async_computation.2 | async-start | bytes 33554432 | tf_op jit(solution)/shard_map/all_to_all | solution.py:92
  440.4 5.3 fusion.42
  445.7 4.1 convolution_bitcast_fusion
  450.0 193.2 %all-to-all-done.2 = f32[32,6,16384]{2,1,0:T(8,128)} async-done(((f32[32,6,16384]{2,1,0:T(8,128)}), f32[32,6,16384]{2,1,0:T(8,128)}, u32[]{:S(2)}, u32[]{:S(2)}) %all-to-all-start.2) | async-done | bytes 12582944 | tf_op jit(solution)/shard_map/all_to_all | solution.py:92
  643.2 12.7 %reshape.107 = f32[192,16384]{1,0:T(8,128)} reshape(f32[32,6,16384]{2,1,0:T(8,128)} %all-to-all-done.2) | data formatting | bytes 25165824 | tf_op jit(solution)/shard_map/reshape | solution.py:97
  655.8 8.9 %fusion = f32[128,128,128]{2,0,1:T(8,128)S(1)} fusion(s32[128]{0:T(128)S(1)} %multiply_add_fusion.1, f32[192,16384]{1,0:T(8,128)} %reshape.107), kind=kOutput, calls=%fused_computation.1 | convolution fusion | flops 4831862784 | bytes 20972032 | tf_op jit(solution)/shard_map/dot_general | solution.py:95
  664.8 24.5 %fusion.12 = f32[128,128,128]{1,2,0:T(8,128)} fusion(f32[128,128,128]{2,1,0:T(8,128)} %param.10, f32[128,128,128]{2,0,1:T(8,128)S(1)} %fusion), kind=kOutput, calls=%fused_computation.11 | convolution fusion | flops 3221225472 | bytes 25165824 | tf_op jit(solution)/shard_map/kji,kjf->kif/dot_general | solution.py:101
  689.2 9.6 %copy.49 = f32[128,128,128]{0,2,1:T(8,128)} copy(f32[128,128,128]{1,2,0:T(8,128)} %fusion.12) | data formatting | bytes 16777216 | tf_op jit(solution)/shard_map/kji,kjf->kif/dot_general | solution.py:101
  698.8 10.3 %fusion.30 = f32[64,16384]{1,0:T(8,128)} fusion(f32[128,16384]{0,1:T(8,128)} %bitcast.54, s32[128]{0:T(128)S(1)} %copy-done.3), kind=kOutput, calls=%fused_computation.37 | convolution fusion | flops 1610620928 | bytes 12583424 | tf_op jit(solution)/shard_map/dot_general | solution.py:107
  709.1 4.9 reshape.109
  714.1 74.2 %psum.23 = f32[256]{0:T(256)S(1)} all-reduce(f32[256]{0:T(256)S(1)} %get-tuple-element.27), channel_id=1, replica_groups=mesh['rep'=4,'row'=32] {'rep','row'}, use_global_device_ids=true, to_apply=%region_6.7 | all-reduce | flops 256 | bytes 2048 | tf_op jit(solution)/shard_map/psum | solution.py:80
  791.3 4.0 convolution_add_fusion.1
  (39 shorter events, 12.0 us)
Async XLA Ops:
  7.2 377.8 %copy-start = (f32[128,256]{1,0:T(8,128)S(1)}, f32[128,256]{1,0:T(8,128)}, u32[]{:S(2)}) copy-start(f32[128,256]{1,0:T(8,128)} %param.15) | copy-start | bytes 393220
  7.2 52.2 %all-gather.2.cloned.1.call-start = ((), (), s32[]{:S(2)}) async-start(), calls=%async_computation.4 | async-start | bytes 5242880 | tf_op jit(solution)/shard_map/all_gather | solution.py:23
  11.9 142.4 %all-to-all-start = ((f32[32,1,6]{2,1,0:T(1,128)}), f32[32,1,6]{2,1,0:T(1,128)S(1)}, u32[]{:S(2)}, u32[]{:S(2)}) async-start(f32[32,1,6]{2,1,0:T(1,128)} %bitcast.3), calls=%async_computation | async-start | bytes 32768 | tf_op jit(solution)/shard_map/all_to_all | solution.py:53
  154.3 8.5 %copy-start.1 = (f32[2048,128]{1,0:T(8,128)S(1)}, f32[2048,128]{1,0:T(8,128)}, u32[]{:S(2)}) copy-start(f32[2048,128]{1,0:T(8,128)} %param.9) | copy-start | bytes 3145732
  154.3 8.5 %copy-start.2 = (f32[128,256]{1,0:T(8,128)S(1)}, f32[128,256]{1,0:T(8,128)}, u32[]{:S(2)}) copy-start(f32[128,256]{1,0:T(8,128)} %param.14) | copy-start | bytes 393220
  154.3 209.9 %all-to-all-start.1 = ((f32[32,6,16384]{2,1,0:T(8,128)}), f32[32,6,16384]{2,1,0:T(8,128)}, u32[]{:S(2)}, u32[]{:S(2)}) async-start(f32[32,6,16384]{2,1,0:T(8,128)} %copy.44), calls=%async_computation.1 | async-start | bytes 33554432 | tf_op jit(solution)/shard_map/all_to_all | solution.py:50
  376.9 8.1 %copy-start.4 = (f32[256]{0:T(256)S(1)}, f32[256]{0:T(256)}, u32[]{:S(2)}) copy-start(f32[256]{0:T(256)} %param.16) | copy-start | bytes 3076
  423.5 219.7 %all-to-all-start.2 = ((f32[32,6,16384]{2,1,0:T(8,128)}), f32[32,6,16384]{2,1,0:T(8,128)}, u32[]{:S(2)}, u32[]{:S(2)}) async-start(f32[32,6,16384]{2,1,0:T(8,128)} %copy.46), calls=%async_computation.2 | async-start | bytes 33554432 | tf_op jit(solution)/shard_map/all_to_all | solution.py:92
  440.3 348.5 %all-reduce.3.cloned.1.call-start = ((), (), s32[]{:S(2)}) async-start(), calls=%async_computation.6 | async-start | bytes 524288 | tf_op jit(solution)/shard_map/psum | solution.py:80
  449.8 341.5 %reduce-scatter.2.cloned.1.call-start = ((), (), s32[]{:S(2)}) async-start(), calls=%async_computation.5 | async-start | bytes 5242880 | tf_op jit(solution)/shard_map/reduce_scatter | solution.py:111
  689.2 9.6 %copy-start.3 = (s32[128]{0:T(128)S(1)}, s32[128]{0:T(128)}, u32[]{:S(2)}) copy-start(s32[128]{0:T(128)} %param.13) | copy-start | bytes 1540
Sparse Core Ops, SparseCore 0:
  9.7 49.6 all-gather.1
  449.9 278.0 all-reduce.2
  730.4 43.7 reduce-scatter.1
where the time goes:
time: 813 us; the launch traced here: 802 us
  waiting for transfers between devices  428 us (53%)
  local copies, waits for them, and re-layouts  125 us (15%)
  matrix products  120 us (15%)
  blocking collectives  74.2 us (9%)
  starting transfers between devices  34.4 us (4%)
  between operations  14.3 us (2%)
    all_to_all x1, waiting for transfers between devices, local(): lax.all_to_all(send_rows.reshape(n_row, SLOTS, width), 'row', split_axis=...  197 us
    all_to_all x1, waiting for transfers between devices, local(): lax.all_to_all(back_rows.reshape(n_row, SLOTS, width), 'row', split_axis=...  193 us
    psum x1, blocking collectives, local(): lax.psum((term_self, term_neigh, term_bias), ('rep', 'row'))  74.2 us
    all_gather x1, waiting for transfers between devices, local(): slab = lax.all_gather(features, 'rep', axis=0, tiled=True)  37.3 us
    dot_general x1, matrix products, local(): jnp.einsum('kji,kjf->kif', tile_values, tile_grads.reshape(tiles_dev, blo...  24.5 us
    dot_general x1, matrix products, local(): jnp.einsum('kij,kjf->kif', tile_values, source_rows.reshape(tiles_dev, bl...  23.3 us
    gather x2, local copies, waits for them, and re-layouts, local(): jnp.take(slab.reshape(slab_blocks, width), tile_source, axis=0)  20.8 us
    dot_general x1, local copies, waits for them, and re-layouts, local(): jnp.dot(send_hot, partial_rows, precision=highest, preferred_element_type...  17.8 us
  transfers between devices with their start and end apart: 6, of which 3 were waited for; matrix products, arithmetic and copies ran while one was open for 23% of the time, Pallas kernels for 0%

commit v1 on v0

v1 whole, which is shorter than its diff:
```python
import functools
import math

import jax
import jax.numpy as jnp
from jax import lax
from jax.experimental import pallas as pl
from jax.experimental.pallas import tpu as pltpu
from jax.sharding import PartitionSpec as P

SLOTS = 6
BLOCK = 128
FEAT = 128
HID = 256
BLOCKS_DEV = 16
TILES_DEV = 128
N_REP = 4
SIDE = 4
N_ROW = 32
ROW_PARTS = 2
PART = BLOCK // ROW_PARTS
HALF = PART // 2
MSG = 2 * SIDE * SLOTS
DENSE = SIDE * BLOCKS_DEV
ORDER = ((0, 1), (0, 2), (1, 2), (1, 1), (0, 3), (1, 3))
STEP = 8
F32 = jnp.float32
BF16 = jnp.bfloat16
VMEM_LIMIT = 56 * 1024 * 1024

NN = (((1,), (0,)), ((), ()))
NT = (((1,), (1,)), ((), ()))
TN = (((0,), (0,)), ((), ()))


def params():
    return pltpu.CompilerParams(vmem_limit_bytes=VMEM_LIMIT)


def split(x):
    high = x.astype(BF16)
    return high, (x - high.astype(F32)).astype(BF16)


def dot(a, b, dims):
    return lax.dot_general(a, b, dims, preferred_element_type=F32)


def dot3(a, b, dims):
    a_high, a_low = a
    b_high, b_low = b
    return dot(a_high, b_high, dims) + dot(a_low, b_high, dims) + dot(a_high, b_low, dims)


def whole(shape):
    return pl.BlockSpec(shape, lambda *_: (0,) * len(shape))


ANY = pl.BlockSpec(memory_space=pl.ANY)


def forward_kernel(meta, tiles, f0, f1, f2, f3, *rest):
    outs, (slab, send, sems) = rest[: 2 * SIDE], rest[2 * SIDE :]
    step = pl.program_id(0)

    @pl.when(step == 0)
    def _():
        for d, ref in enumerate((f0, f1, f2, f3)):
            high, low = split(ref[...])
            slab[d * BLOCKS_DEV : (d + 1) * BLOCKS_DEV, :, :FEAT] = high
            slab[d * BLOCKS_DEV : (d + 1) * BLOCKS_DEV, :, FEAT:] = low

    for t in range(STEP):
        i = step * STEP + t
        both = dot(jnp.concatenate(split(tiles[t]), axis=0), slab[meta[i]], NN)
        part = both[:PART, :FEAT] + both[PART:, :FEAT] + both[:PART, FEAT:]
        send[meta[TILES_DEV + i]] = part[:HALF]
        send[meta[2 * TILES_DEV + i]] = part[HALF:]

    @pl.when(step == pl.num_programs(0) - 1)
    def _():
        copies = [
            pltpu.make_async_copy(send.at[pl.ds(k * MSG, MSG)], out, sems.at[k])
            for k, out in enumerate(outs)
        ]
        for copy in copies:
            copy.start()
        for copy in copies:
            copy.wait()


def forward_tiles(meta, tile_values, parts, number):
    spec = pltpu.PrefetchScalarGridSpec(
        num_scalar_prefetch=1,
        grid=(TILES_DEV // STEP,),
        in_specs=[pl.BlockSpec((STEP, PART, BLOCK), lambda i, _: (i, number, 0))]
        + [whole((BLOCKS_DEV, BLOCK, FEAT))] * N_REP,
        out_specs=[ANY] * (2 * SIDE),
        scratch_shapes=[
            pltpu.VMEM((N_REP * BLOCKS_DEV, BLOCK, 2 * FEAT), BF16),
            pltpu.VMEM((2 * SIDE * MSG, HALF, FEAT), F32),
            pltpu.SemaphoreType.DMA((2 * SIDE,)),
        ],
    )
    return pl.pallas_call(
        forward_kernel,
        grid_spec=spec,
        out_shape=[jax.ShapeDtypeStruct((MSG, HALF, FEAT), F32)] * (2 * SIDE),
        compiler_params=params(),
        name="forward_tiles",
    )(meta, tile_values, *[p.reshape(BLOCKS_DEV, BLOCK, FEAT) for p in parts])


def combine_kernel(ids, place, *rest):
    received, (keep, give) = rest[: 2 * SIDE], rest[2 * SIDE : 2 * SIDE + 2]
    got, acc, in_sems, sems = rest[-4:]
    z, y, c = place[0], place[1], place[2]
    rows = BLOCKS_DEV + 1
    arrivals = [
        pltpu.make_async_copy(ref, got.at[k], in_sems.at[k]) for k, ref in enumerate(received)
    ]
    for copy in arrivals:
        copy.start()
    acc[...] = jnp.zeros_like(acc)
    copies = []
    for path in range(2):
        for d in range(SIDE):
            if path == 0:
                sender = (z * SIDE + (y + SIDE - d) % SIDE) * 2 + c
            else:
                sender = ((z + SIDE - d) % SIDE * SIDE + y) * 2 + c
            base = sender * (2 * MSG) + path * MSG
            arrivals[path * SIDE + d].wait()
            for s in range(MSG):
                row = (path * 2 * SIDE + s // SLOTS) * rows + ids[base + s]
                acc[row] += got[path * SIDE + d, s]
        for d in range(SIDE):
            target = ((z if path == 0 else y) + d) % SIDE
            for other, out in enumerate((keep, give)):
                copy = pltpu.make_async_copy(
                    acc.at[pl.ds(((path * 2 + other) * SIDE + target) * rows, BLOCKS_DEV)],
                    out.at[pl.ds((path * SIDE + d) * BLOCKS_DEV, BLOCKS_DEV)],
                    sems.at[(path * 2 + other) * SIDE + d],
                )
                copy.start()
                copies.append(copy)
    for copy in copies:
        copy.wait()


def combine(ids, place, received):
    spec = pltpu.PrefetchScalarGridSpec(
        num_scalar_prefetch=2,
        grid=(1,),
        in_specs=[ANY] * (2 * SIDE),
        out_specs=[ANY] * 2,
        scratch_shapes=[
            pltpu.VMEM((2 * SIDE, MSG, HALF, FEAT), F32),
            pltpu.VMEM((4 * SIDE * (BLOCKS_DEV + 1), HALF, FEAT), F32),
            pltpu.SemaphoreType.DMA((2 * SIDE,)),
            pltpu.SemaphoreType.DMA((4 * SIDE,)),
        ],
    )
    return pl.pallas_call(
        combine_kernel,
        grid_spec=spec,
        out_shape=[jax.ShapeDtypeStruct((2 * DENSE, HALF, FEAT), F32)] * 2,
        compiler_params=params(),
        name="combine_blocks",
    )(ids, place, *received)


def add_kernel(keep, taken, *rest):
    outs, (left, right, in_sems, out_sems) = rest[: 2 * SIDE], rest[2 * SIDE :]
    loads, stores = [], []
    for k in range(2 * SIDE):
        rows = pl.ds(k * BLOCKS_DEV, BLOCKS_DEV)
        for n, (ref, buffer) in enumerate(((keep, left), (taken, right))):
            copy = pltpu.make_async_copy(ref.at[rows], buffer.at[k], in_sems.at[2 * k + n])
            copy.start()
            loads.append(copy)
    for k, out in enumerate(outs):
        loads[2 * k].wait()
        loads[2 * k + 1].wait()
        left[k] += right[k]
        copy = pltpu.make_async_copy(left.at[k], out, out_sems.at[k])
        copy.start()
        stores.append(copy)
    for copy in stores:
        copy.wait()


def add_cores(keep, taken):
    return pl.pallas_call(
        add_kernel,
        in_specs=[ANY] * 2,
        out_specs=[ANY] * (2 * SIDE),
        out_shape=[jax.ShapeDtypeStruct((BLOCKS_DEV, HALF, FEAT), F32)] * (2 * SIDE),
        scratch_shapes=[
            pltpu.VMEM((2 * SIDE, BLOCKS_DEV, HALF, FEAT), F32),
            pltpu.VMEM((2 * SIDE, BLOCKS_DEV, HALF, FEAT), F32),
            pltpu.SemaphoreType.DMA((4 * SIDE,)),
            pltpu.SemaphoreType.DMA((2 * SIDE,)),
        ],
        compiler_params=params(),
        name="add_cores",
    )(keep, taken)


PER = 2


def layer_kernel(features, cotangent, w_self, w_neigh, bias, *rest):
    sums, (output, grad_pre, aggregated, grads) = rest[:-4], rest[-4:]
    halves = []
    for b in range(PER):
        for piece in range(2 * ROW_PARTS):
            refs = sums[piece * SIDE : (piece + 1) * SIDE]
            halves.append((refs[0][b] + refs[1][b]) + (refs[2][b] + refs[3][b]))
    agg = jnp.concatenate(halves, axis=0)
    aggregated[...] = agg
    w_neigh_split = split(w_neigh[...])
    pre = (
        dot3(split(features[...]), split(w_self[...]), NN)
        + dot3(split(agg), w_neigh_split, NN)
        + bias[...]
    )
    sigma = jax.nn.sigmoid(pre)
    output[...] = pre * sigma
    grad = cotangent[...] * sigma * (1.0 + pre * (1.0 - sigma))
    grad_pre[...] = grad
    high, low = split(grad)
    for b in range(PER):
        rows = slice(b * BLOCK, (b + 1) * BLOCK)
        grads[b] = dot3(w_neigh_split, (high[rows], low[rows]), NT)


def layer(features, cotangent, w_self, w_neigh, bias, sums):
    nodes = features.shape[0]
    row = lambda width: pl.BlockSpec((PER * BLOCK, width), lambda i: (i, 0))
    block = lambda depth: pl.BlockSpec((PER, depth, BLOCK), lambda i: (i, 0, 0))
    return pl.pallas_call(
        layer_kernel,
        grid=(BLOCKS_DEV // PER,),
        in_specs=[row(FEAT), row(HID), whole((FEAT, HID)), whole((FEAT, HID)), whole((1, HID))]
        + [block(HALF)] * (2 * ROW_PARTS * SIDE),
        out_specs=[row(HID), row(HID), row(FEAT), block(FEAT)],
        out_shape=[
            jax.ShapeDtypeStruct((nodes, HID), F32),
            jax.ShapeDtypeStruct((nodes, HID), F32),
            jax.ShapeDtypeStruct((nodes, FEAT), F32),
            jax.ShapeDtypeStruct((BLOCKS_DEV, FEAT, BLOCK), F32),
        ],
        compiler_params=params(),
        name="layer",
    )(features, cotangent, w_self, w_neigh, bias, *sums)


TERM_ROWS = 2 * FEAT // N_ROW


def terms_kernel(features, aggregated, grad_pre, w_self, own, terms, acc, acc_bias):
    step = pl.program_id(0)

    @pl.when(step == 0)
    def _():
        acc[...] = jnp.zeros_like(acc)
        acc_bias[...] = jnp.zeros_like(acc_bias)

    grad = grad_pre[...]
    parts = split(grad)
    own[...] = dot3(parts, split(w_self[...]), NT)
    acc[:FEAT] += dot3(split(features[...]), parts, TN)
    acc[FEAT:] += dot3(split(aggregated[...]), parts, TN)
    acc_bias[...] += jnp.sum(grad.reshape(-1, 8, HID), axis=0)

    @pl.when(step == pl.num_programs(0) - 1)
    def _():
        total = jnp.sum(acc_bias[...], axis=0, keepdims=True)
        for r in range(N_ROW):
            terms[r, :, :HID] = acc[r * TERM_ROWS : (r + 1) * TERM_ROWS]
            terms[r, :, HID:] = jnp.concatenate(
                [jnp.broadcast_to(total[:, :128], (4, 128)), jnp.broadcast_to(total[:, 128:], (4, 128))],
                axis=0,
            )


def weight_terms(features, aggregated, grad_pre, w_self):
    nodes = features.shape[0]
    row = lambda width: pl.BlockSpec((PER * BLOCK, width), lambda i: (i, 0))
    return pl.pallas_call(
        terms_kernel,
        grid=(BLOCKS_DEV // PER,),
        in_specs=[row(FEAT), row(FEAT), row(HID), whole((FEAT, HID))],
        out_specs=[row(FEAT), whole((N_ROW, TERM_ROWS, HID + 128))],
        out_shape=[
            jax.ShapeDtypeStruct((nodes, FEAT), F32),
            jax.ShapeDtypeStruct((N_ROW, TERM_ROWS, HID + 128), F32),
        ],
        scratch_shapes=[pltpu.VMEM((2 * FEAT, HID), F32), pltpu.VMEM((8, HID), F32)],
        compiler_params=params(),
        name="weight_terms",
    )(features, aggregated, grad_pre, w_self)


def backward_kernel(meta, tiles, grads, *rest):
    outs, (got, acc, sems, out_sems) = rest[:N_REP], rest[N_REP:]
    step = pl.program_id(0)
    steps = pl.num_programs(0)

    @pl.when(step == 0)
    def _():
        def fetch(i, _):
            pltpu.make_async_copy(
                grads.at[meta[TILES_DEV + i]], got.at[i // STEP, i % STEP], sems.at[i // STEP]
            ).start()
            return 0

        lax.fori_loop(0, TILES_DEV, fetch, 0)
        acc[...] = jnp.zeros_like(acc)

    pltpu.make_async_copy(grads.at[pl.ds(0, STEP)], got.at[step], sems.at[step]).wait()
    for t in range(STEP):
        grad = jnp.concatenate(split(got[step, t]), axis=0)
        both = dot(grad, jnp.concatenate(split(tiles[t]), axis=1), NN)
        part = both[:FEAT, :BLOCK] + both[FEAT:, :BLOCK] + both[:FEAT, BLOCK:]
        acc[meta[step * STEP + t]] += part

    @pl.when(step == steps - 1)
    def _():
        rep = meta[2 * TILES_DEV]
        copies = [
            pltpu.make_async_copy(
                acc.at[pl.ds((rep + d) % N_REP * BLOCKS_DEV, BLOCKS_DEV)], out, out_sems.at[d]
            )
            for d, out in enumerate(outs)
        ]
        for copy in copies:
            copy.start()
        for copy in copies:
            copy.wait()


def backward_tiles(meta, tile_values, grads):
    spec = pltpu.PrefetchScalarGridSpec(
        num_scalar_prefetch=1,
        grid=(TILES_DEV // STEP,),
        in_specs=[pl.BlockSpec((STEP, BLOCK, BLOCK), lambda i, _: (i, 0, 0)), ANY],
        out_specs=[ANY] * N_REP,
        scratch_shapes=[
            pltpu.VMEM((TILES_DEV // STEP, STEP, FEAT, BLOCK), F32),
            pltpu.VMEM((N_REP * BLOCKS_DEV, FEAT, BLOCK), F32),
            pltpu.SemaphoreType.DMA((TILES_DEV // STEP,)),
            pltpu.SemaphoreType.DMA((N_REP,)),
        ],
    )
    return pl.pallas_call(
        backward_kernel,
        grid_spec=spec,
        out_shape=[jax.ShapeDtypeStruct((BLOCKS_DEV, FEAT, BLOCK), F32)] * N_REP,
        compiler_params=params(),
        name="backward_tiles",
    )(meta, tile_values, grads)


def finish_kernel(own, *rest):
    sums, out = rest[:-1], rest[-1]
    for b in range(PER):
        total = (sums[0][b] + sums[1][b]) + (sums[2][b] + sums[3][b])
        rows = slice(b * BLOCK, (b + 1) * BLOCK)
        out[rows, :] = own[rows, :] + total.T


def finish(own, sums):
    row = pl.BlockSpec((PER * BLOCK, FEAT), lambda i: (i, 0))
    return pl.pallas_call(
        finish_kernel,
        grid=(BLOCKS_DEV // PER,),
        in_specs=[row] + [pl.BlockSpec((PER, FEAT, BLOCK), lambda i: (i, 0, 0))] * N_REP,
        out_specs=row,
        out_shape=jax.ShapeDtypeStruct(own.shape, F32),
        compiler_params=params(),
        name="finish_grad_x",
    )(own, *sums)


def row_index(z, y, c):
    return (z % SIDE * SIDE + y % SIDE) * 2 + c % 2


def shift(x, dz, dy, dc=0):
    pairs = [
        (row_index(z, y, c), row_index(z + dz, y + dy, c + dc))
        for z in range(SIDE)
        for y in range(SIDE)
        for c in range(2)
    ]
    return lax.ppermute(x, "row", pairs)


def shift_rep(x, d):
    return x if d == 0 else lax.ppermute(x, "rep", [(i, (i + d) % N_REP) for i in range(N_REP)])


def local(
    features, tile_values, tile_owner, tile_local, tile_source, w_self, w_neigh, bias, cotangent
):
    rep, row = lax.axis_index("rep"), lax.axis_index("row")
    z, y, c = row // (2 * SIDE), row // 2 % SIDE, row % 2

    owner = tile_owner[:, 0]
    owner_hot = owner[:, None] == jnp.arange(N_ROW, dtype=jnp.int32)[None, :]
    same = owner[:, None] == owner[None, :]
    earlier = jnp.arange(TILES_DEV)[:, None] > jnp.arange(TILES_DEV)[None, :]
    rank = jnp.sum((same & earlier).astype(jnp.int32), axis=1)
    slot = owner * SLOTS + rank
    o_z, o_y, o_c = owner // (2 * SIDE), owner // 2 % SIDE, owner % 2
    o_core = (o_c - c) % 2
    pos_y = (o_y - y) % SIDE * MSG + (o_core * SIDE + o_z) * SLOTS + rank
    pos_z = ((o_z - z) % SIDE + SIDE) * MSG + (o_core * SIDE + o_y) * SLOTS + rank
    src_rep, src_block = tile_source // BLOCKS_DEV, tile_source % BLOCKS_DEV
    src = (rep - src_rep) % N_REP * BLOCKS_DEV + src_block
    forward_meta = jnp.concatenate([src, pos_y, pos_z]).astype(jnp.int32)
    backward_meta = jnp.concatenate(
        [tile_source, owner * BLOCKS_DEV + tile_local, rep[None]]
    ).astype(jnp.int32)
    place = jnp.stack([z, y, c]).astype(jnp.int32)

    hit = slot[None, :] == jnp.arange(N_ROW * SLOTS, dtype=jnp.int32)[:, None]
    named = jnp.sum(jnp.where(hit, (tile_local - BLOCKS_DEV)[None, :], 0), axis=1) + BLOCKS_DEV
    named = named.reshape(SIDE, SIDE, 2, SLOTS)
    both = jnp.stack([named, named[:, :, ::-1]], axis=3)
    grid = (SIDE, SIDE, 2, 2, SIDE, SLOTS)
    along_z = jnp.broadcast_to(both.transpose(1, 2, 3, 0, 4)[None], grid)
    along_y = jnp.broadcast_to(both.transpose(0, 2, 3, 1, 4)[:, None], grid)
    to_send = jnp.concatenate(
        [along_z.reshape(N_ROW, MSG), along_y.reshape(N_ROW, MSG)], axis=1
    ).astype(jnp.int32)
    ids = lax.all_to_all(to_send, "row", split_axis=0, concat_axis=0, tiled=True).reshape(-1)

    forward_meta, ids = lax.optimization_barrier((forward_meta, ids))
    parts = [features] + [shift_rep(features, d) for d in (1, 2, 3)]
    sums = []
    for number in range(ROW_PARTS):
        got = list(forward_tiles(forward_meta, tile_values, parts, number))
        for path, d in ORDER:
            k = path * SIDE + d
            got[k] = shift(got[k], 0, d) if path == 0 else shift(got[k], d, 0)
        keep, give = combine(ids, place, got)
        dense = list(add_cores(keep, shift(give, 0, 0, 1)))
        for path, d in ORDER:
            k = path * SIDE + d
            dense[k] = shift(dense[k], d, 0) if path == 0 else shift(dense[k], 0, d)
        sums.extend(dense)

    output, grad_pre, aggregated, grads = layer(
        features, cotangent, w_self, w_neigh, bias[None, :], sums
    )

    own, terms = weight_terms(features, aggregated, grad_pre, w_self)
    dealt = lax.all_to_all(terms, "row", split_axis=0, concat_axis=0, tiled=True)
    mine = lax.psum(jnp.sum(dealt, axis=0), "rep")
    full = lax.all_gather(mine, "row", axis=0, tiled=True)
    scale = 1.0 / math.sqrt(features.shape[0] * N_REP * N_ROW)
    grad_self = full[:FEAT, :HID] * scale
    grad_neigh = full[FEAT:, :HID] * scale
    grad_bias = jnp.concatenate([full[0, HID:], full[4, HID:]]) * scale

    gathered = lax.all_gather(grads, "row", axis=0, tiled=True)
    backward_meta, grad_self, grad_neigh, grad_bias = lax.optimization_barrier(
        (backward_meta, grad_self, grad_neigh, grad_bias)
    )
    slab = backward_tiles(backward_meta, tile_values, gathered)
    back = [slab[0]] + [shift_rep(slab[d], d) for d in (1, 2, 3)]
    grad_x = finish(own, back)
    return (output, grad_x, grad_self, grad_neigh, grad_bias)


def solution(mesh):
    return jax.shard_map(
        local,
        mesh=mesh,
        in_specs=(
            P(("rep", "row"), None),
            P(("rep", "row"), None, None),
            P(("rep", "row"), None),
            P(("rep", "row")),
            P(("rep", "row")),
            P(),
            P(),
            P(),
            P(("rep", "row"), None),
        ),
        out_specs=(P(("rep", "row"), None), P(("rep", "row"), None), P(), P(), P()),
        check_vma=False,
    )
```

time: 813 us -> 433 us (0.53)
  waiting for transfers between devices: 428 us -> 215 us
  matrix products: 120 us -> 0 us
  local copies, waits for them, and re-layouts: 125 us -> 6.26 us
  Pallas kernels: 0 us -> 91.4 us
  blocking collectives: 74.2 us -> 38.5 us
  starting transfers between devices: 34.4 us -> 57.9 us
    all_to_all x3 -> x2, waiting for transfers between devices: 390 us -> 18.8 us  [the longest x1 13.3 us: local(): lax.all_to_all(terms, 'row', split_axis=0, concat_axis=0, tiled=True)]
    ppermute x0 -> x32, waiting for transfers between devices: none -> 144 us  [the longest x26 72.2 us: shift(): return lax.ppermute(x, 'row', pairs)]
    dot_general x14 -> x0, matrix products: 120 us -> none  [the longest x1 24.5 us: local(): jnp.einsum('kji,kjf->kif', tile_values, tile_grads.reshape(tiles_dev, blo...]
    pallas_call x0 -> x10, Pallas kernels: none -> 91.4 us  [the longest x2 32.5 us: forward_tiles(): pl.pallas_call(forward_kernel, grid_spec=spec, out_shape=[jax.ShapeDtypeS...]
    psum x1, blocking collectives: 74.2 us -> 11.4 us  [local(): mine = lax.psum(jnp.sum(dealt, axis=0), 'rep')]
    dot_general x4 -> x0, local copies, waits for them, and re-layouts: 54.6 us -> none  [the longest x1 17.8 us: local(): jnp.dot(send_hot, partial_rows, precision=highest, preferred_element_type...]
    ppermute x0 -> x32, starting transfers between devices: none -> 42.4 us  [the longest x26 37.2 us: shift(): return lax.ppermute(x, 'row', pairs)]
    reshape x6 -> x3, local copies, waits for them, and re-layouts: 38.7 us -> 0.93 us  [the longest x1 0.67 us: local(): lax.all_to_all(to_send, 'row', split_axis=0, concat_axis=0, tiled=True)]
  transfers between devices with their start and end apart: 6 -> 35, of which waited for: 3 -> 19; matrix products, arithmetic and copies ran while one was open for 23% -> 2% of each run, Pallas kernels for 0% -> 10%
where the time goes in v1:
time: 433 us; the launch traced here: 430 us
  waiting for transfers between devices  215 us (50%)
  Pallas kernels  91.4 us (21%)
  starting transfers between devices  57.9 us (13%)
  blocking collectives  38.5 us (9%)
  between operations  14.5 us (3%)
  other arithmetic  6.85 us (2%)
  local copies, waits for them, and re-layouts  6.26 us (1%)
    ppermute x26, waiting for transfers between devices, shift(): return lax.ppermute(x, 'row', pairs)  72.2 us
    ppermute x6, waiting for transfers between devices, shift_rep(): lax.ppermute(x, 'rep', [(i, (i + d) % N_REP) for i in range(N_REP)])  72 us
    all_gather x1, waiting for transfers between devices, local(): gathered = lax.all_gather(grads, 'row', axis=0, tiled=True)  51.6 us
    ppermute x26, starting transfers between devices, shift(): return lax.ppermute(x, 'row', pairs)  37.2 us
    pallas_call x2, Pallas kernels, forward_tiles(): pl.pallas_call(forward_kernel, grid_spec=spec, out_shape=[jax.ShapeDtypeS...  32.5 us
    all_gather x1, blocking collectives, local(): full = lax.all_gather(mine, 'row', axis=0, tiled=True)  27.1 us
    pallas_call x1, Pallas kernels, backward_tiles(): pl.pallas_call(backward_kernel, grid_spec=spec, out_shape=[jax.ShapeDtype...  17.7 us
    all_to_all x1, waiting for transfers between devices, local(): lax.all_to_all(terms, 'row', split_axis=0, concat_axis=0, tiled=True)  13.3 us
  transfers between devices with their start and end apart: 35, of which 19 were waited for; matrix products, arithmetic and copies ran while one was open for 2% of the time, Pallas kernels for 10%

profile of v1, /device:TPU:5, one launch (start us, length us, event | category | flops | bytes accessed | tf_op | source)
XLA Modules:
  0.0 430.0 jit_solution(16092358741920309416)
XLA Ops:
  7.5 2.5 collective-permute-start.1
  13.1 9.3 %all-to-all-start = ((s32[32,1,96]{2,1,0:T(1,128)}), s32[32,1,96]{2,1,0:T(1,128)S(1)}, u32[]{:S(2)}, u32[]{:S(2)}) async-start(s32[32,1,96]{2,1,0:T(1,128)} %bitcast.5), calls=%async_computation | async-start | bytes 32768 | tf_op jit(solution)/shard_map/all_to_all | solution.py:439
  23.7 5.5 %all-to-all-done = s32[32,1,96]{2,1,0:T(1,128)S(1)} async-done(((s32[32,1,96]{2,1,0:T(1,128)}), s32[32,1,96]{2,1,0:T(1,128)S(1)}, u32[]{:S(2)}, u32[]{:S(2)}) %all-to-all-start) | async-done | bytes 12320 | tf_op jit(solution)/shard_map/all_to_all | solution.py:439
  33.0 23.8 %collective-permute-done = f32[2048,128]{1,0:T(8,128)S(1)} collective-permute-done((f32[2048,128]{1,0:T(8,128)}, f32[2048,128]{1,0:T(8,128)S(1)}, u32[]{:S(2)}, u32[]{:S(2)}) %collective-permute-start) | collective-permute-done | bytes 1048608 | tf_op jit(solution)/shard_map/ppermute | solution.py:402
  57.7 16.2 %forward_tiles.3 = (f32[48,32,128]{2,1,0:T(8,128)}, f32[48,32,128]{2,1,0:T(8,128)}, f32[48,32,128]{2,1,0:T(8,128)}, f32[48,32,128]{2,1,0:T(8,128)}, f32[48,32,12...) custom-call(s32[384]{0:T(512)} %pad_add_fusion.2.meta, ...), custom_call_target="tpu_custom_call" | custom-call | tf_op jit(solution)/shard_map/forward_tiles/pallas_call | solution.py:105
  75.3 2.6 collective-permute-start.17
  80.6 16.3 %forward_tiles.2 = (f32[48,32,128]{2,1,0:T(8,128)}, f32[48,32,128]{2,1,0:T(8,128)}, f32[48,32,128]{2,1,0:T(8,128)}, f32[48,32,128]{2,1,0:T(8,128)}, f32[48,32,12...) custom-call(s32[384]{0:T(512)} %pad_add_fusion.2.meta, ...), custom_call_target="tpu_custom_call" | custom-call | tf_op jit(solution)/shard_map/forward_tiles/pallas_call | solution.py:105
  96.9 3.4 collective-permute-start.20
  101.1 11.0 %collective-permute-done.17.rest_2_ = f32[48,32,128]{2,1,0:T(8,128)S(1)} collective-permute-done((f32[48,32,128]{2,1,0:T(8,128)}, f32[48,32,128]{2,1,0:T(8,128)S(1)}, u32[]{:S(2)}, u32[]{:S(2)}) %collective-permute-start.17) | collective-permute-done | bytes 786464 | tf_op jit(solution)/shard_map/ppermute | solution.py:398
  117.9 15.9 %collective-permute-done.21.rest_7_ = f32[48,32,128]{2,1,0:T(8,128)S(1)} collective-permute-done((f32[48,32,128]{2,1,0:T(8,128)}, f32[48,32,128]{2,1,0:T(8,128)S(1)}, u32[]{:S(2)}, u32[]{:S(2)}) %collective-permute-start.21) | collective-permute-done | bytes 786464 | tf_op jit(solution)/shard_map/ppermute | solution.py:398
  136.0 12.2 %collective-permute-done.3.rest_1_ = f32[48,32,128]{2,1,0:T(8,128)S(1)} collective-permute-done((f32[48,32,128]{2,1,0:T(8,128)}, f32[48,32,128]{2,1,0:T(8,128)S(1)}, u32[]{:S(2)}, u32[]{:S(2)}) %collective-permute-start.3) | collective-permute-done | bytes 786464 | tf_op jit(solution)/shard_map/ppermute | solution.py:398
  148.2 3.8 collective-permute-start.8
  152.6 5.5 %combine_blocks.3 = (f32[128,32,128]{2,1,0:T(8,128)}, f32[128,32,128]{2,1,0:T(8,128)}) custom-call(s32[3072]{0:T(1024)} %reshape.66.ids, s32[3]{0:T(128)} %pad_add_fusion.4.place, f32[48,32,128]{2,1,0:T(8,128)} %get-tuple-element.77.rest_0_, f32[48,32,128]{2,1,0:T(8,128)} %copy-done.8, f32[48,32,128]{2,1,0:T(8,128)} %copy-done.9, f32[48,32,128]{2,1,0:T(8,128)} %copy-done.10, ...), custom_call_target="tpu_custom_call" | custom-call | tf_op jit(solution)/shard_map/combine_blocks/pallas_call | solution.py:164
  158.1 2.7 collective-permute-start.22
  160.8 11.2 %collective-permute-done.8.rest_7_ = f32[48,32,128]{2,1,0:T(8,128)} collective-permute-done((f32[48,32,128]{2,1,0:T(8,128)}, f32[48,32,128]{2,1,0:T(8,128)}, u32[]{:S(2)}, u32[]{:S(2)}) %collective-permute-start.8) | collective-permute-done | bytes 786464 | tf_op jit(solution)/shard_map/ppermute | solution.py:398
  172.0 5.4 %combine_blocks.2 = (f32[128,32,128]{2,1,0:T(8,128)}, f32[128,32,128]{2,1,0:T(8,128)}) custom-call(s32[3072]{0:T(1024)} %reshape.66.ids, s32[3]{0:T(128)} %pad_add_fusion.4.place, f32[48,32,128]{2,1,0:T(8,128)} %get-tuple-element.59.rest_0_, f32[48,32,128]{2,1,0:T(8,128)} %copy-done.11, f32[48,32,128]{2,1,0:T(8,128)} %copy-done.13, ...), custom_call_target="tpu_custom_call" | custom-call | tf_op jit(solution)/shard_map/combine_blocks/pallas_call | solution.py:164
  180.2 3.4 add_cores.3
  189.7 3.4 add_cores.2
  195.5 4.0 collective-permute-done.24.rest_10_
  204.5 9.2 %collective-permute-done.10.rest_1_ = f32[16,32,128]{2,1,0:T(8,128)S(1)} collective-permute-done((f32[16,32,128]{2,1,0:T(8,128)}, f32[16,32,128]{2,1,0:T(8,128)S(1)}, u32[]{:S(2)}, u32[]{:S(2)}) %collective-permute-start.10) | collective-permute-done | bytes 262176 | tf_op jit(solution)/shard_map/ppermute | solution.py:398
  215.4 4.5 %collective-permute-done.15.rest_7_ = f32[16,32,128]{2,1,0:T(8,128)S(1)} collective-permute-done((f32[16,32,128]{2,1,0:T(8,128)}, f32[16,32,128]{2,1,0:T(8,128)S(1)}, u32[]{:S(2)}, u32[]{:S(2)}) %collective-permute-start.15) | collective-permute-done | bytes 262176 | tf_op jit(solution)/shard_map/ppermute | solution.py:398
  220.7 9.6 %layer.1 = (f32[2048,256]{1,0:T(8,128)}, f32[2048,256]{1,0:T(8,128)}, f32[2048,128]{1,0:T(8,128)}, f32[16,128,128]{2,1,0:T(8,128)}) custom-call(f32[2048,128]{1,0:T(8,128)} %features.3, f32[2048,256]{1,0:T(8,128)} %cotangent.1, f32[128,256]{1,0:T(8,128)} %w_self.3, f32[128,256]{1,0:T(8,128)} %w_neigh.1, f32[1,256]{1,0:T(1,128)} %bitcast.48, ...), custom_call_target="tpu_custom_call" | custom-call | tf_op jit(solution)/shard_map/layer/pallas_call | solution.py:242
  230.3 7.6 %weight_terms.1 = (f32[2048,128]{1,0:T(8,128)}, f32[32,8,384]{2,1,0:T(8,128)}) custom-call(f32[2048,128]{1,0:T(8,128)} %features.3, f32[2048,128]{1,0:T(8,128)} %get-tuple-element.96.aggregated, f32[2048,256]{1,0:T(8,128)} %get-tuple-element.97.grad_pre, f32[128,256]{1,0:T(8,128)} %w_self.3), custom_call_target="tpu_custom_call" | custom-call | tf_op jit(solution)/shard_map/weight_terms/pallas_call | solution.py:291
  237.9 6.2 %all-to-all-start.1 = ((f32[32,8,384]{2,1,0:T(8,128)}), f32[32,8,384]{2,1,0:T(8,128)S(1)}, u32[]{:S(2)}, u32[]{:S(2)}) async-start(f32[32,8,384]{2,1,0:T(8,128)} %get-tuple-element.99), calls=%async_computation.1 | async-start | bytes 786432 | tf_op jit(solution)/shard_map/all_to_all | solution.py:461
  244.6 13.3 %all-to-all-done.1 = f32[32,8,384]{2,1,0:T(8,128)S(1)} async-done(((f32[32,8,384]{2,1,0:T(8,128)}), f32[32,8,384]{2,1,0:T(8,128)S(1)}, u32[]{:S(2)}, u32[]{:S(2)}) %all-to-all-start.1) | async-done | bytes 393248 | tf_op jit(solution)/shard_map/all_to_all | solution.py:461
  257.9 11.4 %psum.7 = f32[8,384]{1,0:T(8,128)S(1)} all-reduce(f32[8,384]{1,0:T(8,128)S(1)} %reduce_sum.32), channel_id=1, replica_groups=mesh['rep'=4,'row'=32] {'rep'}, use_global_device_ids=true, to_apply=%region_3.4 | all-reduce | flops 3072 | bytes 24576 | tf_op jit(solution)/shard_map/psum | solution.py:462
  269.3 27.1 %all_gather.6 = f32[256,384]{1,0:T(8,128)S(1)} all-gather(f32[8,384]{1,0:T(8,128)S(1)} %psum.7), channel_id=1, replica_groups=mesh['rep'=4,'row'=32] {'row'}, dimensions={0}, use_global_device_ids=true | all-gather | bytes 405504 | tf_op jit(solution)/shard_map/all_gather | solution.py:463
  297.7 51.6 %all-gather.2.cloned.1.call-done.grads = f32[512,128,128]{2,1,0:T(8,128)} async-done(((f32[16,128,128]{2,1,0:T(8,128)}), f32[512,128,128]{2,1,0:T(8,128)}) %all-gather.2.cloned.1.call-update) | async-done | bytes 33554448 | tf_op jit(solution)/shard_map/all_gather | solution.py:469
  349.3 17.7 %backward_tiles.1 = (f32[16,128,128]{2,1,0:T(8,128)}, f32[16,128,128]{2,1,0:T(8,128)}, f32[16,128,128]{2,1,0:T(8,128)}, f32[16,128,128]{2,1,0:T(8,128)}) custom-call(s32[257]{0:T(512)} %pad_add_fusion.3.meta, f32[128,128,128]{2,1,0:T(8,128)} %tiles.5, f32[512,128,128]{2,1,0:T(8,128)} %all-gather.2.cloned.1.call-done.grads), custom_call_target="tpu_custom_call" | custom-call | tf_op jit(solution)/shard_map/backward_tiles/pallas_call | solution.py:357
  369.4 22.4 %collective-permute-done.29.rest_1_ = f32[16,128,128]{2,1,0:T(8,128)S(1)} collective-permute-done((f32[16,128,128]{2,1,0:T(8,128)}, f32[16,128,128]{2,1,0:T(8,128)S(1)}, u32[]{:S(2)}, u32[]{:S(2)}) %collective-permute-start.29) | collective-permute-done | bytes 1048608 | tf_op jit(solution)/shard_map/ppermute | solution.py:402
  391.8 22.4 %collective-permute-done.30.rest_2_ = f32[16,128,128]{2,1,0:T(8,128)S(1)} collective-permute-done((f32[16,128,128]{2,1,0:T(8,128)}, f32[16,128,128]{2,1,0:T(8,128)S(1)}, u32[]{:S(2)}, u32[]{:S(2)}) %collective-permute-start.30) | collective-permute-done | bytes 1048608 | tf_op jit(solution)/shard_map/ppermute | solution.py:402
  416.7 6.4 %finish_grad_x.1 = f32[2048,128]{1,0:T(8,128)} custom-call(f32[2048,128]{1,0:T(8,128)} %get-tuple-element.98.own, f32[16,128,128]{2,1,0:T(8,128)} %get-tuple-element.102.rest_0_, f32[16,128,128]{2,1,0:T(8,128)} %copy-done.5, f32[16,128,128]{2,1,0:T(8,128)} %copy-done.6, f32[16,128,128]{2,1,0:T(8,128)} %copy-done.7), custom_call_target="tpu_custom_call" | custom-call | tf_op jit(solution)/shard_map/finish_grad_x/pallas_call | solution.py:376
  (145 shorter events, 48.1 us)
Async XLA Ops:
  7.2 24.3 %collective-permute-start.2 = (f32[2048,128]{1,0:T(8,128)}, f32[2048,128]{1,0:T(8,128)S(1)}, u32[]{:S(2)}, u32[]{:S(2)}) collective-permute-start(f32[2048,128]{1,0:T(8,128)} %features.3), channel_id=1, source_target_pairs={{0,96},{32,0},{64,32},{96,64},{1,97},{33,1},{65,33},{97,65},{2,98}... | collective-permute-start | bytes 3145736 | tf_op jit(solution)/shard_map/ppermute | solution.py:402
  7.5 25.5 %collective-permute-start.1 = (f32[2048,128]{1,0:T(8,128)}, f32[2048,128]{1,0:T(8,128)S(1)}, u32[]{:S(2)}, u32[]{:S(2)}) collective-permute-start(f32[2048,128]{1,0:T(8,128)} %features.3), channel_id=1, source_target_pairs={{0,64},{32,96},{64,0},{96,32},{1,65},{33,97},{65,1},{97,33},{2,66}... | collective-permute-start | bytes 3145736 | tf_op jit(solution)/shard_map/ppermute | solution.py:402
  9.9 46.8 %collective-permute-start = (f32[2048,128]{1,0:T(8,128)}, f32[2048,128]{1,0:T(8,128)S(1)}, u32[]{:S(2)}, u32[]{:S(2)}) collective-permute-start(f32[2048,128]{1,0:T(8,128)} %features.3), channel_id=1, source_target_pairs={{0,32},{32,64},{64,96},{96,0},{1,33},{33,65},{65,97},{97,1},{2,34}... | collective-permute-start | bytes 3145736 | tf_op jit(solution)/shard_map/ppermute | solution.py:402
  13.1 16.2 %all-to-all-start = ((s32[32,1,96]{2,1,0:T(1,128)}), s32[32,1,96]{2,1,0:T(1,128)S(1)}, u32[]{:S(2)}, u32[]{:S(2)}) async-start(s32[32,1,96]{2,1,0:T(1,128)} %bitcast.5), calls=%async_computation | async-start | bytes 32768 | tf_op jit(solution)/shard_map/all_to_all | solution.py:439
  22.4 326.9 %all-gather.2.cloned.1.call-start = ((), (), s32[]{:S(2)}) async-start(), calls=%async_computation.2 | async-start | bytes 34603008 | tf_op jit(solution)/shard_map/all_gather | solution.py:469
  73.9 26.4 %collective-permute-start.16 = (f32[48,32,128]{2,1,0:T(8,128)}, f32[48,32,128]{2,1,0:T(8,128)S(1)}, u32[]{:S(2)}, u32[]{:S(2)}) collective-permute-start(f32[48,32,128]{2,1,0:T(8,128)} %get-tuple-element.78), channel_id=1, source_target_pairs={{0,2},{1,3},{2,4},{3,5},{4,6},{5,7},{6,0},{7,1},{8,10},{9,11},{10,... | collective-permute-start | bytes 2359304 | tf_op jit(solution)/shard_map/ppermute | solution.py:398
  75.3 36.8 %collective-permute-start.17 = (f32[48,32,128]{2,1,0:T(8,128)}, f32[48,32,128]{2,1,0:T(8,128)S(1)}, u32[]{:S(2)}, u32[]{:S(2)}) collective-permute-start(f32[48,32,128]{2,1,0:T(8,128)} %get-tuple-element.79), channel_id=1, source_target_pairs={{0,4},{1,5},{2,6},{3,7},{4,0},{5,1},{6,2},{7,3},{8,12},{9,13},{10,... | collective-permute-start | bytes 2359304 | tf_op jit(solution)/shard_map/ppermute | solution.py:398
  77.9 34.2 %collective-permute-start.18 = (f32[48,32,128]{2,1,0:T(8,128)}, f32[48,32,128]{2,1,0:T(8,128)S(1)}, u32[]{:S(2)}, u32[]{:S(2)}) collective-permute-start(f32[48,32,128]{2,1,0:T(8,128)} %get-tuple-element.80), channel_id=1, source_target_pairs={{0,6},{1,7},{2,0},{3,1},{4,2},{5,3},{6,4},{7,5},{8,14},{9,15},{10,... | collective-permute-start | bytes 2359304 | tf_op jit(solution)/shard_map/ppermute | solution.py:398
  79.0 35.2 %collective-permute-start.19 = (f32[48,32,128]{2,1,0:T(8,128)}, f32[48,32,128]{2,1,0:T(8,128)S(1)}, u32[]{:S(2)}, u32[]{:S(2)}) collective-permute-start(f32[48,32,128]{2,1,0:T(8,128)} %get-tuple-element.82), channel_id=1, source_target_pairs={{0,8},{1,9},{2,10},{3,11},{4,12},{5,13},{6,14},{7,15},{8,16},{9,17... | collective-permute-start | bytes 2359304 | tf_op jit(solution)/shard_map/ppermute | solution.py:398
  96.9 20.9 %collective-permute-start.20 = (f32[48,32,128]{2,1,0:T(8,128)S(1)}, f32[48,32,128]{2,1,0:T(8,128)S(1)}, u32[]{:S(2)}, u32[]{:S(2)}) collective-permute-start(f32[48,32,128]{2,1,0:T(8,128)S(1)} %copy-done.31), channel_id=1, source_target_pairs={{0,16},{1,17},{2,18},{3,19},{4,20},{5,21},{6,22},{7,23},{8,24},{9,... | collective-permute-start | bytes 2359304 | tf_op jit(solution)/shard_map/ppermute | solution.py:398
  100.3 33.5 %collective-permute-start.21 = (f32[48,32,128]{2,1,0:T(8,128)}, f32[48,32,128]{2,1,0:T(8,128)S(1)}, u32[]{:S(2)}, u32[]{:S(2)}) collective-permute-start(f32[48,32,128]{2,1,0:T(8,128)} %get-tuple-element.84), channel_id=1, source_target_pairs={{0,24},{1,25},{2,26},{3,27},{4,28},{5,29},{6,30},{7,31},{8,0},{9,1... | collective-permute-start | bytes 2359304 | tf_op jit(solution)/shard_map/ppermute | solution.py:398
  112.1 36.1 %collective-permute-start.3 = (f32[48,32,128]{2,1,0:T(8,128)}, f32[48,32,128]{2,1,0:T(8,128)S(1)}, u32[]{:S(2)}, u32[]{:S(2)}) collective-permute-start(f32[48,32,128]{2,1,0:T(8,128)} %get-tuple-element.60), channel_id=1, source_target_pairs={{0,2},{1,3},{2,4},{3,5},{4,6},{5,7},{6,0},{7,1},{8,10},{9,11},{10,... | collective-permute-start | bytes 2359304 | tf_op jit(solution)/shard_map/ppermute | solution.py:398
  112.1 45.9 %collective-permute-start.4 = (f32[48,32,128]{2,1,0:T(8,128)}, f32[48,32,128]{2,1,0:T(8,128)S(1)}, u32[]{:S(2)}, u32[]{:S(2)}) collective-permute-start(f32[48,32,128]{2,1,0:T(8,128)} %get-tuple-element.61), channel_id=1, source_target_pairs={{0,4},{1,5},{2,6},{3,7},{4,0},{5,1},{6,2},{7,3},{8,12},{9,13},{10,... | collective-permute-start | bytes 2359304 | tf_op jit(solution)/shard_map/ppermute | solution.py:398
  114.1 46.6 %collective-permute-start.5 = (f32[48,32,128]{2,1,0:T(8,128)}, f32[48,32,128]{2,1,0:T(8,128)S(1)}, u32[]{:S(2)}, u32[]{:S(2)}) collective-permute-start(f32[48,32,128]{2,1,0:T(8,128)} %get-tuple-element.62), channel_id=1, source_target_pairs={{0,6},{1,7},{2,0},{3,1},{4,2},{5,3},{6,4},{7,5},{8,14},{9,15},{10,... | collective-permute-start | bytes 2359304 | tf_op jit(solution)/shard_map/ppermute | solution.py:398
  117.9 42.9 %collective-permute-start.6 = (f32[48,32,128]{2,1,0:T(8,128)}, f32[48,32,128]{2,1,0:T(8,128)S(1)}, u32[]{:S(2)}, u32[]{:S(2)}) collective-permute-start(f32[48,32,128]{2,1,0:T(8,128)} %get-tuple-element.64), channel_id=1, source_target_pairs={{0,8},{1,9},{2,10},{3,11},{4,12},{5,13},{6,14},{7,15},{8,16},{9,17... | collective-permute-start | bytes 2359304 | tf_op jit(solution)/shard_map/ppermute | solution.py:398
  133.8 27.0 %collective-permute-start.7 = (f32[48,32,128]{2,1,0:T(8,128)}, f32[48,32,128]{2,1,0:T(8,128)}, u32[]{:S(2)}, u32[]{:S(2)}) collective-permute-start(f32[48,32,128]{2,1,0:T(8,128)} %get-tuple-element.65), channel_id=1, source_target_pairs={{0,16},{1,17},{2,18},{3,19},{4,20},{5,21},{6,22},{7,23},{8,24},{9,... | collective-permute-start | bytes 2359304 | tf_op jit(solution)/shard_map/ppermute | solution.py:398
  148.2 23.8 %collective-permute-start.8 = (f32[48,32,128]{2,1,0:T(8,128)}, f32[48,32,128]{2,1,0:T(8,128)}, u32[]{:S(2)}, u32[]{:S(2)}) collective-permute-start(f32[48,32,128]{2,1,0:T(8,128)} %get-tuple-element.66), channel_id=1, source_target_pairs={{0,24},{1,25},{2,26},{3,27},{4,28},{5,29},{6,30},{7,31},{8,0},{9,1... | collective-permute-start | bytes 2359304 | tf_op jit(solution)/shard_map/ppermute | solution.py:398
  158.1 20.8 %collective-permute-start.22 = (f32[128,32,128]{2,1,0:T(8,128)}, f32[128,32,128]{2,1,0:T(8,128)S(1)}, u32[]{:S(2)}, u32[]{:S(2)}) collective-permute-start(f32[128,32,128]{2,1,0:T(8,128)} %get-tuple-element.86), channel_id=1, source_target_pairs={{0,1},{1,0},{2,3},{3,2},{4,5},{5,4},{6,7},{7,6},{8,9},{9,8},{10,11... | collective-permute-start | bytes 6291464 | tf_op jit(solution)/shard_map/ppermute | solution.py:398
  177.5 10.9 %collective-permute-start.9 = (f32[128,32,128]{2,1,0:T(8,128)}, f32[128,32,128]{2,1,0:T(8,128)S(1)}, u32[]{:S(2)}, u32[]{:S(2)}) collective-permute-start(f32[128,32,128]{2,1,0:T(8,128)} %get-tuple-element.68), channel_id=1, source_target_pairs={{0,1},{1,0},{2,3},{3,2},{4,5},{5,4},{6,7},{7,6},{8,9},{9,8},{10,11... | collective-permute-start | bytes 6291464 | tf_op jit(solution)/shard_map/ppermute | solution.py:398
  185.3 14.3 %collective-permute-start.24 = (f32[16,32,128]{2,1,0:T(8,128)}, f32[16,32,128]{2,1,0:T(8,128)S(1)}, u32[]{:S(2)}, u32[]{:S(2)}) collective-permute-start(f32[16,32,128]{2,1,0:T(8,128)} %get-tuple-element.89), channel_id=1, source_target_pairs={{0,16},{1,17},{2,18},{3,19},{4,20},{5,21},{6,22},{7,23},{8,24},{9,... | collective-permute-start | bytes 786440 | tf_op jit(solution)/shard_map/ppermute | solution.py:398
  187.3 12.3 %collective-permute-start.25 = (f32[16,32,128]{2,1,0:T(8,128)}, f32[16,32,128]{2,1,0:T(8,128)S(1)}, u32[]{:S(2)}, u32[]{:S(2)}) collective-permute-start(f32[16,32,128]{2,1,0:T(8,128)} %get-tuple-element.90), channel_id=1, source_target_pairs={{0,24},{1,25},{2,26},{3,27},{4,28},{5,29},{6,30},{7,31},{8,0},{9,1... | collective-permute-start | bytes 786440 | tf_op jit(solution)/shard_map/ppermute | solution.py:398
  188.0 13.2 %collective-permute-start.26 = (f32[16,32,128]{2,1,0:T(8,128)}, f32[16,32,128]{2,1,0:T(8,128)S(1)}, u32[]{:S(2)}, u32[]{:S(2)}) collective-permute-start(f32[16,32,128]{2,1,0:T(8,128)} %get-tuple-element.92), channel_id=1, source_target_pairs={{0,2},{1,3},{2,4},{3,5},{4,6},{5,7},{6,0},{7,1},{8,10},{9,11},{10,... | collective-permute-start | bytes 786440 | tf_op jit(solution)/shard_map/ppermute | solution.py:398
  188.4 14.8 %collective-permute-start.27 = (f32[16,32,128]{2,1,0:T(8,128)}, f32[16,32,128]{2,1,0:T(8,128)S(1)}, u32[]{:S(2)}, u32[]{:S(2)}) collective-permute-start(f32[16,32,128]{2,1,0:T(8,128)} %get-tuple-element.93), channel_id=1, source_target_pairs={{0,4},{1,5},{2,6},{3,7},{4,0},{5,1},{6,2},{7,3},{8,12},{9,13},{10,... | collective-permute-start | bytes 786440 | tf_op jit(solution)/shard_map/ppermute | solution.py:398
  199.6 14.1 %collective-permute-start.10 = (f32[16,32,128]{2,1,0:T(8,128)}, f32[16,32,128]{2,1,0:T(8,128)S(1)}, u32[]{:S(2)}, u32[]{:S(2)}) collective-permute-start(f32[16,32,128]{2,1,0:T(8,128)} %get-tuple-element.70), channel_id=1, source_target_pairs={{0,8},{1,9},{2,10},{3,11},{4,12},{5,13},{6,14},{7,15},{8,16},{9,17... | collective-permute-start | bytes 786440 | tf_op jit(solution)/shard_map/ppermute | solution.py:398
  199.6 14.1 %collective-permute-start.11 = (f32[16,32,128]{2,1,0:T(8,128)}, f32[16,32,128]{2,1,0:T(8,128)S(1)}, u32[]{:S(2)}, u32[]{:S(2)}) collective-permute-start(f32[16,32,128]{2,1,0:T(8,128)} %get-tuple-element.71), channel_id=1, source_target_pairs={{0,16},{1,17},{2,18},{3,19},{4,20},{5,21},{6,22},{7,23},{8,24},{9,... | collective-permute-start | bytes 786440 | tf_op jit(solution)/shard_map/ppermute | solution.py:398
  201.2 13.3 %collective-permute-start.12 = (f32[16,32,128]{2,1,0:T(8,128)}, f32[16,32,128]{2,1,0:T(8,128)S(1)}, u32[]{:S(2)}, u32[]{:S(2)}) collective-permute-start(f32[16,32,128]{2,1,0:T(8,128)} %get-tuple-element.72), channel_id=1, source_target_pairs={{0,24},{1,25},{2,26},{3,27},{4,28},{5,29},{6,30},{7,31},{8,0},{9,1... | collective-permute-start | bytes 786440 | tf_op jit(solution)/shard_map/ppermute | solution.py:398
  203.2 11.3 %collective-permute-start.13 = (f32[16,32,128]{2,1,0:T(8,128)}, f32[16,32,128]{2,1,0:T(8,128)S(1)}, u32[]{:S(2)}, u32[]{:S(2)}) collective-permute-start(f32[16,32,128]{2,1,0:T(8,128)} %get-tuple-element.74), channel_id=1, source_target_pairs={{0,2},{1,3},{2,4},{3,5},{4,6},{5,7},{6,0},{7,1},{8,10},{9,11},{10,... | collective-permute-start | bytes 786440 | tf_op jit(solution)/shard_map/ppermute | solution.py:398
  203.7 11.7 %collective-permute-start.14 = (f32[16,32,128]{2,1,0:T(8,128)}, f32[16,32,128]{2,1,0:T(8,128)S(1)}, u32[]{:S(2)}, u32[]{:S(2)}) collective-permute-start(f32[16,32,128]{2,1,0:T(8,128)} %get-tuple-element.75), channel_id=1, source_target_pairs={{0,4},{1,5},{2,6},{3,7},{4,0},{5,1},{6,2},{7,3},{8,12},{9,13},{10,... | collective-permute-start | bytes 786440 | tf_op jit(solution)/shard_map/ppermute | solution.py:398
  237.9 20.0 %all-to-all-start.1 = ((f32[32,8,384]{2,1,0:T(8,128)}), f32[32,8,384]{2,1,0:T(8,128)S(1)}, u32[]{:S(2)}, u32[]{:S(2)}) async-start(f32[32,8,384]{2,1,0:T(8,128)} %get-tuple-element.99), calls=%async_computation.1 | async-start | bytes 786432 | tf_op jit(solution)/shard_map/all_to_all | solution.py:461
  367.0 24.8 %collective-permute-start.29 = (f32[16,128,128]{2,1,0:T(8,128)}, f32[16,128,128]{2,1,0:T(8,128)S(1)}, u32[]{:S(2)}, u32[]{:S(2)}) collective-permute-start(f32[16,128,128]{2,1,0:T(8,128)} %get-tuple-element.103), channel_id=1, source_target_pairs={{0,32},{32,64},{64,96},{96,0},{1,33},{33,65},{65,97},{97,1},{2,34}... | collective-permute-start | bytes 3145736 | tf_op jit(solution)/shard_map/ppermute | solution.py:402
  367.9 46.3 %collective-permute-start.30 = (f32[16,128,128]{2,1,0:T(8,128)}, f32[16,128,128]{2,1,0:T(8,128)S(1)}, u32[]{:S(2)}, u32[]{:S(2)}) collective-permute-start(f32[16,128,128]{2,1,0:T(8,128)} %get-tuple-element.104), channel_id=1, source_target_pairs={{0,64},{32,96},{64,0},{96,32},{1,65},{33,97},{65,1},{97,33},{2,66}... | collective-permute-start | bytes 3145736 | tf_op jit(solution)/shard_map/ppermute | solution.py:402
  368.5 47.3 %collective-permute-start.31 = (f32[16,128,128]{2,1,0:T(8,128)}, f32[16,128,128]{2,1,0:T(8,128)S(1)}, u32[]{:S(2)}, u32[]{:S(2)}) collective-permute-start(f32[16,128,128]{2,1,0:T(8,128)} %get-tuple-element.105), channel_id=1, source_target_pairs={{0,96},{32,0},{64,32},{96,64},{1,97},{33,1},{65,33},{97,65},{2,98}... | collective-permute-start | bytes 3145736 | tf_op jit(solution)/shard_map/ppermute | solution.py:402
  (36 other events, 560.6 us)
Sparse Core Ops, SparseCore 0:
  230.4 118.8 all-gather.1

commit v2 on v1

--- a/solution.py
+++ b/solution.py
@@ -17,13 +17,15 @@
 N_REP = 4
 SIDE = 4
 N_ROW = 32
-ROW_PARTS = 2
-PART = BLOCK // ROW_PARTS
-HALF = PART // 2
+SUMMED = 48
+HALF = (BLOCK - SUMMED) // 2
 MSG = 2 * SIDE * SLOTS
 DENSE = SIDE * BLOCKS_DEV
+GATHERED = 80
+REPLIED = FEAT - GATHERED
+REPLY = REPLIED // 2
 ORDER = ((0, 1), (0, 2), (1, 2), (1, 1), (0, 3), (1, 3))
-STEP = 8
+STEP = 32
 F32 = jnp.float32
 BF16 = jnp.bfloat16
 VMEM_LIMIT = 56 * 1024 * 1024
@@ -59,56 +61,78 @@
 ANY = pl.BlockSpec(memory_space=pl.ANY)
 
 
-def forward_kernel(meta, tiles, f0, f1, f2, f3, *rest):
-    outs, (slab, send, sems) = rest[: 2 * SIDE], rest[2 * SIDE :]
+SOURCES = 7
+
+
+def fill_slab(slab, refs):
+    first = 0
+    for ref in refs:
+        high, low = split(ref[...])
+        slab[first : first + ref.shape[0], :, :FEAT] = high
+        slab[first : first + ref.shape[0], :, FEAT:] = low
+        first += ref.shape[0]
+
+
+def forward_product(tile, source):
+    rows = tile.shape[0]
+    both = dot(jnp.concatenate(split(tile), axis=0), source, NN)
+    return both[:rows, :FEAT] + both[rows:, :FEAT] + both[:rows, FEAT:]
+
+
+def forward_kernel(meta, tiles, *rest):
+    sources, outs = rest[:SOURCES], rest[SOURCES : SOURCES + 2 * SIDE + 1]
+    slab, send, acc, sems = rest[SOURCES + 2 * SIDE + 1 :]
     step = pl.program_id(0)
 
     @pl.when(step == 0)
     def _():
-        for d, ref in enumerate((f0, f1, f2, f3)):
-            high, low = split(ref[...])
-            slab[d * BLOCKS_DEV : (d + 1) * BLOCKS_DEV, :, :FEAT] = high
-            slab[d * BLOCKS_DEV : (d + 1) * BLOCKS_DEV, :, FEAT:] = low
+        fill_slab(slab, sources)
+        acc[...] = jnp.zeros_like(acc)
 
     for t in range(STEP):
         i = step * STEP + t
-        both = dot(jnp.concatenate(split(tiles[t]), axis=0), slab[meta[i]], NN)
-        part = both[:PART, :FEAT] + both[PART:, :FEAT] + both[:PART, FEAT:]
+        part = forward_product(tiles[t], slab[meta[i]])
         send[meta[TILES_DEV + i]] = part[:HALF]
-        send[meta[2 * TILES_DEV + i]] = part[HALF:]
+        send[meta[2 * TILES_DEV + i]] = part[HALF : 2 * HALF]
+        acc[meta[3 * TILES_DEV + i]] += part[2 * HALF :]
 
     @pl.when(step == pl.num_programs(0) - 1)
     def _():
         copies = [
             pltpu.make_async_copy(send.at[pl.ds(k * MSG, MSG)], out, sems.at[k])
-            for k, out in enumerate(outs)
+            for k, out in enumerate(outs[:-1])
         ]
+        copies.append(pltpu.make_async_copy(acc, outs[-1], sems.at[2 * SIDE]))
         for copy in copies:
             copy.start()
         for copy in copies:
             copy.wait()
 
 
-def forward_tiles(meta, tile_values, parts, number):
+def forward_tiles(meta, tile_values, sources):
+    blocks = N_ROW * BLOCKS_DEV
+    sources = [x.reshape(-1, BLOCK, FEAT) for x in sources]
     spec = pltpu.PrefetchScalarGridSpec(
         num_scalar_prefetch=1,
         grid=(TILES_DEV // STEP,),
-        in_specs=[pl.BlockSpec((STEP, PART, BLOCK), lambda i, _: (i, number, 0))]
-        + [whole((BLOCKS_DEV, BLOCK, FEAT))] * N_REP,
-        out_specs=[ANY] * (2 * SIDE),
+        in_specs=[pl.BlockSpec((STEP, BLOCK, BLOCK), lambda i, _: (i, 0, 0))]
+        + [whole(x.shape) for x in sources],
+        out_specs=[ANY] * (2 * SIDE + 1),
         scratch_shapes=[
             pltpu.VMEM((N_REP * BLOCKS_DEV, BLOCK, 2 * FEAT), BF16),
             pltpu.VMEM((2 * SIDE * MSG, HALF, FEAT), F32),
-            pltpu.SemaphoreType.DMA((2 * SIDE,)),
+            pltpu.VMEM((blocks, SUMMED, FEAT), F32),
+            pltpu.SemaphoreType.DMA((2 * SIDE + 1,)),
         ],
     )
     return pl.pallas_call(
         forward_kernel,
         grid_spec=spec,
-        out_shape=[jax.ShapeDtypeStruct((MSG, HALF, FEAT), F32)] * (2 * SIDE),
+        out_shape=[jax.ShapeDtypeStruct((MSG, HALF, FEAT), F32)] * (2 * SIDE)
+        + [jax.ShapeDtypeStruct((blocks, SUMMED, FEAT), F32)],
         compiler_params=params(),
         name="forward_tiles",
-    )(meta, tile_values, *[p.reshape(BLOCKS_DEV, BLOCK, FEAT) for p in parts])
+    )(meta, tile_values, *sources)
 
 
 def combine_kernel(ids, place, *rest):
@@ -207,16 +231,17 @@
     )(keep, taken)
 
 
-PER = 2
+PER = 4
 
 
 def layer_kernel(features, cotangent, w_self, w_neigh, bias, *rest):
-    sums, (output, grad_pre, aggregated, grads) = rest[:-4], rest[-4:]
+    sums, (output, grad_pre, aggregated, gathered, first, second) = rest[:-6], rest[-6:]
     halves = []
     for b in range(PER):
-        for piece in range(2 * ROW_PARTS):
+        for piece in range(2):
             refs = sums[piece * SIDE : (piece + 1) * SIDE]
             halves.append((refs[0][b] + refs[1][b]) + (refs[2][b] + refs[3][b]))
+        halves.append(sums[-1][b])
     agg = jnp.concatenate(halves, axis=0)
     aggregated[...] = agg
     w_neigh_split = split(w_neigh[...])
@@ -232,7 +257,10 @@
     high, low = split(grad)
     for b in range(PER):
         rows = slice(b * BLOCK, (b + 1) * BLOCK)
-        grads[b] = dot3(w_neigh_split, (high[rows], low[rows]), NT)
+        turned = dot3(w_neigh_split, (high[rows], low[rows]), NT)
+        gathered[b] = turned[:GATHERED]
+        first[b] = turned[GATHERED : GATHERED + REPLY]
+        second[b] = turned[GATHERED + REPLY :]
 
 
 def layer(features, cotangent, w_self, w_neigh, bias, sums):
@@ -243,13 +271,16 @@
         layer_kernel,
         grid=(BLOCKS_DEV // PER,),
         in_specs=[row(FEAT), row(HID), whole((FEAT, HID)), whole((FEAT, HID)), whole((1, HID))]
-        + [block(HALF)] * (2 * ROW_PARTS * SIDE),
-        out_specs=[row(HID), row(HID), row(FEAT), block(FEAT)],
+        + [block(HALF)] * (2 * SIDE)
+        + [block(SUMMED)],
+        out_specs=[row(HID), row(HID), row(FEAT), block(GATHERED), block(REPLY), block(REPLY)],
         out_shape=[
             jax.ShapeDtypeStruct((nodes, HID), F32),
             jax.ShapeDtypeStruct((nodes, HID), F32),
             jax.ShapeDtypeStruct((nodes, FEAT), F32),
-            jax.ShapeDtypeStruct((BLOCKS_DEV, FEAT, BLOCK), F32),
+            jax.ShapeDtypeStruct((BLOCKS_DEV, GATHERED, BLOCK), F32),
+            jax.ShapeDtypeStruct((BLOCKS_DEV, REPLY, BLOCK), F32),
+            jax.ShapeDtypeStruct((BLOCKS_DEV, REPLY, BLOCK), F32),
         ],
         compiler_params=params(),
         name="layer",
@@ -303,10 +334,83 @@
     )(features, aggregated, grad_pre, w_self)
 
 
-def backward_kernel(meta, tiles, grads, *rest):
+def reply_kernel(ids, place, mine, taken, *rest):
+    outs, (dense, reply, in_sems, out_sems) = rest[: 2 * SIDE], rest[2 * SIDE :]
+    z, y, c = place[0], place[1], place[2]
+    loads = []
+    for n, ref in enumerate((mine, taken)):
+        copy = pltpu.make_async_copy(ref, dense.at[n], in_sems.at[n])
+        copy.start()
+        loads.append(copy)
+    for copy in loads:
+        copy.wait()
+    stores = []
+    for path in range(2):
+        for d in range(SIDE):
+            if path == 0:
+                holder = (z * SIDE + (y + SIDE - d) % SIDE) * 2 + c
+            else:
+                holder = ((z + SIDE - d) % SIDE * SIDE + y) * 2 + c
+            base = holder * (2 * MSG) + path * MSG
+            k = path * SIDE + d
+            for s in range(MSG):
+                other, chip = s // (SIDE * SLOTS), s // SLOTS % SIDE
+                away = ((z if path == 0 else y) + SIDE - chip) % SIDE
+                block = jnp.minimum(ids[base + s], BLOCKS_DEV - 1)
+                reply[k, s] = dense[other, (path * SIDE + away) * BLOCKS_DEV + block]
+            copy = pltpu.make_async_copy(reply.at[k], outs[k], out_sems.at[k])
+            copy.start()
+            stores.append(copy)
+    for copy in stores:
+        copy.wait()
+
+
+def make_replies(ids, place, mine, taken):
+    spec = pltpu.PrefetchScalarGridSpec(
+        num_scalar_prefetch=2,
+        grid=(1,),
+        in_specs=[ANY] * 2,
+        out_specs=[ANY] * (2 * SIDE),
+        scratch_shapes=[
+            pltpu.VMEM((2, 2 * DENSE, REPLY, BLOCK), F32),
+            pltpu.VMEM((2 * SIDE, MSG, REPLY, BLOCK), F32),
+            pltpu.SemaphoreType.DMA((2,)),
+            pltpu.SemaphoreType.DMA((2 * SIDE,)),
+        ],
+    )
+    return pl.pallas_call(
+        reply_kernel,
+        grid_spec=spec,
+        out_shape=[jax.ShapeDtypeStruct((MSG, REPLY, BLOCK), F32)] * (2 * SIDE),
+        compiler_params=params(),
+        name="make_replies",
+    )(ids, place, mine, taken)
+
+
+def add_product(acc, row, grad, tile):
+    depth = grad.shape[0]
+    high, low = split(tile)
+    both = dot(jnp.concatenate(split(grad), axis=0), high, NN)
+    acc[row] += both[:depth] + both[depth:] + dot(grad.astype(BF16), low, NN)
+
+
+def hand_out(meta, acc, outs, sems):
+    rep = meta[4 * TILES_DEV]
+    copies = [
+        pltpu.make_async_copy(
+            acc.at[pl.ds((rep + d) % N_REP * BLOCKS_DEV, BLOCKS_DEV)], out, sems.at[d]
+        )
+        for d, out in enumerate(outs)
+    ]
+    for copy in copies:
+        copy.start()
+    for copy in copies:
+        copy.wait()
+
+
+def gathered_kernel(meta, tiles, grads, *rest):
     outs, (got, acc, sems, out_sems) = rest[:N_REP], rest[N_REP:]
     step = pl.program_id(0)
-    steps = pl.num_programs(0)
 
     @pl.when(step == 0)
     def _():
@@ -321,62 +425,102 @@
 
     pltpu.make_async_copy(grads.at[pl.ds(0, STEP)], got.at[step], sems.at[step]).wait()
     for t in range(STEP):
-        grad = jnp.concatenate(split(got[step, t]), axis=0)
-        both = dot(grad, jnp.concatenate(split(tiles[t]), axis=1), NN)
-        part = both[:FEAT, :BLOCK] + both[FEAT:, :BLOCK] + both[:FEAT, BLOCK:]
-        acc[meta[step * STEP + t]] += part
-
-    @pl.when(step == steps - 1)
-    def _():
-        rep = meta[2 * TILES_DEV]
-        copies = [
-            pltpu.make_async_copy(
-                acc.at[pl.ds((rep + d) % N_REP * BLOCKS_DEV, BLOCKS_DEV)], out, out_sems.at[d]
-            )
-            for d, out in enumerate(outs)
-        ]
-        for copy in copies:
-            copy.start()
-        for copy in copies:
-            copy.wait()
-
-
-def backward_tiles(meta, tile_values, grads):
+        add_product(acc, meta[step * STEP + t], got[step, t], tiles[t])
+
+    @pl.when(step == pl.num_programs(0) - 1)
+    def _():
+        hand_out(meta, acc, outs, out_sems)
+
+
+def gathered_tiles(meta, tile_values, grads):
     spec = pltpu.PrefetchScalarGridSpec(
         num_scalar_prefetch=1,
         grid=(TILES_DEV // STEP,),
         in_specs=[pl.BlockSpec((STEP, BLOCK, BLOCK), lambda i, _: (i, 0, 0)), ANY],
         out_specs=[ANY] * N_REP,
         scratch_shapes=[
-            pltpu.VMEM((TILES_DEV // STEP, STEP, FEAT, BLOCK), F32),
-            pltpu.VMEM((N_REP * BLOCKS_DEV, FEAT, BLOCK), F32),
+            pltpu.VMEM((TILES_DEV // STEP, STEP, GATHERED, BLOCK), F32),
+            pltpu.VMEM((N_REP * BLOCKS_DEV, GATHERED, BLOCK), F32),
             pltpu.SemaphoreType.DMA((TILES_DEV // STEP,)),
             pltpu.SemaphoreType.DMA((N_REP,)),
         ],
     )
     return pl.pallas_call(
-        backward_kernel,
+        gathered_kernel,
         grid_spec=spec,
-        out_shape=[jax.ShapeDtypeStruct((BLOCKS_DEV, FEAT, BLOCK), F32)] * N_REP,
-        compiler_params=params(),
-        name="backward_tiles",
+        out_shape=[jax.ShapeDtypeStruct((BLOCKS_DEV, GATHERED, BLOCK), F32)] * N_REP,
+        compiler_params=params(),
+        name="gathered_tiles",
     )(meta, tile_values, grads)
+
+
+def replied_kernel(meta, tiles, *rest):
+    replies, (out, got, acc, sems, out_sem) = rest[: 2 * SIDE], rest[2 * SIDE :]
+    step = pl.program_id(0)
+
+    @pl.when(step == 0)
+    def _():
+        copies = [
+            pltpu.make_async_copy(ref, got.at[pl.ds(k * MSG, MSG)], sems.at[k])
+            for k, ref in enumerate(replies)
+        ]
+        for copy in copies:
+            copy.start()
+        acc[...] = jnp.zeros_like(acc)
+        for copy in copies:
+            copy.wait()
+
+    for t in range(STEP):
+        i = step * STEP + t
+        grad = jnp.concatenate(
+            [got[meta[2 * TILES_DEV + i]], got[meta[3 * TILES_DEV + i]]], axis=0
+        )
+        add_product(acc, meta[i], grad, tiles[t])
+
+    @pl.when(step == pl.num_programs(0) - 1)
+    def _():
+        copy = pltpu.make_async_copy(acc, out, out_sem)
+        copy.start()
+        copy.wait()
+
+
+def replied_tiles(meta, tile_values, replies):
+    spec = pltpu.PrefetchScalarGridSpec(
+        num_scalar_prefetch=1,
+        grid=(TILES_DEV // STEP,),
+        in_specs=[pl.BlockSpec((STEP, BLOCK, BLOCK), lambda i, _: (i, 0, 0))] + [ANY] * (2 * SIDE),
+        out_specs=ANY,
+        scratch_shapes=[
+            pltpu.VMEM((2 * SIDE * MSG, REPLY, BLOCK), F32),
+            pltpu.VMEM((N_REP * BLOCKS_DEV, REPLIED, BLOCK), F32),
+            pltpu.SemaphoreType.DMA((2 * SIDE,)),
+            pltpu.SemaphoreType.DMA,
+        ],
+    )
+    return pl.pallas_call(
+        replied_kernel,
+        grid_spec=spec,
+        out_shape=jax.ShapeDtypeStruct((N_REP * BLOCKS_DEV, REPLIED, BLOCK), F32),
+        compiler_params=params(),
+        name="replied_tiles",
+    )(meta, tile_values, *replies)
 
 
 def finish_kernel(own, *rest):
     sums, out = rest[:-1], rest[-1]
     for b in range(PER):
-        total = (sums[0][b] + sums[1][b]) + (sums[2][b] + sums[3][b])
+        pieces = [(sums[0][b] + sums[1][b]) + (sums[2][b] + sums[3][b]), sums[4][b]]
         rows = slice(b * BLOCK, (b + 1) * BLOCK)
-        out[rows, :] = own[rows, :] + total.T
+        out[rows, :] = own[rows, :] + jnp.concatenate(pieces, axis=0).T
 
 
 def finish(own, sums):
     row = pl.BlockSpec((PER * BLOCK, FEAT), lambda i: (i, 0))
+    block = lambda depth: pl.BlockSpec((PER, depth, BLOCK), lambda i: (i, 0, 0))
     return pl.pallas_call(
         finish_kernel,
         grid=(BLOCKS_DEV // PER,),
-        in_specs=[row] + [pl.BlockSpec((PER, FEAT, BLOCK), lambda i: (i, 0, 0))] * N_REP,
+        in_specs=[row] + [block(GATHERED)] * N_REP + [block(REPLIED)],
         out_specs=row,
         out_shape=jax.ShapeDtypeStruct(own.shape, F32),
         compiler_params=params(),
@@ -420,9 +564,10 @@
     pos_z = ((o_z - z) % SIDE + SIDE) * MSG + (o_core * SIDE + o_y) * SLOTS + rank
     src_rep, src_block = tile_source // BLOCKS_DEV, tile_source % BLOCKS_DEV
     src = (rep - src_rep) % N_REP * BLOCKS_DEV + src_block
-    forward_meta = jnp.concatenate([src, pos_y, pos_z]).astype(jnp.int32)
+    dest = owner * BLOCKS_DEV + tile_local
+    forward_meta = jnp.concatenate([src, pos_y, pos_z, dest]).astype(jnp.int32)
     backward_meta = jnp.concatenate(
-        [tile_source, owner * BLOCKS_DEV + tile_local, rep[None]]
+        [tile_source, dest, pos_y, pos_z, rep[None]]
     ).astype(jnp.int32)
     place = jnp.stack([z, y, c]).astype(jnp.int32)
 
@@ -438,40 +583,73 @@
     ).astype(jnp.int32)
     ids = lax.all_to_all(to_send, "row", split_axis=0, concat_axis=0, tiled=True).reshape(-1)
 
-    forward_meta, ids = lax.optimization_barrier((forward_meta, ids))
-    parts = [features] + [shift_rep(features, d) for d in (1, 2, 3)]
-    sums = []
-    for number in range(ROW_PARTS):
-        got = list(forward_tiles(forward_meta, tile_values, parts, number))
-        for path, d in ORDER:
-            k = path * SIDE + d
-            got[k] = shift(got[k], 0, d) if path == 0 else shift(got[k], d, 0)
-        keep, give = combine(ids, place, got)
-        dense = list(add_cores(keep, shift(give, 0, 0, 1)))
-        for path, d in ORDER:
-            k = path * SIDE + d
-            dense[k] = shift(dense[k], d, 0) if path == 0 else shift(dense[k], 0, d)
-        sums.extend(dense)
-
-    output, grad_pre, aggregated, grads = layer(
-        features, cotangent, w_self, w_neigh, bias[None, :], sums
-    )
+    half = features.shape[0] // 2
+    low, high = features[:half], features[half:]
+    low_1, high_3 = shift_rep(low, 1), shift_rep(high, 3)
+    high_1, low_3 = shift_rep(high, 1), shift_rep(low, 3)
+    to_low, to_high, forward_meta, ids = lax.optimization_barrier(
+        (low_1, high_3, forward_meta, ids)
+    )
+    low_2, high_2 = shift_rep(to_low, 1), shift_rep(to_high, 3)
+    *got, all_sums = forward_tiles(
+        forward_meta,
+        tile_values,
+        [features, low_1, high_1, low_2, high_2, low_3, high_3],
+    )
+    last_rows = lax.psum_scatter(
+        all_sums.reshape(-1, FEAT), "row", scatter_dimension=0, tiled=True
+    ).reshape(BLOCKS_DEV, SUMMED, FEAT)
+    for path, d in ORDER:
+        k = path * SIDE + d
+        got[k] = shift(got[k], 0, d) if path == 0 else shift(got[k], d, 0)
+    keep, give = combine(ids, place, got)
+    sums = list(add_cores(keep, shift(give, 0, 0, 1)))
+    for path, d in ORDER:
+        k = path * SIDE + d
+        sums[k] = shift(sums[k], d, 0) if path == 0 else shift(sums[k], 0, d)
+
+    output, grad_pre, aggregated, to_all, first, second = layer(
+        features, cotangent, w_self, w_neigh, bias[None, :], sums + [last_rows]
+    )
+
+    gathered = lax.all_gather(to_all, "row", axis=0, tiled=True)
+    dense = [first] * SIDE + [second] * SIDE
+    for path, d in ORDER:
+        dense[path * SIDE + d] = shift(first, d, 0) if path == 0 else shift(second, 0, d)
+    mine = jnp.concatenate(dense, axis=0)
+    replies = list(make_replies(ids, place, mine, shift(mine, 0, 0, 1)))
+    for path, d in ORDER:
+        k = path * SIDE + d
+        replies[k] = shift(replies[k], 0, -d) if path == 0 else shift(replies[k], -d, 0)
+    first = ORDER[0][0] * SIDE + ORDER[0][1]
+    grad_pre, replies[first] = lax.optimization_barrier((grad_pre, replies[first]))
 
     own, terms = weight_terms(features, aggregated, grad_pre, w_self)
     dealt = lax.all_to_all(terms, "row", split_axis=0, concat_axis=0, tiled=True)
-    mine = lax.psum(jnp.sum(dealt, axis=0), "rep")
-    full = lax.all_gather(mine, "row", axis=0, tiled=True)
+    backward_meta, dealt = lax.optimization_barrier((backward_meta, dealt))
+    slab = replied_tiles(backward_meta, tile_values, replies)
+    replied = lax.psum_scatter(
+        slab.reshape(-1, BLOCK), "rep", scatter_dimension=0, tiled=True
+    ).reshape(BLOCKS_DEV, REPLIED, BLOCK)
+    row_sum = jnp.sum(dealt, axis=0)
+    by_rep = jnp.stack([shift_rep(row_sum, d) for d in range(N_REP)])
+    by_rep = jnp.take(by_rep, (rep - jnp.arange(N_REP)) % N_REP, axis=0)
+    total = jnp.sum(by_rep, axis=0)
+    slab = list(gathered_tiles(backward_meta, tile_values, gathered))
+    back = [slab[0]] + [shift_rep(slab[d], d) for d in (1, 2, 3)] + [replied]
+    total, back[1] = lax.optimization_barrier((total, back[1]))
+    full = lax.all_to_all(
+        jnp.broadcast_to(total[None], (N_ROW,) + total.shape),
+        "row",
+        split_axis=0,
+        concat_axis=0,
+        tiled=True,
+    ).reshape(2 * FEAT, HID + 128)
     scale = 1.0 / math.sqrt(features.shape[0] * N_REP * N_ROW)
     grad_self = full[:FEAT, :HID] * scale
     grad_neigh = full[FEAT:, :HID] * scale
     grad_bias = jnp.concatenate([full[0, HID:], full[4, HID:]]) * scale
 
-    gathered = lax.all_gather(grads, "row", axis=0, tiled=True)
-    backward_meta, grad_self, grad_neigh, grad_bias = lax.optimization_barrier(
-        (backward_meta, grad_self, grad_neigh, grad_bias)
-    )
-    slab = backward_tiles(backward_meta, tile_values, gathered)
-    back = [slab[0]] + [shift_rep(slab[d], d) for d in (1, 2, 3)]
     grad_x = finish(own, back)
     return (output, grad_x, grad_self, grad_neigh, grad_bias)
 

time: 433 us -> 388 us (0.90)
  starting transfers between devices: 57.9 us -> 113 us
  waiting for transfers between devices: 215 us -> 170 us
  blocking collectives: 38.5 us -> 0 us
  Pallas kernels: 91.4 us -> 70.4 us
  local copies, waits for them, and re-layouts: 6.26 us -> 13.8 us
    all_gather x1, waiting for transfers between devices: 51.6 us -> 3.57 us  [local(): gathered = lax.all_gather(to_all, 'row', axis=0, tiled=True)]
    ppermute x6 -> x12, waiting for transfers between devices: 72 us -> 34.8 us  [shift_rep(): lax.ppermute(x, 'rep', [(i, (i + d) % N_REP) for i in range(N_REP)])]
    all_gather x1 -> x0, blocking collectives: 27.1 us -> none  [local(): full = lax.all_gather(mine, 'row', axis=0, tiled=True)]
    ppermute x26, starting transfers between devices: 37.2 us -> 61.9 us  [shift(): return lax.ppermute(x, 'row', pairs)]
    all_to_all x0 -> x1, starting transfers between devices: none -> 18 us  [local(): lax.all_to_all(jnp.broadcast_to(total[None], (N_ROW,) + total.shape), 'ro...]
    ppermute x26, waiting for transfers between devices: 72.2 us -> 88.7 us  [shift(): return lax.ppermute(x, 'row', pairs)]
    pallas_call x2 -> x1, Pallas kernels: 32.5 us -> 17.9 us  [forward_tiles(): pl.pallas_call(forward_kernel, grid_spec=spec, out_shape=[jax.ShapeDtypeS...]
    reduce_scatter x0 -> x2, waiting for transfers between devices: none -> 13.2 us  [the longest x1 13.2 us: local(): lax.psum_scatter(all_sums.reshape(-1, FEAT), 'row', scatter_dimension=0,...]
  transfers between devices with their start and end apart: 35 -> 44, of which waited for: 19 -> 24; matrix products, arithmetic and copies ran while one was open for 2% -> 2% of each run, Pallas kernels for 10% -> 12%
where the time goes in v2:
time: 388 us; the launch traced here: 387 us
  waiting for transfers between devices  170 us (44%)
  starting transfers between devices  113 us (29%)
  Pallas kernels  70.4 us (18%)
  between operations  14.4 us (4%)
  local copies, waits for them, and re-layouts  13.8 us (4%)
  other arithmetic  4.39 us (1%)
    ppermute x26, waiting for transfers between devices, shift(): return lax.ppermute(x, 'row', pairs)  88.7 us
    ppermute x26, starting transfers between devices, shift(): return lax.ppermute(x, 'row', pairs)  61.9 us
    ppermute x12, waiting for transfers between devices, shift_rep(): lax.ppermute(x, 'rep', [(i, (i + d) % N_REP) for i in range(N_REP)])  34.8 us
    all_to_all x1, waiting for transfers between devices, local(): lax.all_to_all(terms, 'row', split_axis=0, concat_axis=0, tiled=True)  18.7 us
    all_to_all x1, starting transfers between devices, local(): lax.all_to_all(jnp.broadcast_to(total[None], (N_ROW,) + total.shape), 'ro...  18 us
    pallas_call x1, Pallas kernels, forward_tiles(): pl.pallas_call(forward_kernel, grid_spec=spec, out_shape=[jax.ShapeDtypeS...  17.9 us
    reduce_scatter x1, waiting for transfers between devices, local(): lax.psum_scatter(all_sums.reshape(-1, FEAT), 'row', scatter_dimension=0,...  13.2 us
    ppermute x12, starting transfers between devices, shift_rep(): lax.ppermute(x, 'rep', [(i, (i + d) % N_REP) for i in range(N_REP)])  12 us
  transfers between devices with their start and end apart: 44, of which 24 were waited for; matrix products, arithmetic and copies ran while one was open for 2% of the time, Pallas kernels for 12%

profile of v2, /device:TPU:5, one launch (start us, length us, event | category | flops | bytes accessed | tf_op | source)
XLA Modules:
  0.0 386.7 jit_solution(7489484182333966036)
XLA Ops:
  13.9 9.6 %all-to-all-start = ((s32[32,1,96]{2,1,0:T(1,128)}), s32[32,1,96]{2,1,0:T(1,128)S(1)}, u32[]{:S(2)}, u32[]{:S(2)}) async-start(s32[32,1,96]{2,1,0:T(1,128)} %bitcast.5), calls=%async_computation | async-start | bytes 32768 | tf_op jit(solution)/shard_map/all_to_all | solution.py:584
  24.2 6.2 %all-to-all-done = s32[32,1,96]{2,1,0:T(1,128)S(1)} async-done(((s32[32,1,96]{2,1,0:T(1,128)}), s32[32,1,96]{2,1,0:T(1,128)S(1)}, u32[]{:S(2)}, u32[]{:S(2)}) %all-to-all-start) | async-done | bytes 12320 | tf_op jit(solution)/shard_map/all_to_all | solution.py:584
  34.3 10.1 %collective-permute-done.3 = f32[1024,128]{1,0:T(8,128)S(1)} collective-permute-done((f32[1024,128]{1,0:T(8,128)S(1)}, f32[1024,128]{1,0:T(8,128)S(1)}, u32[]{:S(2)}, u32[]{:S(2)}) %collective-permute-start.3) | collective-permute-done | bytes 524320 | tf_op jit(solution)/shard_map/ppermute | solution.py:546
  48.0 17.9 %forward_tiles.1 = (f32[48,40,128]{2,1,0:T(8,128)}, f32[48,40,128]{2,1,0:T(8,128)}, f32[48,40,128]{2,1,0:T(8,128)}, f32[48,40,128]{2,1,0:T(8,128)}, f32[48,40,12...) custom-call(s32[512]{0:T(512)} %pad_add_fusion.2.meta, ...), custom_call_target="tpu_custom_call" | custom-call | tf_op jit(solution)/shard_map/forward_tiles/pallas_call | solution.py:128
  73.7 3.3 collective-permute-start.10
  77.1 11.9 %collective-permute-done.6.rest_1_ = f32[48,40,128]{2,1,0:T(8,128)S(1)} collective-permute-done((f32[48,40,128]{2,1,0:T(8,128)S(1)}, f32[48,40,128]{2,1,0:T(8,128)S(1)}, u32[]{:S(2)}, u32[]{:S(2)}) %collective-permute-start.6) | collective-permute-done | bytes 983072 | tf_op jit(solution)/shard_map/ppermute | solution.py:542
  88.9 3.8 collective-permute-start.11
  93.3 17.8 %collective-permute-done.7.rest_2_ = f32[48,40,128]{2,1,0:T(8,128)S(1)} collective-permute-done((f32[48,40,128]{2,1,0:T(8,128)}, f32[48,40,128]{2,1,0:T(8,128)S(1)}, u32[]{:S(2)}, u32[]{:S(2)}) %collective-permute-start.7) | collective-permute-done | bytes 983072 | tf_op jit(solution)/shard_map/ppermute | solution.py:542
  113.0 3.5 collective-permute-done.10.rest_6_
  117.8 6.1 %combine_blocks.1 = (f32[128,40,128]{2,1,0:T(8,128)}, f32[128,40,128]{2,1,0:T(8,128)}) custom-call(s32[3072]{0:T(1024)} %reshape.141.ids, s32[3]{0:T(128)} %pad_add_fusion.3.place, f32[48,40,128]{2,1,0:T(8,128)} %get-tuple-element.58.rest_0_, f32[48,40,128]{2,1,0:T(8,128)} %copy-done.3, f32[48,40,128]{2,1,0:T(8,128)} %copy-done.4, f32[48,40,128]{2,1,0:T(8,128)} %copy-done.5, ...), custom_call_target="tpu_custom_call" | custom-call | tf_op jit(solution)/shard_map/combine_blocks/pallas_call | solution.py:188
  123.9 6.9 %collective-permute-start.12 = (f32[128,40,128]{2,1,0:T(8,128)}, f32[128,40,128]{2,1,0:T(8,128)S(1)}, u32[]{:S(2)}, u32[]{:S(2)}) collective-permute-start(f32[128,40,128]{2,1,0:T(8,128)} %get-tuple-element.67), channel_id=1, source_target_pairs={{0,1},{1,0},{2,3},{3,2},{4,5},{5,4},{6,7},{7,6},{8,9},{9,8},{10,11... | collective-permute-start | bytes 7864328 | tf_op jit(solution)/shard_map/ppermute | solution.py:542
  130.8 4.7 %collective-permute-done.12.taken = f32[128,40,128]{2,1,0:T(8,128)S(1)} collective-permute-done((f32[128,40,128]{2,1,0:T(8,128)}, f32[128,40,128]{2,1,0:T(8,128)S(1)}, u32[]{:S(2)}, u32[]{:S(2)}) %collective-permute-start.12) | collective-permute-done | bytes 2621472 | tf_op jit(solution)/shard_map/ppermute | solution.py:542
  137.0 4.1 %add_cores.1 = (f32[16,40,128]{2,1,0:T(8,128)}, f32[16,40,128]{2,1,0:T(8,128)}, f32[16,40,128]{2,1,0:T(8,128)}, f32[16,40,128]{2,1,0:T(8,128)}, f32[16,40,128]{2...) custom-call(f32[128,40,128]{2,1,0:T(8,128)} %get-tuple-element.66.keep, ...), custom_call_target="tpu_custom_call" | custom-call | tf_op jit(solution)/shard_map/add_cores/pallas_call | solution.py:218
  144.1 16.6 %collective-permute-start.17 = (f32[16,40,128]{2,1,0:T(8,128)}, f32[16,40,128]{2,1,0:T(8,128)S(1)}, u32[]{:S(2)}, u32[]{:S(2)}) collective-permute-start(f32[16,40,128]{2,1,0:T(8,128)} %get-tuple-element.74), channel_id=1, source_target_pairs={{0,4},{1,5},{2,6},{3,7},{4,0},{5,1},{6,2},{7,3},{8,12},{9,13},{10,... | collective-permute-start | bytes 983048 | tf_op jit(solution)/shard_map/ppermute | solution.py:542
  162.8 4.0 %collective-permute-done.14.rest_2_ = f32[16,40,128]{2,1,0:T(8,128)S(1)} collective-permute-done((f32[16,40,128]{2,1,0:T(8,128)}, f32[16,40,128]{2,1,0:T(8,128)S(1)}, u32[]{:S(2)}, u32[]{:S(2)}) %collective-permute-start.14) | collective-permute-done | bytes 327712 | tf_op jit(solution)/shard_map/ppermute | solution.py:542
  166.9 8.3 %collective-permute-done.17.rest_6_ = f32[16,40,128]{2,1,0:T(8,128)S(1)} collective-permute-done((f32[16,40,128]{2,1,0:T(8,128)}, f32[16,40,128]{2,1,0:T(8,128)S(1)}, u32[]{:S(2)}, u32[]{:S(2)}) %collective-permute-start.17) | collective-permute-done | bytes 327712 | tf_op jit(solution)/shard_map/ppermute | solution.py:542
  175.1 13.2 %reduce-scatter.3.cloned.1.call-done = f32[768,128]{1,0:T(8,128)} async-done(((f32[24576,128]{1,0:T(8,128)}), f32[768,128]{1,0:T(8,128)}) %reduce-scatter.3.cloned.1.call-update) | async-done | bytes 393232 | tf_op jit(solution)/shard_map/reduce_scatter | solution.py:599
  188.4 7.6 %layer.1 = (f32[2048,256]{1,0:T(8,128)}, f32[2048,256]{1,0:T(8,128)}, f32[2048,128]{1,0:T(8,128)}, f32[16,80,128]{2,1,0:T(8,128)}, f32[16,24,128]{2,1,0:T(8,128)}, /*index=5*/f32[16,24,128]{2,1,0:T(8,128)}) custom-call(f32[2048,128]{1,0:T(8,128)} %features.3, f32[2048,256]{1,0:T(8,128)} %cotangent.1, f32[128,256]{1,0:T(8,128)} %w_self.3, ...), custom_call_target="tpu_custom_call" | custom-call | tf_op jit(solution)/shard_map/layer/pallas_call | solution.py:270
  209.4 4.1 %collective-permute-done.24 = f32[16,24,128]{2,1,0:T(8,128)S(1)} collective-permute-done((f32[16,24,128]{2,1,0:T(8,128)}, f32[16,24,128]{2,1,0:T(8,128)S(1)}, u32[]{:S(2)}, u32[]{:S(2)}) %collective-permute-start.24) | collective-permute-done | bytes 196640 | tf_op jit(solution)/shard_map/ppermute | solution.py:542
  213.5 6.6 %collective-permute-start.25 = (f32[128,24,128]{2,1,0:T(8,128)S(1)}, f32[128,24,128]{2,1,0:T(8,128)S(1)}, u32[]{:S(2)}, u32[]{:S(2)}) collective-permute-start(f32[128,24,128]{2,1,0:T(8,128)S(1)} %constant_dynamic-update-slice_fusion.mine), channel_id=1, source_target_pairs={{0,1},{1,0},{2,3},{3,2},{4,5},{5,4},{6,7},{7,6},{8,9},{9,8},{10,11... | collective-permute-start | bytes 4718600 | tf_op jit(solution)/shard_map/ppermute | solution.py:542
  224.3 5.1 %make_replies.1 = (f32[48,24,128]{2,1,0:T(8,128)}, f32[48,24,128]{2,1,0:T(8,128)}, f32[48,24,128]{2,1,0:T(8,128)}, f32[48,24,128]{2,1,0:T(8,128)}, f32[48,24,128...) custom-call(s32[3072]{0:T(1024)} %reshape.141.ids, ...), custom_call_target="tpu_custom_call" | custom-call | tf_op jit(solution)/shard_map/make_replies/pallas_call | solution.py:381
  233.0 26.6 %collective-permute-done.26.rest_1_ = f32[48,24,128]{2,1,0:T(8,128)S(1)} collective-permute-done((f32[48,24,128]{2,1,0:T(8,128)}, f32[48,24,128]{2,1,0:T(8,128)S(1)}, u32[]{:S(2)}, u32[]{:S(2)}) %collective-permute-start.26) | collective-permute-done | bytes 589856 | tf_op jit(solution)/shard_map/ppermute | solution.py:542
  259.6 5.7 %weight_terms.1 = (f32[2048,128]{1,0:T(8,128)}, f32[32,8,384]{2,1,0:T(8,128)}) custom-call(f32[2048,128]{1,0:T(8,128)} %features.3, f32[2048,128]{1,0:T(8,128)} %get-tuple-element.78.aggregated, f32[2048,256]{1,0:T(8,128)} %get-tuple-element.83.grad_pre, f32[128,256]{1,0:T(8,128)} %w_self.3), custom_call_target="tpu_custom_call" | custom-call | tf_op jit(solution)/shard_map/weight_terms/pallas_call | solution.py:322
  265.3 11.6 %all-to-all-start.1 = ((f32[32,8,384]{2,1,0:T(8,128)}), f32[32,8,384]{2,1,0:T(8,128)S(1)}, u32[]{:S(2)}, u32[]{:S(2)}) async-start(f32[32,8,384]{2,1,0:T(8,128)} %get-tuple-element.85), calls=%async_computation.2 | async-start | bytes 786432 | tf_op jit(solution)/shard_map/all_to_all | solution.py:628
  277.2 18.7 %all-to-all-done.1 = f32[32,8,384]{2,1,0:T(8,128)S(1)} async-done(((f32[32,8,384]{2,1,0:T(8,128)}), f32[32,8,384]{2,1,0:T(8,128)S(1)}, u32[]{:S(2)}, u32[]{:S(2)}) %all-to-all-start.1) | async-done | bytes 393248 | tf_op jit(solution)/shard_map/all_to_all | solution.py:628
  297.4 10.1 %replied_tiles.1 = f32[64,48,128]{2,1,0:T(8,128)} custom-call(s32[513]{0:T(1024)} %copy-done.30, f32[128,128,128]{2,1,0:T(8,128)} %tiles.5, f32[48,24,128]{2,1,0:T(8,128)} %get-tuple-element.94.rest_0_, f32[48,24,128]{2,1,0:T(8,128)} %copy-done.12, f32[48,24,128]{2,1,0:T(8,128)} %copy-done.13, f32[48,24,128]{2,1,0:T(8,128)} %copy-done.14, ...), custom_call_target="tpu_custom_call" | custom-call | tf_op jit(solution)/shard_map/replied_tiles/pallas_call | solution.py:500
  307.5 3.6 all-gather.2.cloned.1.call-done.grads
  311.1 9.6 %gathered_tiles.1 = (f32[16,80,128]{2,1,0:T(8,128)}, f32[16,80,128]{2,1,0:T(8,128)}, f32[16,80,128]{2,1,0:T(8,128)}, f32[16,80,128]{2,1,0:T(8,128)}) custom-call(s32[513]{0:T(1024)} %copy-done.30, f32[128,128,128]{2,1,0:T(8,128)} %tiles.5, f32[512,80,128]{2,1,0:T(8,128)} %all-gather.2.cloned.1.call-done.grads), custom_call_target="tpu_custom_call" | custom-call | tf_op jit(solution)/shard_map/gathered_tiles/pallas_call | solution.py:448
  327.4 20.6 %collective-permute-done.28 = f32[8,384]{1,0:T(8,128)S(1)} collective-permute-done((f32[8,384]{1,0:T(8,128)S(1)}, f32[8,384]{1,0:T(8,128)S(1)}, u32[]{:S(2)}, u32[]{:S(2)}) %collective-permute-start.28) | collective-permute-done | bytes 12320 | tf_op jit(solution)/shard_map/ppermute | solution.py:546
  350.5 18.0 %all-to-all-start.2 = ((f32[32,8,384]{2,1,0:T(8,128)}), f32[32,8,384]{2,1,0:T(8,128)S(1)}, u32[]{:S(2)}, u32[]{:S(2)}) async-start(f32[32,8,384]{2,1,0:T(8,128)} %broadcast_in_dim.59), calls=%async_computation.4 | async-start | bytes 786432 | tf_op jit(solution)/shard_map/all_to_all | solution.py:641
  369.7 4.2 %finish_grad_x.1 = f32[2048,128]{1,0:T(8,128)} custom-call(f32[2048,128]{1,0:T(8,128)} %get-tuple-element.84.own, f32[16,80,128]{2,1,0:T(8,128)} %get-tuple-element.88.rest_0_, f32[16,80,128]{2,1,0:T(8,128)} %copy-done.9, f32[16,80,128]{2,1,0:T(8,128)} %copy-done.10, f32[16,80,128]{2,1,0:T(8,128)} %copy-done.11, f32[16,48,128]{2,1,0:T(8,128)} %bitcast.66), custom_call_target="tpu_custom_call" | custom-call | tf_op jit(solution)/shard_map/finish_grad_x/pallas_call | solution.py:520
  373.8 5.0 %all-to-all-done.2 = f32[32,8,384]{2,1,0:T(8,128)S(1)} async-done(((f32[32,8,384]{2,1,0:T(8,128)}), f32[32,8,384]{2,1,0:T(8,128)S(1)}, u32[]{:S(2)}, u32[]{:S(2)}) %all-to-all-start.2) | async-done | bytes 393248 | tf_op jit(solution)/shard_map/all_to_all | solution.py:641
  (188 shorter events, 67.2 us)
Async XLA Ops:
  8.5 24.0 %collective-permute-start.1 = (f32[1024,128]{1,0:T(8,128)S(1)}, f32[1024,128]{1,0:T(8,128)S(1)}, u32[]{:S(2)}, u32[]{:S(2)}) collective-permute-start(f32[1024,128]{1,0:T(8,128)S(1)} %get-tuple-element.112), channel_id=1, source_target_pairs={{0,96},{32,0},{64,32},{96,64},{1,97},{33,1},{65,33},{97,65},{2,98}... | collective-permute-start | bytes 1572872 | tf_op jit(solution)/shard_map/ppermute | solution.py:546
  8.8 25.5 %collective-permute-start.2 = (f32[1024,128]{1,0:T(8,128)S(1)}, f32[1024,128]{1,0:T(8,128)S(1)}, u32[]{:S(2)}, u32[]{:S(2)}) collective-permute-start(f32[1024,128]{1,0:T(8,128)S(1)} %get-tuple-element.112), channel_id=1, source_target_pairs={{0,32},{32,64},{64,96},{96,0},{1,33},{33,65},{65,97},{97,1},{2,34}... | collective-permute-start | bytes 1572872 | tf_op jit(solution)/shard_map/ppermute | solution.py:546
  10.0 22.5 %collective-permute-start = (f32[1024,128]{1,0:T(8,128)S(1)}, f32[1024,128]{1,0:T(8,128)S(1)}, u32[]{:S(2)}, u32[]{:S(2)}) collective-permute-start(f32[1024,128]{1,0:T(8,128)S(1)} %get-tuple-element.113), channel_id=1, source_target_pairs={{0,32},{32,64},{64,96},{96,0},{1,33},{33,65},{65,97},{97,1},{2,34}... | collective-permute-start | bytes 1572872 | tf_op jit(solution)/shard_map/ppermute | solution.py:546
  12.1 22.1 %collective-permute-start.5 = (f32[1024,128]{1,0:T(8,128)S(1)}, f32[1024,128]{1,0:T(8,128)S(1)}, u32[]{:S(2)}, u32[]{:S(2)}) collective-permute-start(f32[1024,128]{1,0:T(8,128)S(1)} %get-tuple-element.113), channel_id=1, source_target_pairs={{0,96},{32,0},{64,32},{96,64},{1,97},{33,1},{65,33},{97,65},{2,98}... | collective-permute-start | bytes 1572872 | tf_op jit(solution)/shard_map/ppermute | solution.py:546
  13.9 16.5 %all-to-all-start = ((s32[32,1,96]{2,1,0:T(1,128)}), s32[32,1,96]{2,1,0:T(1,128)S(1)}, u32[]{:S(2)}, u32[]{:S(2)}) async-start(s32[32,1,96]{2,1,0:T(1,128)} %bitcast.5), calls=%async_computation | async-start | bytes 32768 | tf_op jit(solution)/shard_map/all_to_all | solution.py:584
  23.6 164.8 %reduce-scatter.3.cloned.1.call-start = ((), (), s32[]{:S(2)}) async-start(), calls=%async_computation.5 | async-start | bytes 12976128 | tf_op jit(solution)/shard_map/reduce_scatter | solution.py:599
  66.0 245.1 %all-gather.2.cloned.1.call-start = ((), (), s32[]{:S(2)}) async-start(), calls=%async_computation.6 | async-start | bytes 21626880 | tf_op jit(solution)/shard_map/all_gather | solution.py:615
  67.1 21.8 %collective-permute-start.6 = (f32[48,40,128]{2,1,0:T(8,128)S(1)}, f32[48,40,128]{2,1,0:T(8,128)S(1)}, u32[]{:S(2)}, u32[]{:S(2)}) collective-permute-start(f32[48,40,128]{2,1,0:T(8,128)S(1)} %copy-done.36), channel_id=1, source_target_pairs={{0,2},{1,3},{2,4},{3,5},{4,6},{5,7},{6,0},{7,1},{8,10},{9,11},{10,... | collective-permute-start | bytes 2949128 | tf_op jit(solution)/shard_map/ppermute | solution.py:542
  68.4 42.7 %collective-permute-start.7 = (f32[48,40,128]{2,1,0:T(8,128)}, f32[48,40,128]{2,1,0:T(8,128)S(1)}, u32[]{:S(2)}, u32[]{:S(2)}) collective-permute-start(f32[48,40,128]{2,1,0:T(8,128)} %get-tuple-element.60), channel_id=1, source_target_pairs={{0,4},{1,5},{2,6},{3,7},{4,0},{5,1},{6,2},{7,3},{8,12},{9,13},{10,... | collective-permute-start | bytes 2949128 | tf_op jit(solution)/shard_map/ppermute | solution.py:542
  71.0 42.0 %collective-permute-start.8 = (f32[48,40,128]{2,1,0:T(8,128)}, f32[48,40,128]{2,1,0:T(8,128)S(1)}, u32[]{:S(2)}, u32[]{:S(2)}) collective-permute-start(f32[48,40,128]{2,1,0:T(8,128)} %get-tuple-element.61), channel_id=1, source_target_pairs={{0,6},{1,7},{2,0},{3,1},{4,2},{5,3},{6,4},{7,5},{8,14},{9,15},{10,... | collective-permute-start | bytes 2949128 | tf_op jit(solution)/shard_map/ppermute | solution.py:542
  72.1 40.9 %collective-permute-start.9 = (f32[48,40,128]{2,1,0:T(8,128)}, f32[48,40,128]{2,1,0:T(8,128)S(1)}, u32[]{:S(2)}, u32[]{:S(2)}) collective-permute-start(f32[48,40,128]{2,1,0:T(8,128)} %get-tuple-element.63), channel_id=1, source_target_pairs={{0,8},{1,9},{2,10},{3,11},{4,12},{5,13},{6,14},{7,15},{8,16},{9,17... | collective-permute-start | bytes 2949128 | tf_op jit(solution)/shard_map/ppermute | solution.py:542
  73.7 42.7 %collective-permute-start.10 = (f32[48,40,128]{2,1,0:T(8,128)S(1)}, f32[48,40,128]{2,1,0:T(8,128)S(1)}, u32[]{:S(2)}, u32[]{:S(2)}) collective-permute-start(f32[48,40,128]{2,1,0:T(8,128)S(1)} %copy-done.35), channel_id=1, source_target_pairs={{0,16},{1,17},{2,18},{3,19},{4,20},{5,21},{6,22},{7,23},{8,24},{9,... | collective-permute-start | bytes 2949128 | tf_op jit(solution)/shard_map/ppermute | solution.py:542
  88.9 27.6 %collective-permute-start.11 = (f32[48,40,128]{2,1,0:T(8,128)S(1)}, f32[48,40,128]{2,1,0:T(8,128)S(1)}, u32[]{:S(2)}, u32[]{:S(2)}) collective-permute-start(f32[48,40,128]{2,1,0:T(8,128)S(1)} %copy-done.34), channel_id=1, source_target_pairs={{0,24},{1,25},{2,26},{3,27},{4,28},{5,29},{6,30},{7,31},{8,0},{9,1... | collective-permute-start | bytes 2949128 | tf_op jit(solution)/shard_map/ppermute | solution.py:542
  141.2 19.6 %collective-permute-start.13 = (f32[16,40,128]{2,1,0:T(8,128)}, f32[16,40,128]{2,1,0:T(8,128)S(1)}, u32[]{:S(2)}, u32[]{:S(2)}) collective-permute-start(f32[16,40,128]{2,1,0:T(8,128)} %get-tuple-element.69), channel_id=1, source_target_pairs={{0,8},{1,9},{2,10},{3,11},{4,12},{5,13},{6,14},{7,15},{8,16},{9,17... | collective-permute-start | bytes 983048 | tf_op jit(solution)/shard_map/ppermute | solution.py:542
  141.6 25.2 %collective-permute-start.14 = (f32[16,40,128]{2,1,0:T(8,128)}, f32[16,40,128]{2,1,0:T(8,128)S(1)}, u32[]{:S(2)}, u32[]{:S(2)}) collective-permute-start(f32[16,40,128]{2,1,0:T(8,128)} %get-tuple-element.70), channel_id=1, source_target_pairs={{0,16},{1,17},{2,18},{3,19},{4,20},{5,21},{6,22},{7,23},{8,24},{9,... | collective-permute-start | bytes 983048 | tf_op jit(solution)/shard_map/ppermute | solution.py:542
  142.1 24.7 %collective-permute-start.15 = (f32[16,40,128]{2,1,0:T(8,128)}, f32[16,40,128]{2,1,0:T(8,128)S(1)}, u32[]{:S(2)}, u32[]{:S(2)}) collective-permute-start(f32[16,40,128]{2,1,0:T(8,128)} %get-tuple-element.71), channel_id=1, source_target_pairs={{0,24},{1,25},{2,26},{3,27},{4,28},{5,29},{6,30},{7,31},{8,0},{9,1... | collective-permute-start | bytes 983048 | tf_op jit(solution)/shard_map/ppermute | solution.py:542
  144.1 22.7 %collective-permute-start.16 = (f32[16,40,128]{2,1,0:T(8,128)}, f32[16,40,128]{2,1,0:T(8,128)S(1)}, u32[]{:S(2)}, u32[]{:S(2)}) collective-permute-start(f32[16,40,128]{2,1,0:T(8,128)} %get-tuple-element.73), channel_id=1, source_target_pairs={{0,2},{1,3},{2,4},{3,5},{4,6},{5,7},{6,0},{7,1},{8,10},{9,11},{10,... | collective-permute-start | bytes 983048 | tf_op jit(solution)/shard_map/ppermute | solution.py:542
  144.1 31.0 %collective-permute-start.17 = (f32[16,40,128]{2,1,0:T(8,128)}, f32[16,40,128]{2,1,0:T(8,128)S(1)}, u32[]{:S(2)}, u32[]{:S(2)}) collective-permute-start(f32[16,40,128]{2,1,0:T(8,128)} %get-tuple-element.74), channel_id=1, source_target_pairs={{0,4},{1,5},{2,6},{3,7},{4,0},{5,1},{6,2},{7,3},{8,12},{9,13},{10,... | collective-permute-start | bytes 983048 | tf_op jit(solution)/shard_map/ppermute | solution.py:542
  229.4 30.2 %collective-permute-start.26 = (f32[48,24,128]{2,1,0:T(8,128)}, f32[48,24,128]{2,1,0:T(8,128)S(1)}, u32[]{:S(2)}, u32[]{:S(2)}) collective-permute-start(f32[48,24,128]{2,1,0:T(8,128)} %get-tuple-element.82), channel_id=1, source_target_pairs={{0,6},{1,7},{2,0},{3,1},{4,2},{5,3},{6,4},{7,5},{8,14},{9,15},{10,... | collective-permute-start | bytes 1769480 | tf_op jit(solution)/shard_map/ppermute | solution.py:542
  232.3 63.6 %collective-permute-start.33 = (f32[48,24,128]{2,1,0:T(8,128)}, f32[48,24,128]{2,1,0:T(8,128)S(1)}, u32[]{:S(2)}, u32[]{:S(2)}) collective-permute-start(f32[48,24,128]{2,1,0:T(8,128)} %get-tuple-element.96), channel_id=1, source_target_pairs={{0,4},{1,5},{2,6},{3,7},{4,0},{5,1},{6,2},{7,3},{8,12},{9,13},{10,... | collective-permute-start | bytes 1769480 | tf_op jit(solution)/shard_map/ppermute | solution.py:542
  232.4 63.6 %collective-permute-start.34 = (f32[48,24,128]{2,1,0:T(8,128)}, f32[48,24,128]{2,1,0:T(8,128)S(1)}, u32[]{:S(2)}, u32[]{:S(2)}) collective-permute-start(f32[48,24,128]{2,1,0:T(8,128)} %get-tuple-element.97), channel_id=1, source_target_pairs={{0,2},{1,3},{2,4},{3,5},{4,6},{5,7},{6,0},{7,1},{8,10},{9,11},{10,... | collective-permute-start | bytes 1769480 | tf_op jit(solution)/shard_map/ppermute | solution.py:542
  233.0 62.9 %collective-permute-start.35 = (f32[48,24,128]{2,1,0:T(8,128)}, f32[48,24,128]{2,1,0:T(8,128)S(1)}, u32[]{:S(2)}, u32[]{:S(2)}) collective-permute-start(f32[48,24,128]{2,1,0:T(8,128)} %get-tuple-element.99), channel_id=1, source_target_pairs={{0,24},{1,25},{2,26},{3,27},{4,28},{5,29},{6,30},{7,31},{8,0},{9,1... | collective-permute-start | bytes 1769480 | tf_op jit(solution)/shard_map/ppermute | solution.py:542
  233.0 62.9 %collective-permute-start.36 = (f32[48,24,128]{2,1,0:T(8,128)}, f32[48,24,128]{2,1,0:T(8,128)S(1)}, u32[]{:S(2)}, u32[]{:S(2)}) collective-permute-start(f32[48,24,128]{2,1,0:T(8,128)} %get-tuple-element.100), channel_id=1, source_target_pairs={{0,16},{1,17},{2,18},{3,19},{4,20},{5,21},{6,22},{7,23},{8,24},{9,... | collective-permute-start | bytes 1769480 | tf_op jit(solution)/shard_map/ppermute | solution.py:542
  259.6 36.4 %collective-permute-start.37 = (f32[48,24,128]{2,1,0:T(8,128)}, f32[48,24,128]{2,1,0:T(8,128)}, u32[]{:S(2)}, u32[]{:S(2)}) collective-permute-start(f32[48,24,128]{2,1,0:T(8,128)} %get-tuple-element.101), channel_id=1, source_target_pairs={{0,8},{1,9},{2,10},{3,11},{4,12},{5,13},{6,14},{7,15},{8,16},{9,17... | collective-permute-start | bytes 1769480 | tf_op jit(solution)/shard_map/ppermute | solution.py:542
  265.3 30.6 %all-to-all-start.1 = ((f32[32,8,384]{2,1,0:T(8,128)}), f32[32,8,384]{2,1,0:T(8,128)S(1)}, u32[]{:S(2)}, u32[]{:S(2)}) async-start(f32[32,8,384]{2,1,0:T(8,128)} %get-tuple-element.85), calls=%async_computation.2 | async-start | bytes 786432 | tf_op jit(solution)/shard_map/all_to_all | solution.py:628
  276.9 91.7 %reduce-scatter.5.cloned.1.call-start = ((), (), s32[]{:S(2)}) async-start(), calls=%async_computation.7 | async-start | bytes 1966080 | tf_op jit(solution)/shard_map/reduce_scatter | solution.py:631
  320.7 29.0 %collective-permute-start.30 = (f32[16,80,128]{2,1,0:T(8,128)}, f32[16,80,128]{2,1,0:T(8,128)S(1)}, u32[]{:S(2)}, u32[]{:S(2)}) collective-permute-start(f32[16,80,128]{2,1,0:T(8,128)} %get-tuple-element.90), channel_id=1, source_target_pairs={{0,32},{32,64},{64,96},{96,0},{1,33},{33,65},{65,97},{97,1},{2,34}... | collective-permute-start | bytes 1966088 | tf_op jit(solution)/shard_map/ppermute | solution.py:546
  322.3 25.7 %collective-permute-start.28 = (f32[8,384]{1,0:T(8,128)S(1)}, f32[8,384]{1,0:T(8,128)S(1)}, u32[]{:S(2)}, u32[]{:S(2)}) collective-permute-start(f32[8,384]{1,0:T(8,128)S(1)} %reduce_sum.41), channel_id=1, source_target_pairs={{0,64},{32,96},{64,0},{96,32},{1,65},{33,97},{65,1},{97,33},{2,66}... | collective-permute-start | bytes 36872 | tf_op jit(solution)/shard_map/ppermute | solution.py:546
  323.8 25.2 %collective-permute-start.27 = (f32[8,384]{1,0:T(8,128)S(1)}, f32[8,384]{1,0:T(8,128)S(1)}, u32[]{:S(2)}, u32[]{:S(2)}) collective-permute-start(f32[8,384]{1,0:T(8,128)S(1)} %reduce_sum.41), channel_id=1, source_target_pairs={{0,32},{32,64},{64,96},{96,0},{1,33},{33,65},{65,97},{97,1},{2,34}... | collective-permute-start | bytes 36872 | tf_op jit(solution)/shard_map/ppermute | solution.py:546
  324.4 44.2 %collective-permute-start.31 = (f32[16,80,128]{2,1,0:T(8,128)}, f32[16,80,128]{2,1,0:T(8,128)S(1)}, u32[]{:S(2)}, u32[]{:S(2)}) collective-permute-start(f32[16,80,128]{2,1,0:T(8,128)} %get-tuple-element.92), channel_id=1, source_target_pairs={{0,64},{32,96},{64,0},{96,32},{1,65},{33,97},{65,1},{97,33},{2,66}... | collective-permute-start | bytes 1966088 | tf_op jit(solution)/shard_map/ppermute | solution.py:546
  325.6 43.0 %collective-permute-start.32 = (f32[16,80,128]{2,1,0:T(8,128)}, f32[16,80,128]{2,1,0:T(8,128)S(1)}, u32[]{:S(2)}, u32[]{:S(2)}) collective-permute-start(f32[16,80,128]{2,1,0:T(8,128)} %get-tuple-element.93), channel_id=1, source_target_pairs={{0,96},{32,0},{64,32},{96,64},{1,97},{33,1},{65,33},{97,65},{2,98}... | collective-permute-start | bytes 1966088 | tf_op jit(solution)/shard_map/ppermute | solution.py:546
  350.5 28.3 %all-to-all-start.2 = ((f32[32,8,384]{2,1,0:T(8,128)}), f32[32,8,384]{2,1,0:T(8,128)S(1)}, u32[]{:S(2)}, u32[]{:S(2)}) async-start(f32[32,8,384]{2,1,0:T(8,128)} %broadcast_in_dim.59), calls=%async_computation.4 | async-start | bytes 786432 | tf_op jit(solution)/shard_map/all_to_all | solution.py:641
  (49 other events, 455.9 us)
Sparse Core Ops, SparseCore 0:
  66.1 122.1 reduce-scatter.2
  196.2 114.8 all-gather.1
  313.6 40.4 reduce-scatter.4

commit v3 on v2

--- a/solution.py
+++ b/solution.py
@@ -635,7 +635,8 @@
     by_rep = jnp.stack([shift_rep(row_sum, d) for d in range(N_REP)])
     by_rep = jnp.take(by_rep, (rep - jnp.arange(N_REP)) % N_REP, axis=0)
     total = jnp.sum(by_rep, axis=0)
-    slab = list(gathered_tiles(backward_meta, tile_values, gathered))
+    gathered_meta, total = lax.optimization_barrier((backward_meta, total))
+    slab = list(gathered_tiles(gathered_meta, tile_values, gathered))
     back = [slab[0]] + [shift_rep(slab[d], d) for d in (1, 2, 3)] + [replied]
     total, back[1] = lax.optimization_barrier((total, back[1]))
     full = lax.all_to_all(

time: 388 us -> 380 us (0.979)
  starting transfers between devices: 113 us -> 107 us
  waiting for transfers between devices: 170 us -> 166 us
    all_to_all x1, starting transfers between devices: 18 us -> 9.58 us  [local(): lax.all_to_all(jnp.broadcast_to(total[None], (N_ROW,) + total.shape), 'ro...]
    all_to_all x1, waiting for transfers between devices: 5.01 us -> 0.65 us  [local(): lax.all_to_all(jnp.broadcast_to(total[None], (N_ROW,) + total.shape), 'ro...]
  transfers between devices with their start and end apart: 44 -> 44, of which waited for: 24 -> 25; matrix products, arithmetic and copies ran while one was open for 2% -> 2% of each run, Pallas kernels for 12% -> 12%
where the time goes in v3:
time: 380 us; the launch traced here: 376 us
  waiting for transfers between devices  166 us (44%)
  starting transfers between devices  107 us (28%)
  Pallas kernels  70.4 us (19%)
  between operations  14.4 us (4%)
  local copies, waits for them, and re-layouts  13.7 us (4%)
  other arithmetic  4.4 us (1%)
    ppermute x26, waiting for transfers between devices, shift(): return lax.ppermute(x, 'row', pairs)  88.7 us
    ppermute x26, starting transfers between devices, shift(): return lax.ppermute(x, 'row', pairs)  61.9 us
    ppermute x12, waiting for transfers between devices, shift_rep(): lax.ppermute(x, 'rep', [(i, (i + d) % N_REP) for i in range(N_REP)])  38.6 us
    all_to_all x1, waiting for transfers between devices, local(): lax.all_to_all(terms, 'row', split_axis=0, concat_axis=0, tiled=True)  19 us
    pallas_call x1, Pallas kernels, forward_tiles(): pl.pallas_call(forward_kernel, grid_spec=spec, out_shape=[jax.ShapeDtypeS...  17.9 us
    ppermute x12, starting transfers between devices, shift_rep(): lax.ppermute(x, 'rep', [(i, (i + d) % N_REP) for i in range(N_REP)])  14 us
    reduce_scatter x1, waiting for transfers between devices, local(): lax.psum_scatter(all_sums.reshape(-1, FEAT), 'row', scatter_dimension=0,...  13.1 us
    all_to_all x1, starting transfers between devices, local(): lax.all_to_all(terms, 'row', split_axis=0, concat_axis=0, tiled=True)  11.6 us
  transfers between devices with their start and end apart: 44, of which 25 were waited for; matrix products, arithmetic and copies ran while one was open for 2% of the time, Pallas kernels for 12%

profile of v3, /device:TPU:5, one launch (start us, length us, event | category | flops | bytes accessed | tf_op | source)
XLA Modules:
  0.0 375.8 jit_solution(6497884607925533773)
XLA Ops:
  13.9 9.6 %all-to-all-start = ((s32[32,1,96]{2,1,0:T(1,128)}), s32[32,1,96]{2,1,0:T(1,128)S(1)}, u32[]{:S(2)}, u32[]{:S(2)}) async-start(s32[32,1,96]{2,1,0:T(1,128)} %bitcast.5), calls=%async_computation | async-start | bytes 32768 | tf_op jit(solution)/shard_map/all_to_all | solution.py:584
  24.2 6.2 %all-to-all-done = s32[32,1,96]{2,1,0:T(1,128)S(1)} async-done(((s32[32,1,96]{2,1,0:T(1,128)}), s32[32,1,96]{2,1,0:T(1,128)S(1)}, u32[]{:S(2)}, u32[]{:S(2)}) %all-to-all-start) | async-done | bytes 12320 | tf_op jit(solution)/shard_map/all_to_all | solution.py:584
  34.3 10.1 %collective-permute-done.3 = f32[1024,128]{1,0:T(8,128)S(1)} collective-permute-done((f32[1024,128]{1,0:T(8,128)S(1)}, f32[1024,128]{1,0:T(8,128)S(1)}, u32[]{:S(2)}, u32[]{:S(2)}) %collective-permute-start.3) | collective-permute-done | bytes 524320 | tf_op jit(solution)/shard_map/ppermute | solution.py:546
  48.0 17.9 %forward_tiles.1 = (f32[48,40,128]{2,1,0:T(8,128)}, f32[48,40,128]{2,1,0:T(8,128)}, f32[48,40,128]{2,1,0:T(8,128)}, f32[48,40,128]{2,1,0:T(8,128)}, f32[48,40,12...) custom-call(s32[512]{0:T(512)} %pad_add_fusion.2.meta, ...), custom_call_target="tpu_custom_call" | custom-call | tf_op jit(solution)/shard_map/forward_tiles/pallas_call | solution.py:128
  73.8 3.3 collective-permute-start.10
  77.1 11.9 %collective-permute-done.6.rest_1_ = f32[48,40,128]{2,1,0:T(8,128)S(1)} collective-permute-done((f32[48,40,128]{2,1,0:T(8,128)S(1)}, f32[48,40,128]{2,1,0:T(8,128)S(1)}, u32[]{:S(2)}, u32[]{:S(2)}) %collective-permute-start.6) | collective-permute-done | bytes 983072 | tf_op jit(solution)/shard_map/ppermute | solution.py:542
  88.9 3.8 collective-permute-start.11
  93.3 17.8 %collective-permute-done.7.rest_2_ = f32[48,40,128]{2,1,0:T(8,128)S(1)} collective-permute-done((f32[48,40,128]{2,1,0:T(8,128)}, f32[48,40,128]{2,1,0:T(8,128)S(1)}, u32[]{:S(2)}, u32[]{:S(2)}) %collective-permute-start.7) | collective-permute-done | bytes 983072 | tf_op jit(solution)/shard_map/ppermute | solution.py:542
  113.0 3.5 collective-permute-done.10.rest_6_
  117.8 6.1 %combine_blocks.1 = (f32[128,40,128]{2,1,0:T(8,128)}, f32[128,40,128]{2,1,0:T(8,128)}) custom-call(s32[3072]{0:T(1024)} %reshape.141.ids, s32[3]{0:T(128)} %pad_add_fusion.3.place, f32[48,40,128]{2,1,0:T(8,128)} %get-tuple-element.60.rest_0_, f32[48,40,128]{2,1,0:T(8,128)} %copy-done.3, f32[48,40,128]{2,1,0:T(8,128)} %copy-done.4, f32[48,40,128]{2,1,0:T(8,128)} %copy-done.5, ...), custom_call_target="tpu_custom_call" | custom-call | tf_op jit(solution)/shard_map/combine_blocks/pallas_call | solution.py:188
  123.9 6.9 %collective-permute-start.12 = (f32[128,40,128]{2,1,0:T(8,128)}, f32[128,40,128]{2,1,0:T(8,128)S(1)}, u32[]{:S(2)}, u32[]{:S(2)}) collective-permute-start(f32[128,40,128]{2,1,0:T(8,128)} %get-tuple-element.69), channel_id=1, source_target_pairs={{0,1},{1,0},{2,3},{3,2},{4,5},{5,4},{6,7},{7,6},{8,9},{9,8},{10,11... | collective-permute-start | bytes 7864328 | tf_op jit(solution)/shard_map/ppermute | solution.py:542
  130.8 4.7 %collective-permute-done.12.taken = f32[128,40,128]{2,1,0:T(8,128)S(1)} collective-permute-done((f32[128,40,128]{2,1,0:T(8,128)}, f32[128,40,128]{2,1,0:T(8,128)S(1)}, u32[]{:S(2)}, u32[]{:S(2)}) %collective-permute-start.12) | collective-permute-done | bytes 2621472 | tf_op jit(solution)/shard_map/ppermute | solution.py:542
  137.1 4.1 %add_cores.1 = (f32[16,40,128]{2,1,0:T(8,128)}, f32[16,40,128]{2,1,0:T(8,128)}, f32[16,40,128]{2,1,0:T(8,128)}, f32[16,40,128]{2,1,0:T(8,128)}, f32[16,40,128]{2...) custom-call(f32[128,40,128]{2,1,0:T(8,128)} %get-tuple-element.68.keep, ...), custom_call_target="tpu_custom_call" | custom-call | tf_op jit(solution)/shard_map/add_cores/pallas_call | solution.py:218
  144.1 16.7 %collective-permute-start.17 = (f32[16,40,128]{2,1,0:T(8,128)}, f32[16,40,128]{2,1,0:T(8,128)S(1)}, u32[]{:S(2)}, u32[]{:S(2)}) collective-permute-start(f32[16,40,128]{2,1,0:T(8,128)} %get-tuple-element.76), channel_id=1, source_target_pairs={{0,4},{1,5},{2,6},{3,7},{4,0},{5,1},{6,2},{7,3},{8,12},{9,13},{10,... | collective-permute-start | bytes 983048 | tf_op jit(solution)/shard_map/ppermute | solution.py:542
  162.9 3.9 %collective-permute-done.14.rest_2_ = f32[16,40,128]{2,1,0:T(8,128)S(1)} collective-permute-done((f32[16,40,128]{2,1,0:T(8,128)}, f32[16,40,128]{2,1,0:T(8,128)S(1)}, u32[]{:S(2)}, u32[]{:S(2)}) %collective-permute-start.14) | collective-permute-done | bytes 327712 | tf_op jit(solution)/shard_map/ppermute | solution.py:542
  166.8 8.4 %collective-permute-done.17.rest_6_ = f32[16,40,128]{2,1,0:T(8,128)S(1)} collective-permute-done((f32[16,40,128]{2,1,0:T(8,128)}, f32[16,40,128]{2,1,0:T(8,128)S(1)}, u32[]{:S(2)}, u32[]{:S(2)}) %collective-permute-start.17) | collective-permute-done | bytes 327712 | tf_op jit(solution)/shard_map/ppermute | solution.py:542
  175.2 13.1 %reduce-scatter.3.cloned.1.call-done = f32[768,128]{1,0:T(8,128)} async-done(((f32[24576,128]{1,0:T(8,128)}), f32[768,128]{1,0:T(8,128)}) %reduce-scatter.3.cloned.1.call-update) | async-done | bytes 393232 | tf_op jit(solution)/shard_map/reduce_scatter | solution.py:599
  188.4 7.6 %layer.1 = (f32[2048,256]{1,0:T(8,128)}, f32[2048,256]{1,0:T(8,128)}, f32[2048,128]{1,0:T(8,128)}, f32[16,80,128]{2,1,0:T(8,128)}, f32[16,24,128]{2,1,0:T(8,128)}, /*index=5*/f32[16,24,128]{2,1,0:T(8,128)}) custom-call(f32[2048,128]{1,0:T(8,128)} %features.3, f32[2048,256]{1,0:T(8,128)} %cotangent.1, f32[128,256]{1,0:T(8,128)} %w_self.3, ...), custom_call_target="tpu_custom_call" | custom-call | tf_op jit(solution)/shard_map/layer/pallas_call | solution.py:270
  209.4 4.2 %collective-permute-done.24 = f32[16,24,128]{2,1,0:T(8,128)S(1)} collective-permute-done((f32[16,24,128]{2,1,0:T(8,128)}, f32[16,24,128]{2,1,0:T(8,128)S(1)}, u32[]{:S(2)}, u32[]{:S(2)}) %collective-permute-start.24) | collective-permute-done | bytes 196640 | tf_op jit(solution)/shard_map/ppermute | solution.py:542
  213.6 6.6 %collective-permute-start.25 = (f32[128,24,128]{2,1,0:T(8,128)S(1)}, f32[128,24,128]{2,1,0:T(8,128)S(1)}, u32[]{:S(2)}, u32[]{:S(2)}) collective-permute-start(f32[128,24,128]{2,1,0:T(8,128)S(1)} %constant_dynamic-update-slice_fusion.mine), channel_id=1, source_target_pairs={{0,1},{1,0},{2,3},{3,2},{4,5},{5,4},{6,7},{7,6},{8,9},{9,8},{10,11... | collective-permute-start | bytes 4718600 | tf_op jit(solution)/shard_map/ppermute | solution.py:542
  220.2 3.0 collective-permute-done.25.taken
  224.4 5.1 %make_replies.1 = (f32[48,24,128]{2,1,0:T(8,128)}, f32[48,24,128]{2,1,0:T(8,128)}, f32[48,24,128]{2,1,0:T(8,128)}, f32[48,24,128]{2,1,0:T(8,128)}, f32[48,24,128...) custom-call(s32[3072]{0:T(1024)} %reshape.141.ids, ...), custom_call_target="tpu_custom_call" | custom-call | tf_op jit(solution)/shard_map/make_replies/pallas_call | solution.py:381
  233.0 26.5 %collective-permute-done.26.rest_1_ = f32[48,24,128]{2,1,0:T(8,128)S(1)} collective-permute-done((f32[48,24,128]{2,1,0:T(8,128)}, f32[48,24,128]{2,1,0:T(8,128)S(1)}, u32[]{:S(2)}, u32[]{:S(2)}) %collective-permute-start.26) | collective-permute-done | bytes 589856 | tf_op jit(solution)/shard_map/ppermute | solution.py:542
  259.6 5.7 %weight_terms.1 = (f32[2048,128]{1,0:T(8,128)}, f32[32,8,384]{2,1,0:T(8,128)}) custom-call(f32[2048,128]{1,0:T(8,128)} %features.3, f32[2048,128]{1,0:T(8,128)} %get-tuple-element.80.aggregated, f32[2048,256]{1,0:T(8,128)} %get-tuple-element.85.grad_pre, f32[128,256]{1,0:T(8,128)} %w_self.3), custom_call_target="tpu_custom_call" | custom-call | tf_op jit(solution)/shard_map/weight_terms/pallas_call | solution.py:322
  265.2 11.6 %all-to-all-start.1 = ((f32[32,8,384]{2,1,0:T(8,128)}), f32[32,8,384]{2,1,0:T(8,128)S(1)}, u32[]{:S(2)}, u32[]{:S(2)}) async-start(f32[32,8,384]{2,1,0:T(8,128)} %get-tuple-element.87), calls=%async_computation.2 | async-start | bytes 786432 | tf_op jit(solution)/shard_map/all_to_all | solution.py:628
  276.9 19.0 %all-to-all-done.1 = f32[32,8,384]{2,1,0:T(8,128)S(1)} async-done(((f32[32,8,384]{2,1,0:T(8,128)}), f32[32,8,384]{2,1,0:T(8,128)S(1)}, u32[]{:S(2)}, u32[]{:S(2)}) %all-to-all-start.1) | async-done | bytes 393248 | tf_op jit(solution)/shard_map/all_to_all | solution.py:628
  297.3 10.1 %replied_tiles.1 = f32[64,48,128]{2,1,0:T(8,128)} custom-call(s32[513]{0:T(1024)} %copy-done.30, f32[128,128,128]{2,1,0:T(8,128)} %tiles.5, f32[48,24,128]{2,1,0:T(8,128)} %get-tuple-element.98.rest_0_, f32[48,24,128]{2,1,0:T(8,128)} %copy-done.12, f32[48,24,128]{2,1,0:T(8,128)} %copy-done.13, f32[48,24,128]{2,1,0:T(8,128)} %copy-done.14, ...), custom_call_target="tpu_custom_call" | custom-call | tf_op jit(solution)/shard_map/replied_tiles/pallas_call | solution.py:500
  312.4 9.6 %gathered_tiles.1 = (f32[16,80,128]{2,1,0:T(8,128)}, f32[16,80,128]{2,1,0:T(8,128)}, f32[16,80,128]{2,1,0:T(8,128)}, f32[16,80,128]{2,1,0:T(8,128)}) custom-call(s32[513]{0:T(1024)} %copy-done.30, f32[128,128,128]{2,1,0:T(8,128)} %tiles.5, f32[512,80,128]{2,1,0:T(8,128)} %all-gather.2.cloned.1.call-done.grads), custom_call_target="tpu_custom_call" | custom-call | tf_op jit(solution)/shard_map/gathered_tiles/pallas_call | solution.py:448
  327.2 20.2 %collective-permute-done.30.rest_1_ = f32[16,80,128]{2,1,0:T(8,128)S(1)} collective-permute-done((f32[16,80,128]{2,1,0:T(8,128)}, f32[16,80,128]{2,1,0:T(8,128)S(1)}, u32[]{:S(2)}, u32[]{:S(2)}) %collective-permute-start.30) | collective-permute-done | bytes 655392 | tf_op jit(solution)/shard_map/ppermute | solution.py:546
  348.3 9.6 %all-to-all-start.2 = ((f32[32,8,384]{2,1,0:T(8,128)}), f32[32,8,384]{2,1,0:T(8,128)S(1)}, u32[]{:S(2)}, u32[]{:S(2)}) async-start(f32[32,8,384]{2,1,0:T(8,128)} %broadcast_in_dim.59), calls=%async_computation.4 | async-start | bytes 786432 | tf_op jit(solution)/shard_map/all_to_all | solution.py:642
  357.9 4.3 %collective-permute-done.31.rest_2_ = f32[16,80,128]{2,1,0:T(8,128)S(1)} collective-permute-done((f32[16,80,128]{2,1,0:T(8,128)}, f32[16,80,128]{2,1,0:T(8,128)S(1)}, u32[]{:S(2)}, u32[]{:S(2)}) %collective-permute-start.31) | collective-permute-done | bytes 655392 | tf_op jit(solution)/shard_map/ppermute | solution.py:546
  363.2 4.2 %finish_grad_x.1 = f32[2048,128]{1,0:T(8,128)} custom-call(f32[2048,128]{1,0:T(8,128)} %get-tuple-element.86.own, f32[16,80,128]{2,1,0:T(8,128)} %get-tuple-element.92.rest_0_, f32[16,80,128]{2,1,0:T(8,128)} %copy-done.9, f32[16,80,128]{2,1,0:T(8,128)} %copy-done.10, f32[16,80,128]{2,1,0:T(8,128)} %copy-done.11, f32[16,48,128]{2,1,0:T(8,128)} %bitcast.66), custom_call_target="tpu_custom_call" | custom-call | tf_op jit(solution)/shard_map/finish_grad_x/pallas_call | solution.py:520
  (188 shorter events, 66.3 us)
Async XLA Ops:
  8.5 24.0 %collective-permute-start.1 = (f32[1024,128]{1,0:T(8,128)S(1)}, f32[1024,128]{1,0:T(8,128)S(1)}, u32[]{:S(2)}, u32[]{:S(2)}) collective-permute-start(f32[1024,128]{1,0:T(8,128)S(1)} %get-tuple-element.116), channel_id=1, source_target_pairs={{0,96},{32,0},{64,32},{96,64},{1,97},{33,1},{65,33},{97,65},{2,98}... | collective-permute-start | bytes 1572872 | tf_op jit(solution)/shard_map/ppermute | solution.py:546
  8.8 25.5 %collective-permute-start.2 = (f32[1024,128]{1,0:T(8,128)S(1)}, f32[1024,128]{1,0:T(8,128)S(1)}, u32[]{:S(2)}, u32[]{:S(2)}) collective-permute-start(f32[1024,128]{1,0:T(8,128)S(1)} %get-tuple-element.116), channel_id=1, source_target_pairs={{0,32},{32,64},{64,96},{96,0},{1,33},{33,65},{65,97},{97,1},{2,34}... | collective-permute-start | bytes 1572872 | tf_op jit(solution)/shard_map/ppermute | solution.py:546
  10.0 22.5 %collective-permute-start = (f32[1024,128]{1,0:T(8,128)S(1)}, f32[1024,128]{1,0:T(8,128)S(1)}, u32[]{:S(2)}, u32[]{:S(2)}) collective-permute-start(f32[1024,128]{1,0:T(8,128)S(1)} %get-tuple-element.117), channel_id=1, source_target_pairs={{0,32},{32,64},{64,96},{96,0},{1,33},{33,65},{65,97},{97,1},{2,34}... | collective-permute-start | bytes 1572872 | tf_op jit(solution)/shard_map/ppermute | solution.py:546
  12.1 22.1 %collective-permute-start.5 = (f32[1024,128]{1,0:T(8,128)S(1)}, f32[1024,128]{1,0:T(8,128)S(1)}, u32[]{:S(2)}, u32[]{:S(2)}) collective-permute-start(f32[1024,128]{1,0:T(8,128)S(1)} %get-tuple-element.117), channel_id=1, source_target_pairs={{0,96},{32,0},{64,32},{96,64},{1,97},{33,1},{65,33},{97,65},{2,98}... | collective-permute-start | bytes 1572872 | tf_op jit(solution)/shard_map/ppermute | solution.py:546
  13.9 16.5 %all-to-all-start = ((s32[32,1,96]{2,1,0:T(1,128)}), s32[32,1,96]{2,1,0:T(1,128)S(1)}, u32[]{:S(2)}, u32[]{:S(2)}) async-start(s32[32,1,96]{2,1,0:T(1,128)} %bitcast.5), calls=%async_computation | async-start | bytes 32768 | tf_op jit(solution)/shard_map/all_to_all | solution.py:584
  23.6 164.8 %reduce-scatter.3.cloned.1.call-start = ((), (), s32[]{:S(2)}) async-start(), calls=%async_computation.5 | async-start | bytes 12976128 | tf_op jit(solution)/shard_map/reduce_scatter | solution.py:599
  34.1 13.1 %collective-permute-start.4 = (f32[1024,128]{1,0:T(8,128)S(1)}, f32[1024,128]{1,0:T(8,128)S(1)}, u32[]{:S(2)}, u32[]{:S(2)}) collective-permute-start(f32[1024,128]{1,0:T(8,128)S(1)} %collective-permute-done.1), channel_id=1, source_target_pairs={{0,96},{32,0},{64,32},{96,64},{1,97},{33,1},{65,33},{97,65},{2,98}... | collective-permute-start | bytes 1572872 | tf_op jit(solution)/shard_map/ppermute | solution.py:546
  66.0 246.4 %all-gather.2.cloned.1.call-start = ((), (), s32[]{:S(2)}) async-start(), calls=%async_computation.6 | async-start | bytes 21626880 | tf_op jit(solution)/shard_map/all_gather | solution.py:615
  67.1 21.8 %collective-permute-start.6 = (f32[48,40,128]{2,1,0:T(8,128)S(1)}, f32[48,40,128]{2,1,0:T(8,128)S(1)}, u32[]{:S(2)}, u32[]{:S(2)}) collective-permute-start(f32[48,40,128]{2,1,0:T(8,128)S(1)} %copy-done.36), channel_id=1, source_target_pairs={{0,2},{1,3},{2,4},{3,5},{4,6},{5,7},{6,0},{7,1},{8,10},{9,11},{10,... | collective-permute-start | bytes 2949128 | tf_op jit(solution)/shard_map/ppermute | solution.py:542
  68.4 42.7 %collective-permute-start.7 = (f32[48,40,128]{2,1,0:T(8,128)}, f32[48,40,128]{2,1,0:T(8,128)S(1)}, u32[]{:S(2)}, u32[]{:S(2)}) collective-permute-start(f32[48,40,128]{2,1,0:T(8,128)} %get-tuple-element.62), channel_id=1, source_target_pairs={{0,4},{1,5},{2,6},{3,7},{4,0},{5,1},{6,2},{7,3},{8,12},{9,13},{10,... | collective-permute-start | bytes 2949128 | tf_op jit(solution)/shard_map/ppermute | solution.py:542
  71.0 42.0 %collective-permute-start.8 = (f32[48,40,128]{2,1,0:T(8,128)}, f32[48,40,128]{2,1,0:T(8,128)S(1)}, u32[]{:S(2)}, u32[]{:S(2)}) collective-permute-start(f32[48,40,128]{2,1,0:T(8,128)} %get-tuple-element.63), channel_id=1, source_target_pairs={{0,6},{1,7},{2,0},{3,1},{4,2},{5,3},{6,4},{7,5},{8,14},{9,15},{10,... | collective-permute-start | bytes 2949128 | tf_op jit(solution)/shard_map/ppermute | solution.py:542
  72.1 40.9 %collective-permute-start.9 = (f32[48,40,128]{2,1,0:T(8,128)}, f32[48,40,128]{2,1,0:T(8,128)S(1)}, u32[]{:S(2)}, u32[]{:S(2)}) collective-permute-start(f32[48,40,128]{2,1,0:T(8,128)} %get-tuple-element.65), channel_id=1, source_target_pairs={{0,8},{1,9},{2,10},{3,11},{4,12},{5,13},{6,14},{7,15},{8,16},{9,17... | collective-permute-start | bytes 2949128 | tf_op jit(solution)/shard_map/ppermute | solution.py:542
  73.8 42.7 %collective-permute-start.10 = (f32[48,40,128]{2,1,0:T(8,128)S(1)}, f32[48,40,128]{2,1,0:T(8,128)S(1)}, u32[]{:S(2)}, u32[]{:S(2)}) collective-permute-start(f32[48,40,128]{2,1,0:T(8,128)S(1)} %copy-done.35), channel_id=1, source_target_pairs={{0,16},{1,17},{2,18},{3,19},{4,20},{5,21},{6,22},{7,23},{8,24},{9,... | collective-permute-start | bytes 2949128 | tf_op jit(solution)/shard_map/ppermute | solution.py:542
  88.9 27.6 %collective-permute-start.11 = (f32[48,40,128]{2,1,0:T(8,128)S(1)}, f32[48,40,128]{2,1,0:T(8,128)S(1)}, u32[]{:S(2)}, u32[]{:S(2)}) collective-permute-start(f32[48,40,128]{2,1,0:T(8,128)S(1)} %copy-done.34), channel_id=1, source_target_pairs={{0,24},{1,25},{2,26},{3,27},{4,28},{5,29},{6,30},{7,31},{8,0},{9,1... | collective-permute-start | bytes 2949128 | tf_op jit(solution)/shard_map/ppermute | solution.py:542
  141.2 19.7 %collective-permute-start.13 = (f32[16,40,128]{2,1,0:T(8,128)}, f32[16,40,128]{2,1,0:T(8,128)S(1)}, u32[]{:S(2)}, u32[]{:S(2)}) collective-permute-start(f32[16,40,128]{2,1,0:T(8,128)} %get-tuple-element.71), channel_id=1, source_target_pairs={{0,8},{1,9},{2,10},{3,11},{4,12},{5,13},{6,14},{7,15},{8,16},{9,17... | collective-permute-start | bytes 983048 | tf_op jit(solution)/shard_map/ppermute | solution.py:542
  141.7 25.2 %collective-permute-start.14 = (f32[16,40,128]{2,1,0:T(8,128)}, f32[16,40,128]{2,1,0:T(8,128)S(1)}, u32[]{:S(2)}, u32[]{:S(2)}) collective-permute-start(f32[16,40,128]{2,1,0:T(8,128)} %get-tuple-element.72), channel_id=1, source_target_pairs={{0,16},{1,17},{2,18},{3,19},{4,20},{5,21},{6,22},{7,23},{8,24},{9,... | collective-permute-start | bytes 983048 | tf_op jit(solution)/shard_map/ppermute | solution.py:542
  142.2 24.7 %collective-permute-start.15 = (f32[16,40,128]{2,1,0:T(8,128)}, f32[16,40,128]{2,1,0:T(8,128)S(1)}, u32[]{:S(2)}, u32[]{:S(2)}) collective-permute-start(f32[16,40,128]{2,1,0:T(8,128)} %get-tuple-element.73), channel_id=1, source_target_pairs={{0,24},{1,25},{2,26},{3,27},{4,28},{5,29},{6,30},{7,31},{8,0},{9,1... | collective-permute-start | bytes 983048 | tf_op jit(solution)/shard_map/ppermute | solution.py:542
  144.1 22.7 %collective-permute-start.16 = (f32[16,40,128]{2,1,0:T(8,128)}, f32[16,40,128]{2,1,0:T(8,128)S(1)}, u32[]{:S(2)}, u32[]{:S(2)}) collective-permute-start(f32[16,40,128]{2,1,0:T(8,128)} %get-tuple-element.75), channel_id=1, source_target_pairs={{0,2},{1,3},{2,4},{3,5},{4,6},{5,7},{6,0},{7,1},{8,10},{9,11},{10,... | collective-permute-start | bytes 983048 | tf_op jit(solution)/shard_map/ppermute | solution.py:542
  144.1 31.1 %collective-permute-start.17 = (f32[16,40,128]{2,1,0:T(8,128)}, f32[16,40,128]{2,1,0:T(8,128)S(1)}, u32[]{:S(2)}, u32[]{:S(2)}) collective-permute-start(f32[16,40,128]{2,1,0:T(8,128)} %get-tuple-element.76), channel_id=1, source_target_pairs={{0,4},{1,5},{2,6},{3,7},{4,0},{5,1},{6,2},{7,3},{8,12},{9,13},{10,... | collective-permute-start | bytes 983048 | tf_op jit(solution)/shard_map/ppermute | solution.py:542
  160.8 14.4 %collective-permute-start.18 = (f32[16,40,128]{2,1,0:T(8,128)}, f32[16,40,128]{2,1,0:T(8,128)S(1)}, u32[]{:S(2)}, u32[]{:S(2)}) collective-permute-start(f32[16,40,128]{2,1,0:T(8,128)} %get-tuple-element.77), channel_id=1, source_target_pairs={{0,6},{1,7},{2,0},{3,1},{4,2},{5,3},{6,4},{7,5},{8,14},{9,15},{10,... | collective-permute-start | bytes 983048 | tf_op jit(solution)/shard_map/ppermute | solution.py:542
  229.5 30.0 %collective-permute-start.26 = (f32[48,24,128]{2,1,0:T(8,128)}, f32[48,24,128]{2,1,0:T(8,128)S(1)}, u32[]{:S(2)}, u32[]{:S(2)}) collective-permute-start(f32[48,24,128]{2,1,0:T(8,128)} %get-tuple-element.84), channel_id=1, source_target_pairs={{0,6},{1,7},{2,0},{3,1},{4,2},{5,3},{6,4},{7,5},{8,14},{9,15},{10,... | collective-permute-start | bytes 1769480 | tf_op jit(solution)/shard_map/ppermute | solution.py:542
  232.4 63.5 %collective-permute-start.33 = (f32[48,24,128]{2,1,0:T(8,128)}, f32[48,24,128]{2,1,0:T(8,128)S(1)}, u32[]{:S(2)}, u32[]{:S(2)}) collective-permute-start(f32[48,24,128]{2,1,0:T(8,128)} %get-tuple-element.100), channel_id=1, source_target_pairs={{0,4},{1,5},{2,6},{3,7},{4,0},{5,1},{6,2},{7,3},{8,12},{9,13},{10,... | collective-permute-start | bytes 1769480 | tf_op jit(solution)/shard_map/ppermute | solution.py:542
  232.4 63.5 %collective-permute-start.34 = (f32[48,24,128]{2,1,0:T(8,128)}, f32[48,24,128]{2,1,0:T(8,128)S(1)}, u32[]{:S(2)}, u32[]{:S(2)}) collective-permute-start(f32[48,24,128]{2,1,0:T(8,128)} %get-tuple-element.101), channel_id=1, source_target_pairs={{0,2},{1,3},{2,4},{3,5},{4,6},{5,7},{6,0},{7,1},{8,10},{9,11},{10,... | collective-permute-start | bytes 1769480 | tf_op jit(solution)/shard_map/ppermute | solution.py:542
  233.0 62.8 %collective-permute-start.35 = (f32[48,24,128]{2,1,0:T(8,128)}, f32[48,24,128]{2,1,0:T(8,128)S(1)}, u32[]{:S(2)}, u32[]{:S(2)}) collective-permute-start(f32[48,24,128]{2,1,0:T(8,128)} %get-tuple-element.103), channel_id=1, source_target_pairs={{0,24},{1,25},{2,26},{3,27},{4,28},{5,29},{6,30},{7,31},{8,0},{9,1... | collective-permute-start | bytes 1769480 | tf_op jit(solution)/shard_map/ppermute | solution.py:542
  233.0 62.9 %collective-permute-start.36 = (f32[48,24,128]{2,1,0:T(8,128)}, f32[48,24,128]{2,1,0:T(8,128)S(1)}, u32[]{:S(2)}, u32[]{:S(2)}) collective-permute-start(f32[48,24,128]{2,1,0:T(8,128)} %get-tuple-element.104), channel_id=1, source_target_pairs={{0,16},{1,17},{2,18},{3,19},{4,20},{5,21},{6,22},{7,23},{8,24},{9,... | collective-permute-start | bytes 1769480 | tf_op jit(solution)/shard_map/ppermute | solution.py:542
  259.6 36.4 %collective-permute-start.37 = (f32[48,24,128]{2,1,0:T(8,128)}, f32[48,24,128]{2,1,0:T(8,128)}, u32[]{:S(2)}, u32[]{:S(2)}) collective-permute-start(f32[48,24,128]{2,1,0:T(8,128)} %get-tuple-element.105), channel_id=1, source_target_pairs={{0,8},{1,9},{2,10},{3,11},{4,12},{5,13},{6,14},{7,15},{8,16},{9,17... | collective-permute-start | bytes 1769480 | tf_op jit(solution)/shard_map/ppermute | solution.py:542
  265.2 30.6 %all-to-all-start.1 = ((f32[32,8,384]{2,1,0:T(8,128)}), f32[32,8,384]{2,1,0:T(8,128)S(1)}, u32[]{:S(2)}, u32[]{:S(2)}) async-start(f32[32,8,384]{2,1,0:T(8,128)} %get-tuple-element.87), calls=%async_computation.2 | async-start | bytes 786432 | tf_op jit(solution)/shard_map/all_to_all | solution.py:628
  276.8 81.1 %reduce-scatter.5.cloned.1.call-start = ((), (), s32[]{:S(2)}) async-start(), calls=%async_computation.7 | async-start | bytes 1966080 | tf_op jit(solution)/shard_map/reduce_scatter | solution.py:631
  322.0 25.4 %collective-permute-start.30 = (f32[16,80,128]{2,1,0:T(8,128)}, f32[16,80,128]{2,1,0:T(8,128)S(1)}, u32[]{:S(2)}, u32[]{:S(2)}) collective-permute-start(f32[16,80,128]{2,1,0:T(8,128)} %get-tuple-element.94), channel_id=1, source_target_pairs={{0,32},{32,64},{64,96},{96,0},{1,33},{33,65},{65,97},{97,1},{2,34}... | collective-permute-start | bytes 1966088 | tf_op jit(solution)/shard_map/ppermute | solution.py:546
  323.8 38.4 %collective-permute-start.31 = (f32[16,80,128]{2,1,0:T(8,128)}, f32[16,80,128]{2,1,0:T(8,128)S(1)}, u32[]{:S(2)}, u32[]{:S(2)}) collective-permute-start(f32[16,80,128]{2,1,0:T(8,128)} %get-tuple-element.96), channel_id=1, source_target_pairs={{0,64},{32,96},{64,0},{96,32},{1,65},{33,97},{65,1},{97,33},{2,66}... | collective-permute-start | bytes 1966088 | tf_op jit(solution)/shard_map/ppermute | solution.py:546
  325.2 37.1 %collective-permute-start.32 = (f32[16,80,128]{2,1,0:T(8,128)}, f32[16,80,128]{2,1,0:T(8,128)S(1)}, u32[]{:S(2)}, u32[]{:S(2)}) collective-permute-start(f32[16,80,128]{2,1,0:T(8,128)} %get-tuple-element.97), channel_id=1, source_target_pairs={{0,96},{32,0},{64,32},{96,64},{1,97},{33,1},{65,33},{97,65},{2,98}... | collective-permute-start | bytes 1966088 | tf_op jit(solution)/shard_map/ppermute | solution.py:546
  348.3 19.8 %all-to-all-start.2 = ((f32[32,8,384]{2,1,0:T(8,128)}), f32[32,8,384]{2,1,0:T(8,128)S(1)}, u32[]{:S(2)}, u32[]{:S(2)}) async-start(f32[32,8,384]{2,1,0:T(8,128)} %broadcast_in_dim.59), calls=%async_computation.4 | async-start | bytes 786432 | tf_op jit(solution)/shard_map/all_to_all | solution.py:642
  (49 other events, 430.8 us)
Sparse Core Ops, SparseCore 0:
  66.1 122.1 reduce-scatter.2
  196.2 114.8 all-gather.1
  313.6 39.8 reduce-scatter.4

commit v4 on v3

--- a/solution.py
+++ b/solution.py
@@ -506,20 +506,23 @@
     )(meta, tile_values, *replies)
 
 
+LAST_PER = 8
+
+
 def finish_kernel(own, *rest):
     sums, out = rest[:-1], rest[-1]
-    for b in range(PER):
+    for b in range(LAST_PER):
         pieces = [(sums[0][b] + sums[1][b]) + (sums[2][b] + sums[3][b]), sums[4][b]]
         rows = slice(b * BLOCK, (b + 1) * BLOCK)
         out[rows, :] = own[rows, :] + jnp.concatenate(pieces, axis=0).T
 
 
 def finish(own, sums):
-    row = pl.BlockSpec((PER * BLOCK, FEAT), lambda i: (i, 0))
-    block = lambda depth: pl.BlockSpec((PER, depth, BLOCK), lambda i: (i, 0, 0))
+    row = pl.BlockSpec((LAST_PER * BLOCK, FEAT), lambda i: (i, 0))
+    block = lambda depth: pl.BlockSpec((LAST_PER, depth, BLOCK), lambda i: (i, 0, 0))
     return pl.pallas_call(
         finish_kernel,
-        grid=(BLOCKS_DEV // PER,),
+        grid=(BLOCKS_DEV // LAST_PER,),
         in_specs=[row] + [block(GATHERED)] * N_REP + [block(REPLIED)],
         out_specs=row,
         out_shape=jax.ShapeDtypeStruct(own.shape, F32),

time: 380 us -> 380 us (level)
  transfers between devices with their start and end apart: 44 -> 44, of which waited for: 25 -> 26; matrix products, arithmetic and copies ran while one was open for 2% -> 2% of each run, Pallas kernels for 12% -> 12%
where the time goes in v4:
time: 380 us; the launch traced here: 376 us
  waiting for transfers between devices  169 us (44%)
  starting transfers between devices  106 us (28%)
  Pallas kernels  69.2 us (18%)
  between operations  14.3 us (4%)
  local copies, waits for them, and re-layouts  13.6 us (4%)
  other arithmetic  4.4 us (1%)
    ppermute x26, waiting for transfers between devices, shift(): return lax.ppermute(x, 'row', pairs)  88.9 us
    ppermute x26, starting transfers between devices, shift(): return lax.ppermute(x, 'row', pairs)  61.8 us
    ppermute x12, waiting for transfers between devices, shift_rep(): lax.ppermute(x, 'rep', [(i, (i + d) % N_REP) for i in range(N_REP)])  39.4 us
    all_to_all x1, waiting for transfers between devices, local(): lax.all_to_all(terms, 'row', split_axis=0, concat_axis=0, tiled=True)  19 us
    pallas_call x1, Pallas kernels, forward_tiles(): pl.pallas_call(forward_kernel, grid_spec=spec, out_shape=[jax.ShapeDtypeS...  17.9 us
    reduce_scatter x1, waiting for transfers between devices, local(): lax.psum_scatter(all_sums.reshape(-1, FEAT), 'row', scatter_dimension=0,...  13.2 us
    ppermute x12, starting transfers between devices, shift_rep(): lax.ppermute(x, 'rep', [(i, (i + d) % N_REP) for i in range(N_REP)])  12.9 us
    all_to_all x1, starting transfers between devices, local(): lax.all_to_all(terms, 'row', split_axis=0, concat_axis=0, tiled=True)  11.6 us
  transfers between devices with their start and end apart: 44, of which 26 were waited for; matrix products, arithmetic and copies ran while one was open for 2% of the time, Pallas kernels for 12%

profile of v4, /device:TPU:5, one launch (start us, length us, event | category | flops | bytes accessed | tf_op | source)
XLA Modules:
  0.0 376.2 jit_solution(4249185805796729596)
XLA Ops:
  13.9 9.6 %all-to-all-start = ((s32[32,1,96]{2,1,0:T(1,128)}), s32[32,1,96]{2,1,0:T(1,128)S(1)}, u32[]{:S(2)}, u32[]{:S(2)}) async-start(s32[32,1,96]{2,1,0:T(1,128)} %bitcast.5), calls=%async_computation | async-start | bytes 32768 | tf_op jit(solution)/shard_map/all_to_all | solution.py:587
  24.2 6.2 %all-to-all-done = s32[32,1,96]{2,1,0:T(1,128)S(1)} async-done(((s32[32,1,96]{2,1,0:T(1,128)}), s32[32,1,96]{2,1,0:T(1,128)S(1)}, u32[]{:S(2)}, u32[]{:S(2)}) %all-to-all-start) | async-done | bytes 12320 | tf_op jit(solution)/shard_map/all_to_all | solution.py:587
  34.3 10.1 %collective-permute-done.3 = f32[1024,128]{1,0:T(8,128)S(1)} collective-permute-done((f32[1024,128]{1,0:T(8,128)S(1)}, f32[1024,128]{1,0:T(8,128)S(1)}, u32[]{:S(2)}, u32[]{:S(2)}) %collective-permute-start.3) | collective-permute-done | bytes 524320 | tf_op jit(solution)/shard_map/ppermute | solution.py:549
  48.0 17.9 %forward_tiles.1 = (f32[48,40,128]{2,1,0:T(8,128)}, f32[48,40,128]{2,1,0:T(8,128)}, f32[48,40,128]{2,1,0:T(8,128)}, f32[48,40,128]{2,1,0:T(8,128)}, f32[48,40,12...) custom-call(s32[512]{0:T(512)} %pad_add_fusion.2.meta, ...), custom_call_target="tpu_custom_call" | custom-call | tf_op jit(solution)/shard_map/forward_tiles/pallas_call | solution.py:128
  73.8 3.3 collective-permute-start.10
  77.0 11.9 %collective-permute-done.6.rest_1_ = f32[48,40,128]{2,1,0:T(8,128)S(1)} collective-permute-done((f32[48,40,128]{2,1,0:T(8,128)S(1)}, f32[48,40,128]{2,1,0:T(8,128)S(1)}, u32[]{:S(2)}, u32[]{:S(2)}) %collective-permute-start.6) | collective-permute-done | bytes 983072 | tf_op jit(solution)/shard_map/ppermute | solution.py:545
  88.9 3.7 collective-permute-start.11
  93.3 17.8 %collective-permute-done.7.rest_2_ = f32[48,40,128]{2,1,0:T(8,128)S(1)} collective-permute-done((f32[48,40,128]{2,1,0:T(8,128)}, f32[48,40,128]{2,1,0:T(8,128)S(1)}, u32[]{:S(2)}, u32[]{:S(2)}) %collective-permute-start.7) | collective-permute-done | bytes 983072 | tf_op jit(solution)/shard_map/ppermute | solution.py:545
  113.0 3.4 collective-permute-done.10.rest_6_
  117.8 6.1 %combine_blocks.1 = (f32[128,40,128]{2,1,0:T(8,128)}, f32[128,40,128]{2,1,0:T(8,128)}) custom-call(s32[3072]{0:T(1024)} %reshape.141.ids, s32[3]{0:T(128)} %pad_add_fusion.3.place, f32[48,40,128]{2,1,0:T(8,128)} %get-tuple-element.60.rest_0_, f32[48,40,128]{2,1,0:T(8,128)} %copy-done.3, f32[48,40,128]{2,1,0:T(8,128)} %copy-done.4, f32[48,40,128]{2,1,0:T(8,128)} %copy-done.5, ...), custom_call_target="tpu_custom_call" | custom-call | tf_op jit(solution)/shard_map/combine_blocks/pallas_call | solution.py:188
  123.9 6.9 %collective-permute-start.12 = (f32[128,40,128]{2,1,0:T(8,128)}, f32[128,40,128]{2,1,0:T(8,128)S(1)}, u32[]{:S(2)}, u32[]{:S(2)}) collective-permute-start(f32[128,40,128]{2,1,0:T(8,128)} %get-tuple-element.69), channel_id=1, source_target_pairs={{0,1},{1,0},{2,3},{3,2},{4,5},{5,4},{6,7},{7,6},{8,9},{9,8},{10,11... | collective-permute-start | bytes 7864328 | tf_op jit(solution)/shard_map/ppermute | solution.py:545
  130.8 4.7 %collective-permute-done.12.taken = f32[128,40,128]{2,1,0:T(8,128)S(1)} collective-permute-done((f32[128,40,128]{2,1,0:T(8,128)}, f32[128,40,128]{2,1,0:T(8,128)S(1)}, u32[]{:S(2)}, u32[]{:S(2)}) %collective-permute-start.12) | collective-permute-done | bytes 2621472 | tf_op jit(solution)/shard_map/ppermute | solution.py:545
  137.1 4.1 %add_cores.1 = (f32[16,40,128]{2,1,0:T(8,128)}, f32[16,40,128]{2,1,0:T(8,128)}, f32[16,40,128]{2,1,0:T(8,128)}, f32[16,40,128]{2,1,0:T(8,128)}, f32[16,40,128]{2...) custom-call(f32[128,40,128]{2,1,0:T(8,128)} %get-tuple-element.68.keep, ...), custom_call_target="tpu_custom_call" | custom-call | tf_op jit(solution)/shard_map/add_cores/pallas_call | solution.py:218
  144.1 16.7 %collective-permute-start.17 = (f32[16,40,128]{2,1,0:T(8,128)}, f32[16,40,128]{2,1,0:T(8,128)S(1)}, u32[]{:S(2)}, u32[]{:S(2)}) collective-permute-start(f32[16,40,128]{2,1,0:T(8,128)} %get-tuple-element.76), channel_id=1, source_target_pairs={{0,4},{1,5},{2,6},{3,7},{4,0},{5,1},{6,2},{7,3},{8,12},{9,13},{10,... | collective-permute-start | bytes 983048 | tf_op jit(solution)/shard_map/ppermute | solution.py:545
  162.9 3.9 %collective-permute-done.14.rest_2_ = f32[16,40,128]{2,1,0:T(8,128)S(1)} collective-permute-done((f32[16,40,128]{2,1,0:T(8,128)}, f32[16,40,128]{2,1,0:T(8,128)S(1)}, u32[]{:S(2)}, u32[]{:S(2)}) %collective-permute-start.14) | collective-permute-done | bytes 327712 | tf_op jit(solution)/shard_map/ppermute | solution.py:545
  166.8 8.3 %collective-permute-done.17.rest_6_ = f32[16,40,128]{2,1,0:T(8,128)S(1)} collective-permute-done((f32[16,40,128]{2,1,0:T(8,128)}, f32[16,40,128]{2,1,0:T(8,128)S(1)}, u32[]{:S(2)}, u32[]{:S(2)}) %collective-permute-start.17) | collective-permute-done | bytes 327712 | tf_op jit(solution)/shard_map/ppermute | solution.py:545
  175.2 13.2 %reduce-scatter.3.cloned.1.call-done = f32[768,128]{1,0:T(8,128)} async-done(((f32[24576,128]{1,0:T(8,128)}), f32[768,128]{1,0:T(8,128)}) %reduce-scatter.3.cloned.1.call-update) | async-done | bytes 393232 | tf_op jit(solution)/shard_map/reduce_scatter | solution.py:602
  188.4 7.6 %layer.1 = (f32[2048,256]{1,0:T(8,128)}, f32[2048,256]{1,0:T(8,128)}, f32[2048,128]{1,0:T(8,128)}, f32[16,80,128]{2,1,0:T(8,128)}, f32[16,24,128]{2,1,0:T(8,128)}, /*index=5*/f32[16,24,128]{2,1,0:T(8,128)}) custom-call(f32[2048,128]{1,0:T(8,128)} %features.3, f32[2048,256]{1,0:T(8,128)} %cotangent.1, f32[128,256]{1,0:T(8,128)} %w_self.3, ...), custom_call_target="tpu_custom_call" | custom-call | tf_op jit(solution)/shard_map/layer/pallas_call | solution.py:270
  209.4 4.2 %collective-permute-done.24 = f32[16,24,128]{2,1,0:T(8,128)S(1)} collective-permute-done((f32[16,24,128]{2,1,0:T(8,128)}, f32[16,24,128]{2,1,0:T(8,128)S(1)}, u32[]{:S(2)}, u32[]{:S(2)}) %collective-permute-start.24) | collective-permute-done | bytes 196640 | tf_op jit(solution)/shard_map/ppermute | solution.py:545
  213.6 6.5 %collective-permute-start.25 = (f32[128,24,128]{2,1,0:T(8,128)S(1)}, f32[128,24,128]{2,1,0:T(8,128)S(1)}, u32[]{:S(2)}, u32[]{:S(2)}) collective-permute-start(f32[128,24,128]{2,1,0:T(8,128)S(1)} %constant_dynamic-update-slice_fusion.mine), channel_id=1, source_target_pairs={{0,1},{1,0},{2,3},{3,2},{4,5},{5,4},{6,7},{7,6},{8,9},{9,8},{10,11... | collective-permute-start | bytes 4718600 | tf_op jit(solution)/shard_map/ppermute | solution.py:545
  220.1 3.0 collective-permute-done.25.taken
  224.3 5.1 %make_replies.1 = (f32[48,24,128]{2,1,0:T(8,128)}, f32[48,24,128]{2,1,0:T(8,128)}, f32[48,24,128]{2,1,0:T(8,128)}, f32[48,24,128]{2,1,0:T(8,128)}, f32[48,24,128...) custom-call(s32[3072]{0:T(1024)} %reshape.141.ids, ...), custom_call_target="tpu_custom_call" | custom-call | tf_op jit(solution)/shard_map/make_replies/pallas_call | solution.py:381
  233.1 26.8 %collective-permute-done.26.rest_1_ = f32[48,24,128]{2,1,0:T(8,128)S(1)} collective-permute-done((f32[48,24,128]{2,1,0:T(8,128)}, f32[48,24,128]{2,1,0:T(8,128)S(1)}, u32[]{:S(2)}, u32[]{:S(2)}) %collective-permute-start.26) | collective-permute-done | bytes 589856 | tf_op jit(solution)/shard_map/ppermute | solution.py:545
  259.8 5.7 %weight_terms.1 = (f32[2048,128]{1,0:T(8,128)}, f32[32,8,384]{2,1,0:T(8,128)}) custom-call(f32[2048,128]{1,0:T(8,128)} %features.3, f32[2048,128]{1,0:T(8,128)} %get-tuple-element.80.aggregated, f32[2048,256]{1,0:T(8,128)} %get-tuple-element.85.grad_pre, f32[128,256]{1,0:T(8,128)} %w_self.3), custom_call_target="tpu_custom_call" | custom-call | tf_op jit(solution)/shard_map/weight_terms/pallas_call | solution.py:322
  265.5 11.6 %all-to-all-start.1 = ((f32[32,8,384]{2,1,0:T(8,128)}), f32[32,8,384]{2,1,0:T(8,128)S(1)}, u32[]{:S(2)}, u32[]{:S(2)}) async-start(f32[32,8,384]{2,1,0:T(8,128)} %get-tuple-element.87), calls=%async_computation.2 | async-start | bytes 786432 | tf_op jit(solution)/shard_map/all_to_all | solution.py:631
  277.1 19.0 %all-to-all-done.1 = f32[32,8,384]{2,1,0:T(8,128)S(1)} async-done(((f32[32,8,384]{2,1,0:T(8,128)}), f32[32,8,384]{2,1,0:T(8,128)S(1)}, u32[]{:S(2)}, u32[]{:S(2)}) %all-to-all-start.1) | async-done | bytes 393248 | tf_op jit(solution)/shard_map/all_to_all | solution.py:631
  297.5 10.0 %replied_tiles.1 = f32[64,48,128]{2,1,0:T(8,128)} custom-call(s32[513]{0:T(1024)} %copy-done.30, f32[128,128,128]{2,1,0:T(8,128)} %tiles.5, f32[48,24,128]{2,1,0:T(8,128)} %get-tuple-element.98.rest_0_, f32[48,24,128]{2,1,0:T(8,128)} %copy-done.12, f32[48,24,128]{2,1,0:T(8,128)} %copy-done.13, f32[48,24,128]{2,1,0:T(8,128)} %copy-done.14, ...), custom_call_target="tpu_custom_call" | custom-call | tf_op jit(solution)/shard_map/replied_tiles/pallas_call | solution.py:500
  313.0 9.6 %gathered_tiles.1 = (f32[16,80,128]{2,1,0:T(8,128)}, f32[16,80,128]{2,1,0:T(8,128)}, f32[16,80,128]{2,1,0:T(8,128)}, f32[16,80,128]{2,1,0:T(8,128)}) custom-call(s32[513]{0:T(1024)} %copy-done.30, f32[128,128,128]{2,1,0:T(8,128)} %tiles.5, f32[512,80,128]{2,1,0:T(8,128)} %all-gather.2.cloned.1.call-done.grads), custom_call_target="tpu_custom_call" | custom-call | tf_op jit(solution)/shard_map/gathered_tiles/pallas_call | solution.py:448
  327.6 19.9 %collective-permute-done.30.rest_1_ = f32[16,80,128]{2,1,0:T(8,128)S(1)} collective-permute-done((f32[16,80,128]{2,1,0:T(8,128)}, f32[16,80,128]{2,1,0:T(8,128)S(1)}, u32[]{:S(2)}, u32[]{:S(2)}) %collective-permute-start.30) | collective-permute-done | bytes 655392 | tf_op jit(solution)/shard_map/ppermute | solution.py:549
  348.4 9.8 %all-to-all-start.2 = ((f32[32,8,384]{2,1,0:T(8,128)}), f32[32,8,384]{2,1,0:T(8,128)S(1)}, u32[]{:S(2)}, u32[]{:S(2)}) async-start(f32[32,8,384]{2,1,0:T(8,128)} %broadcast_in_dim.59), calls=%async_computation.4 | async-start | bytes 786432 | tf_op jit(solution)/shard_map/all_to_all | solution.py:645
  358.2 3.7 collective-permute-done.31.rest_2_
  363.2 3.1 finish_grad_x.1
  (188 shorter events, 68.2 us)
Async XLA Ops:
  8.5 24.0 %collective-permute-start.1 = (f32[1024,128]{1,0:T(8,128)S(1)}, f32[1024,128]{1,0:T(8,128)S(1)}, u32[]{:S(2)}, u32[]{:S(2)}) collective-permute-start(f32[1024,128]{1,0:T(8,128)S(1)} %get-tuple-element.116), channel_id=1, source_target_pairs={{0,96},{32,0},{64,32},{96,64},{1,97},{33,1},{65,33},{97,65},{2,98}... | collective-permute-start | bytes 1572872 | tf_op jit(solution)/shard_map/ppermute | solution.py:549
  8.8 25.5 %collective-permute-start.2 = (f32[1024,128]{1,0:T(8,128)S(1)}, f32[1024,128]{1,0:T(8,128)S(1)}, u32[]{:S(2)}, u32[]{:S(2)}) collective-permute-start(f32[1024,128]{1,0:T(8,128)S(1)} %get-tuple-element.116), channel_id=1, source_target_pairs={{0,32},{32,64},{64,96},{96,0},{1,33},{33,65},{65,97},{97,1},{2,34}... | collective-permute-start | bytes 1572872 | tf_op jit(solution)/shard_map/ppermute | solution.py:549
  10.0 22.5 %collective-permute-start = (f32[1024,128]{1,0:T(8,128)S(1)}, f32[1024,128]{1,0:T(8,128)S(1)}, u32[]{:S(2)}, u32[]{:S(2)}) collective-permute-start(f32[1024,128]{1,0:T(8,128)S(1)} %get-tuple-element.117), channel_id=1, source_target_pairs={{0,32},{32,64},{64,96},{96,0},{1,33},{33,65},{65,97},{97,1},{2,34}... | collective-permute-start | bytes 1572872 | tf_op jit(solution)/shard_map/ppermute | solution.py:549
  12.1 22.1 %collective-permute-start.5 = (f32[1024,128]{1,0:T(8,128)S(1)}, f32[1024,128]{1,0:T(8,128)S(1)}, u32[]{:S(2)}, u32[]{:S(2)}) collective-permute-start(f32[1024,128]{1,0:T(8,128)S(1)} %get-tuple-element.117), channel_id=1, source_target_pairs={{0,96},{32,0},{64,32},{96,64},{1,97},{33,1},{65,33},{97,65},{2,98}... | collective-permute-start | bytes 1572872 | tf_op jit(solution)/shard_map/ppermute | solution.py:549
  13.9 16.5 %all-to-all-start = ((s32[32,1,96]{2,1,0:T(1,128)}), s32[32,1,96]{2,1,0:T(1,128)S(1)}, u32[]{:S(2)}, u32[]{:S(2)}) async-start(s32[32,1,96]{2,1,0:T(1,128)} %bitcast.5), calls=%async_computation | async-start | bytes 32768 | tf_op jit(solution)/shard_map/all_to_all | solution.py:587
  23.6 164.8 %reduce-scatter.3.cloned.1.call-start = ((), (), s32[]{:S(2)}) async-start(), calls=%async_computation.5 | async-start | bytes 12976128 | tf_op jit(solution)/shard_map/reduce_scatter | solution.py:602
  34.1 13.1 %collective-permute-start.4 = (f32[1024,128]{1,0:T(8,128)S(1)}, f32[1024,128]{1,0:T(8,128)S(1)}, u32[]{:S(2)}, u32[]{:S(2)}) collective-permute-start(f32[1024,128]{1,0:T(8,128)S(1)} %collective-permute-done.1), channel_id=1, source_target_pairs={{0,96},{32,0},{64,32},{96,64},{1,97},{33,1},{65,33},{97,65},{2,98}... | collective-permute-start | bytes 1572872 | tf_op jit(solution)/shard_map/ppermute | solution.py:549
  66.0 247.0 %all-gather.2.cloned.1.call-start = ((), (), s32[]{:S(2)}) async-start(), calls=%async_computation.6 | async-start | bytes 21626880 | tf_op jit(solution)/shard_map/all_gather | solution.py:618
  67.1 21.8 %collective-permute-start.6 = (f32[48,40,128]{2,1,0:T(8,128)S(1)}, f32[48,40,128]{2,1,0:T(8,128)S(1)}, u32[]{:S(2)}, u32[]{:S(2)}) collective-permute-start(f32[48,40,128]{2,1,0:T(8,128)S(1)} %copy-done.36), channel_id=1, source_target_pairs={{0,2},{1,3},{2,4},{3,5},{4,6},{5,7},{6,0},{7,1},{8,10},{9,11},{10,... | collective-permute-start | bytes 2949128 | tf_op jit(solution)/shard_map/ppermute | solution.py:545
  68.4 42.7 %collective-permute-start.7 = (f32[48,40,128]{2,1,0:T(8,128)}, f32[48,40,128]{2,1,0:T(8,128)S(1)}, u32[]{:S(2)}, u32[]{:S(2)}) collective-permute-start(f32[48,40,128]{2,1,0:T(8,128)} %get-tuple-element.62), channel_id=1, source_target_pairs={{0,4},{1,5},{2,6},{3,7},{4,0},{5,1},{6,2},{7,3},{8,12},{9,13},{10,... | collective-permute-start | bytes 2949128 | tf_op jit(solution)/shard_map/ppermute | solution.py:545
  71.0 42.0 %collective-permute-start.8 = (f32[48,40,128]{2,1,0:T(8,128)}, f32[48,40,128]{2,1,0:T(8,128)S(1)}, u32[]{:S(2)}, u32[]{:S(2)}) collective-permute-start(f32[48,40,128]{2,1,0:T(8,128)} %get-tuple-element.63), channel_id=1, source_target_pairs={{0,6},{1,7},{2,0},{3,1},{4,2},{5,3},{6,4},{7,5},{8,14},{9,15},{10,... | collective-permute-start | bytes 2949128 | tf_op jit(solution)/shard_map/ppermute | solution.py:545
  72.1 40.9 %collective-permute-start.9 = (f32[48,40,128]{2,1,0:T(8,128)}, f32[48,40,128]{2,1,0:T(8,128)S(1)}, u32[]{:S(2)}, u32[]{:S(2)}) collective-permute-start(f32[48,40,128]{2,1,0:T(8,128)} %get-tuple-element.65), channel_id=1, source_target_pairs={{0,8},{1,9},{2,10},{3,11},{4,12},{5,13},{6,14},{7,15},{8,16},{9,17... | collective-permute-start | bytes 2949128 | tf_op jit(solution)/shard_map/ppermute | solution.py:545
  73.8 42.7 %collective-permute-start.10 = (f32[48,40,128]{2,1,0:T(8,128)S(1)}, f32[48,40,128]{2,1,0:T(8,128)S(1)}, u32[]{:S(2)}, u32[]{:S(2)}) collective-permute-start(f32[48,40,128]{2,1,0:T(8,128)S(1)} %copy-done.35), channel_id=1, source_target_pairs={{0,16},{1,17},{2,18},{3,19},{4,20},{5,21},{6,22},{7,23},{8,24},{9,... | collective-permute-start | bytes 2949128 | tf_op jit(solution)/shard_map/ppermute | solution.py:545
  88.9 27.5 %collective-permute-start.11 = (f32[48,40,128]{2,1,0:T(8,128)S(1)}, f32[48,40,128]{2,1,0:T(8,128)S(1)}, u32[]{:S(2)}, u32[]{:S(2)}) collective-permute-start(f32[48,40,128]{2,1,0:T(8,128)S(1)} %copy-done.34), channel_id=1, source_target_pairs={{0,24},{1,25},{2,26},{3,27},{4,28},{5,29},{6,30},{7,31},{8,0},{9,1... | collective-permute-start | bytes 2949128 | tf_op jit(solution)/shard_map/ppermute | solution.py:545
  141.2 19.6 %collective-permute-start.13 = (f32[16,40,128]{2,1,0:T(8,128)}, f32[16,40,128]{2,1,0:T(8,128)S(1)}, u32[]{:S(2)}, u32[]{:S(2)}) collective-permute-start(f32[16,40,128]{2,1,0:T(8,128)} %get-tuple-element.71), channel_id=1, source_target_pairs={{0,8},{1,9},{2,10},{3,11},{4,12},{5,13},{6,14},{7,15},{8,16},{9,17... | collective-permute-start | bytes 983048 | tf_op jit(solution)/shard_map/ppermute | solution.py:545
  141.6 25.2 %collective-permute-start.14 = (f32[16,40,128]{2,1,0:T(8,128)}, f32[16,40,128]{2,1,0:T(8,128)S(1)}, u32[]{:S(2)}, u32[]{:S(2)}) collective-permute-start(f32[16,40,128]{2,1,0:T(8,128)} %get-tuple-element.72), channel_id=1, source_target_pairs={{0,16},{1,17},{2,18},{3,19},{4,20},{5,21},{6,22},{7,23},{8,24},{9,... | collective-permute-start | bytes 983048 | tf_op jit(solution)/shard_map/ppermute | solution.py:545
  142.1 24.7 %collective-permute-start.15 = (f32[16,40,128]{2,1,0:T(8,128)}, f32[16,40,128]{2,1,0:T(8,128)S(1)}, u32[]{:S(2)}, u32[]{:S(2)}) collective-permute-start(f32[16,40,128]{2,1,0:T(8,128)} %get-tuple-element.73), channel_id=1, source_target_pairs={{0,24},{1,25},{2,26},{3,27},{4,28},{5,29},{6,30},{7,31},{8,0},{9,1... | collective-permute-start | bytes 983048 | tf_op jit(solution)/shard_map/ppermute | solution.py:545
  144.1 22.7 %collective-permute-start.16 = (f32[16,40,128]{2,1,0:T(8,128)}, f32[16,40,128]{2,1,0:T(8,128)S(1)}, u32[]{:S(2)}, u32[]{:S(2)}) collective-permute-start(f32[16,40,128]{2,1,0:T(8,128)} %get-tuple-element.75), channel_id=1, source_target_pairs={{0,2},{1,3},{2,4},{3,5},{4,6},{5,7},{6,0},{7,1},{8,10},{9,11},{10,... | collective-permute-start | bytes 983048 | tf_op jit(solution)/shard_map/ppermute | solution.py:545
  144.1 31.1 %collective-permute-start.17 = (f32[16,40,128]{2,1,0:T(8,128)}, f32[16,40,128]{2,1,0:T(8,128)S(1)}, u32[]{:S(2)}, u32[]{:S(2)}) collective-permute-start(f32[16,40,128]{2,1,0:T(8,128)} %get-tuple-element.76), channel_id=1, source_target_pairs={{0,4},{1,5},{2,6},{3,7},{4,0},{5,1},{6,2},{7,3},{8,12},{9,13},{10,... | collective-permute-start | bytes 983048 | tf_op jit(solution)/shard_map/ppermute | solution.py:545
  160.8 14.4 %collective-permute-start.18 = (f32[16,40,128]{2,1,0:T(8,128)}, f32[16,40,128]{2,1,0:T(8,128)S(1)}, u32[]{:S(2)}, u32[]{:S(2)}) collective-permute-start(f32[16,40,128]{2,1,0:T(8,128)} %get-tuple-element.77), channel_id=1, source_target_pairs={{0,6},{1,7},{2,0},{3,1},{4,2},{5,3},{6,4},{7,5},{8,14},{9,15},{10,... | collective-permute-start | bytes 983048 | tf_op jit(solution)/shard_map/ppermute | solution.py:545
  229.4 30.4 %collective-permute-start.26 = (f32[48,24,128]{2,1,0:T(8,128)}, f32[48,24,128]{2,1,0:T(8,128)S(1)}, u32[]{:S(2)}, u32[]{:S(2)}) collective-permute-start(f32[48,24,128]{2,1,0:T(8,128)} %get-tuple-element.84), channel_id=1, source_target_pairs={{0,6},{1,7},{2,0},{3,1},{4,2},{5,3},{6,4},{7,5},{8,14},{9,15},{10,... | collective-permute-start | bytes 1769480 | tf_op jit(solution)/shard_map/ppermute | solution.py:545
  232.4 63.7 %collective-permute-start.33 = (f32[48,24,128]{2,1,0:T(8,128)}, f32[48,24,128]{2,1,0:T(8,128)S(1)}, u32[]{:S(2)}, u32[]{:S(2)}) collective-permute-start(f32[48,24,128]{2,1,0:T(8,128)} %get-tuple-element.100), channel_id=1, source_target_pairs={{0,4},{1,5},{2,6},{3,7},{4,0},{5,1},{6,2},{7,3},{8,12},{9,13},{10,... | collective-permute-start | bytes 1769480 | tf_op jit(solution)/shard_map/ppermute | solution.py:545
  232.4 63.7 %collective-permute-start.34 = (f32[48,24,128]{2,1,0:T(8,128)}, f32[48,24,128]{2,1,0:T(8,128)S(1)}, u32[]{:S(2)}, u32[]{:S(2)}) collective-permute-start(f32[48,24,128]{2,1,0:T(8,128)} %get-tuple-element.101), channel_id=1, source_target_pairs={{0,2},{1,3},{2,4},{3,5},{4,6},{5,7},{6,0},{7,1},{8,10},{9,11},{10,... | collective-permute-start | bytes 1769480 | tf_op jit(solution)/shard_map/ppermute | solution.py:545
  233.0 63.1 %collective-permute-start.35 = (f32[48,24,128]{2,1,0:T(8,128)}, f32[48,24,128]{2,1,0:T(8,128)S(1)}, u32[]{:S(2)}, u32[]{:S(2)}) collective-permute-start(f32[48,24,128]{2,1,0:T(8,128)} %get-tuple-element.103), channel_id=1, source_target_pairs={{0,24},{1,25},{2,26},{3,27},{4,28},{5,29},{6,30},{7,31},{8,0},{9,1... | collective-permute-start | bytes 1769480 | tf_op jit(solution)/shard_map/ppermute | solution.py:545
  233.0 63.1 %collective-permute-start.36 = (f32[48,24,128]{2,1,0:T(8,128)}, f32[48,24,128]{2,1,0:T(8,128)S(1)}, u32[]{:S(2)}, u32[]{:S(2)}) collective-permute-start(f32[48,24,128]{2,1,0:T(8,128)} %get-tuple-element.104), channel_id=1, source_target_pairs={{0,16},{1,17},{2,18},{3,19},{4,20},{5,21},{6,22},{7,23},{8,24},{9,... | collective-permute-start | bytes 1769480 | tf_op jit(solution)/shard_map/ppermute | solution.py:545
  259.8 36.3 %collective-permute-start.37 = (f32[48,24,128]{2,1,0:T(8,128)}, f32[48,24,128]{2,1,0:T(8,128)}, u32[]{:S(2)}, u32[]{:S(2)}) collective-permute-start(f32[48,24,128]{2,1,0:T(8,128)} %get-tuple-element.105), channel_id=1, source_target_pairs={{0,8},{1,9},{2,10},{3,11},{4,12},{5,13},{6,14},{7,15},{8,16},{9,17... | collective-permute-start | bytes 1769480 | tf_op jit(solution)/shard_map/ppermute | solution.py:545
  265.5 30.6 %all-to-all-start.1 = ((f32[32,8,384]{2,1,0:T(8,128)}), f32[32,8,384]{2,1,0:T(8,128)S(1)}, u32[]{:S(2)}, u32[]{:S(2)}) async-start(f32[32,8,384]{2,1,0:T(8,128)} %get-tuple-element.87), calls=%async_computation.2 | async-start | bytes 786432 | tf_op jit(solution)/shard_map/all_to_all | solution.py:631
  277.1 81.1 %reduce-scatter.5.cloned.1.call-start = ((), (), s32[]{:S(2)}) async-start(), calls=%async_computation.7 | async-start | bytes 1966080 | tf_op jit(solution)/shard_map/reduce_scatter | solution.py:634
  322.6 24.9 %collective-permute-start.30 = (f32[16,80,128]{2,1,0:T(8,128)}, f32[16,80,128]{2,1,0:T(8,128)S(1)}, u32[]{:S(2)}, u32[]{:S(2)}) collective-permute-start(f32[16,80,128]{2,1,0:T(8,128)} %get-tuple-element.94), channel_id=1, source_target_pairs={{0,32},{32,64},{64,96},{96,0},{1,33},{33,65},{65,97},{97,1},{2,34}... | collective-permute-start | bytes 1966088 | tf_op jit(solution)/shard_map/ppermute | solution.py:549
  323.6 38.3 %collective-permute-start.31 = (f32[16,80,128]{2,1,0:T(8,128)}, f32[16,80,128]{2,1,0:T(8,128)S(1)}, u32[]{:S(2)}, u32[]{:S(2)}) collective-permute-start(f32[16,80,128]{2,1,0:T(8,128)} %get-tuple-element.96), channel_id=1, source_target_pairs={{0,64},{32,96},{64,0},{96,32},{1,65},{33,97},{65,1},{97,33},{2,66}... | collective-permute-start | bytes 1966088 | tf_op jit(solution)/shard_map/ppermute | solution.py:549
  325.7 36.7 %collective-permute-start.32 = (f32[16,80,128]{2,1,0:T(8,128)}, f32[16,80,128]{2,1,0:T(8,128)S(1)}, u32[]{:S(2)}, u32[]{:S(2)}) collective-permute-start(f32[16,80,128]{2,1,0:T(8,128)} %get-tuple-element.97), channel_id=1, source_target_pairs={{0,96},{32,0},{64,32},{96,64},{1,97},{33,1},{65,33},{97,65},{2,98}... | collective-permute-start | bytes 1966088 | tf_op jit(solution)/shard_map/ppermute | solution.py:549
  348.4 19.9 %all-to-all-start.2 = ((f32[32,8,384]{2,1,0:T(8,128)}), f32[32,8,384]{2,1,0:T(8,128)S(1)}, u32[]{:S(2)}, u32[]{:S(2)}) async-start(f32[32,8,384]{2,1,0:T(8,128)} %broadcast_in_dim.59), calls=%async_computation.4 | async-start | bytes 786432 | tf_op jit(solution)/shard_map/all_to_all | solution.py:645
  (49 other events, 430.6 us)
Sparse Core Ops, SparseCore 0:
  66.1 122.2 reduce-scatter.2
  196.2 114.7 all-gather.1
  313.6 39.3 reduce-scatter.4
